TPU v7x, 32 devices: a whole 2x2x4 slice. The times are simulated.
32 devices in a mesh: seq: 16 (over z, y, x), head: 2 (over core).
Axes of the slice: x: 2, y: 2, z: 4, core: 2. Of those that a mesh axis runs over, the one named last changes fastest.
Arguments:
- queries: bfloat16 [2048, 8192], P('seq', 'head'), may hold values from -6 to 6
- keys: bfloat16 [2048, 8192], P('seq', 'head'), may hold values from -6 to 6
- values: bfloat16 [2048, 8192], P('seq', 'head'), may hold values from -48 to 48, as said below
- cotangent: bfloat16 [2048, 8192], P('seq', 'head'), may hold values from -6 to 6
- gain: float32 [8192], P('head'), may hold values from 0.1 to 1.9
Outputs:
- query_grad: bfloat16 [2048, 8192], P('seq', 'head')
- key_grad: bfloat16 [2048, 8192], P('seq', 'head')
- value_grad: bfloat16 [2048, 8192], P('seq', 'head')
Inputs may be any that keep to these rules, and one draw needn't show every extreme that they name: Real values.
All inputs are finite; a program needn't handle non-finite values.
Results may differ from a plain program's by a relative error of at most 0.0058.
Values sent between devices are 32-bit elements; how exact they have to be, the bound alone decides.
No kernel may reach another device: no remote copies, remote signals or barrier semaphores. Data moves between devices by JAX's collectives and lax.ppermute only.
A program may use at most 128 MiB of HBM per device.

v0:
```python
import jax
import jax.numpy as jnp
from jax import lax
from jax.sharding import PartitionSpec as P

HEAD_DIM = 128


epsilon = 1e-05


def entering(value, axis, combine, identity, reverse):
    count, mine = (lax.axis_size(axis), lax.axis_index(axis))
    everything = lax.all_gather(value, axis)
    start = jnp.broadcast_to(jnp.asarray(identity, value.dtype), value.shape)

    def step(k, before):
        at = count - 1 - k if reverse else k
        reached = at > mine if reverse else at < mine
        new = combine(before, everything[at])
        return jnp.where(reached, new, before)

    return lax.fori_loop(0, count, step, start)


def causal(tokens):
    rows_index = lax.broadcasted_iota(jnp.int32, (tokens, tokens), 0)
    cols_index = lax.broadcasted_iota(jnp.int32, (tokens, tokens), 1)
    return (rows_index >= cols_index)[None, :, :]


def per_device(queries, keys, values, cotangent, gain):
    tokens, width_local = queries.shape
    heads_local = width_local // HEAD_DIM
    score_scale = HEAD_DIM ** (-0.5)
    total_width = width_local * lax.axis_size("head")
    causal_mask = causal(tokens)
    query_heads = queries.reshape(tokens, heads_local, HEAD_DIM)
    key_heads = keys.reshape(tokens, heads_local, HEAD_DIM)
    value_heads = values.reshape(tokens, heads_local, HEAD_DIM)
    local_state = jnp.einsum(
        "shd,she->hde", key_heads, value_heads, preferred_element_type=jnp.float32
    )
    prefix = entering(local_state, "seq", jnp.add, jnp.zeros_like(local_state), False)
    prefix_low = prefix.astype(jnp.bfloat16)
    scores = (
        jnp.einsum("thd,shd->hts", query_heads, key_heads, preferred_element_type=jnp.float32)
        * score_scale
    )
    weights = jnp.where(causal_mask, scores, 0.0).astype(jnp.bfloat16)
    attended = jnp.einsum("hts,shd->thd", weights, value_heads, preferred_element_type=jnp.float32)
    attended = attended + score_scale * jnp.einsum(
        "thd,hde->the", query_heads, prefix_low, preferred_element_type=jnp.float32
    )
    attended = attended.reshape(tokens, width_local)
    scaled = cotangent.astype(jnp.float32) * gain[None, :]
    squares, cross_terms = lax.psum(
        (jnp.sum(attended * attended, axis=1), jnp.sum(scaled * attended, axis=1)), "head"
    )
    inverse_rms = lax.rsqrt(squares / total_width + epsilon)
    normed = attended * inverse_rms[:, None]
    cross_mean = cross_terms * inverse_rms / total_width
    grad_attended = ((scaled - normed * cross_mean[:, None]) * inverse_rms[:, None]).astype(
        jnp.bfloat16
    )
    grad_heads = grad_attended.reshape(tokens, heads_local, HEAD_DIM)
    local_grad_state = jnp.einsum(
        "thd,the->hde", query_heads, grad_heads, preferred_element_type=jnp.float32
    )
    suffix = entering(local_grad_state, "seq", jnp.add, jnp.zeros_like(local_grad_state), True)
    suffix_low = suffix.astype(jnp.bfloat16)
    grad_scores = (
        jnp.einsum("the,she->hts", grad_heads, value_heads, preferred_element_type=jnp.float32)
        * score_scale
    )
    grad_weights = jnp.where(causal_mask, grad_scores, 0.0).astype(jnp.bfloat16)
    query_grad = jnp.einsum(
        "hts,shd->thd", grad_weights, key_heads, preferred_element_type=jnp.float32
    )
    query_grad = query_grad + score_scale * jnp.einsum(
        "the,hde->thd", grad_heads, prefix_low, preferred_element_type=jnp.float32
    )
    key_grad = jnp.einsum(
        "hts,thd->shd", grad_weights, query_heads, preferred_element_type=jnp.float32
    )
    key_grad = key_grad + score_scale * jnp.einsum(
        "she,hde->shd", value_heads, suffix_low, preferred_element_type=jnp.float32
    )
    value_grad = jnp.einsum("hts,the->she", weights, grad_heads, preferred_element_type=jnp.float32)
    value_grad = value_grad + score_scale * jnp.einsum(
        "shd,hde->she", key_heads, suffix_low, preferred_element_type=jnp.float32
    )
    return (
        query_grad.reshape(tokens, width_local).astype(jnp.bfloat16),
        key_grad.reshape(tokens, width_local).astype(jnp.bfloat16),
        value_grad.reshape(tokens, width_local).astype(jnp.bfloat16),
    )


def solution(mesh):
    return jax.shard_map(
        per_device,
        mesh=mesh,
        in_specs=(
            P("seq", "head"),
            P("seq", "head"),
            P("seq", "head"),
            P("seq", "head"),
            P("head"),
        ),
        out_specs=(P("seq", "head"), P("seq", "head"), P("seq", "head")),
        check_vma=False,
    )
```

profile of v0, /device:TPU:0, one launch (start us, length us, event | category | flops | bytes accessed | tf_op | source)
XLA Modules:
  0.0 829.7 jit_solution(9402370827538780016)
XLA Ops:
  7.2 2.6 copy.62
  19.0 348.2 %all-gather.5.cloned.1.call-done = f32[512,128,128]{2,1,0:T(8,128)} async-done(((f32[32,128,128]{2,1,0:T(8,128)}), f32[512,128,128]{2,1,0:T(8,128)}) %all-gather.5.cloned.1.call-update) | async-done | bytes 33554448 | tf_op jit(solution)/shard_map/all_gather | solution.py:14
  367.3 37.4 %while.30 = (s32[]{:T(128)}, f32[32,128,128]{2,1,0:T(8,128)S(1)}, s32[]{:T(128)}, f32[16,32,128,128]{3,2,1,0:T(8,128)}, s32[]{:T(128)}, /*index=5*/s32[]{:T(128)}) while((s32[]{:T(128)}, f32[32,128,128]{2,1,0:T(8,128)S(1)}, s32[]{:T(128)}, f32[16,32,128,128]{3,2,1,0:T(8,128)}, s32[]{:T(128)}, /*index=5*/s32[]{:T(128)}) %tuple.87), condition=%wide.region_1.2_spmd.clone, body=%wide.region_0.1_spmd.clone.sunk | while | flops 1572868 | bytes 6291557 | solution.py:23
  369.6 2.3 add_select_fusion.4
  371.9 2.3 add_select_fusion.4
  374.3 2.3 add_select_fusion.4
  376.6 2.3 add_select_fusion.4
  378.9 2.3 add_select_fusion.4
  381.3 2.3 add_select_fusion.4
  383.6 2.3 add_select_fusion.4
  388.3 2.3 add_select_fusion.4
  390.6 2.3 add_select_fusion.4
  393.0 2.3 add_select_fusion.4
  395.3 2.3 add_select_fusion.4
  404.6 4.5 multiply_reduce_fusion.1
  412.6 2.5 all-reduce
  415.1 2.7 multiply_convert_fusion
  421.2 2.9 copy.48
  424.2 2.5 select_convert_fusion
  430.4 2.4 copy.53
  432.8 3.4 fusion.30
  436.3 337.1 %all-gather.7.cloned.1.call-done = f32[512,128,128]{2,1,0:T(8,128)} async-done(((f32[32,128,128]{2,1,0:T(8,128)}), f32[512,128,128]{2,1,0:T(8,128)}) %all-gather.7.cloned.1.call-update) | async-done | bytes 33554448 | tf_op jit(solution)/shard_map/all_gather | solution.py:14
  773.4 37.4 %while.31 = (s32[]{:T(128)}, f32[32,128,128]{2,1,0:T(8,128)S(1)}, s32[]{:T(128)}, f32[16,32,128,128]{3,2,1,0:T(8,128)}, s32[]{:T(128)}, /*index=5*/s32[]{:T(128)}, s32[]{:T(128)}, s32[]{:T(128)}) while((s32[]{:T(128)}, f32[32,128,128]{2,1,0:T(8,128)S(1)}, s32[]{:T(128)}, f32[16,32,128,128]{3,2,1,0:T(8,128)}, s32[]{:T(128)}, ...), condition=%wide.region_7.8_spmd.clone, body=%wide.region_6.7_spmd.clone.sunk | while | flops 1572872 | bytes 6291619 | solution.py:23
  816.8 3.8 add_convert_fusion
  (69 shorter events, 76.6 us)
Async XLA Ops:
  7.2 6.5 copy-start
  7.2 360.1 %all-gather.5.cloned.1.call-start = ((), (), s32[]{:S(2)}) async-start(), calls=%async_computation | async-start | bytes 35651584 | tf_op jit(solution)/shard_map/all_gather | solution.py:14
  7.2 4.5 copy-start.5
  11.8 1.8 copy-start.7
  13.6 759.8 %all-gather.7.cloned.1.call-start = ((), (), s32[]{:S(2)}) async-start(), calls=%async_computation.1 | async-start | bytes 35651584 | tf_op jit(solution)/shard_map/all_gather | solution.py:14
  13.6 3.1 copy-start.6
  15.8 0.9 copy-start.11
  404.6 4.5 copy-start.1
  409.1 1.9 copy-start.12
  419.4 1.8 copy-start.3
  424.2 2.5 copy-start.8
  426.7 1.0 copy-start.9
  426.7 2.0 copy-start.2
  426.7 2.2 copy-start.4
  810.8 2.2 copy-start.10
Sparse Core Ops, SparseCore 0:
  13.7 353.5 all-gather.4
  424.3 349.0 all-gather.6
where the time goes:
time: 831 us; the launch traced here: 830 us
  waiting for transfers between devices  685 us (82%)
  other arithmetic  78.3 us (9%)
  matrix products  28.1 us (3%)
  local copies, waits for them, and re-layouts  20.3 us (2%)
  between operations  14.2 us (2%)
    all_gather x2, waiting for transfers between devices, entering(): everything = lax.all_gather(value, axis)  685 us
    select_n x32, other arithmetic, step(): return jnp.where(reached, new, before)  74 us
  transfers between devices with their start and end apart: 2, of which 2 were waited for; matrix products, arithmetic and copies ran while one was open for 2% of the time, Pallas kernels for 0%

commit v1 on v0

v1 whole, which is shorter than its diff:
```python
import functools
import math

import jax
import jax.numpy as jnp
from jax import lax
from jax.experimental import pallas as pl
from jax.experimental.pallas import tpu as pltpu
from jax.sharding import PartitionSpec as P

HEAD_DIM = 128
GROUPS = 2
PLANE = 4

epsilon = 1e-05

CONTRACT_ROWS = (((0,), (0,)), ((), ()))
CONTRACT_COLUMNS = (((1,), (1,)), ((), ()))


def dot(a, b, dims=(((1,), (0,)), ((), ()))):
    return lax.dot_general(a, b, dims, preferred_element_type=jnp.float32)


def call(body, outs, *args, flops=0, aliases=None):
    moved = sum(math.prod(a.shape) * a.dtype.itemsize for a in (*args, *outs))
    return pl.pallas_call(
        body,
        out_shape=outs,
        in_specs=[pl.BlockSpec(memory_space=pltpu.VMEM)] * len(args),
        out_specs=[pl.BlockSpec(memory_space=pltpu.VMEM)] * len(outs),
        input_output_aliases=aliases or {},
        cost_estimate=pl.CostEstimate(flops=flops, bytes_accessed=moved, transcendentals=0),
        compiler_params=pltpu.CompilerParams(vmem_limit_bytes=40 * 1024 * 1024),
    )(*args)


def f32(*shape):
    return jax.ShapeDtypeStruct(shape, jnp.float32)


def bf16(*shape):
    return jax.ShapeDtypeStruct(shape, jnp.bfloat16)


def place():
    me = lax.axis_index("seq")
    return lax.rem(me, PLANE), lax.div(me, PLANE)


def weight(condition):
    return jnp.where(condition, 1.0, 0.0).astype(jnp.float32)


def head_columns(group, owner, per_owner, j):
    return pl.ds(pl.multiple_of(((group * PLANE + owner) * per_owner + j) * HEAD_DIM, HEAD_DIM), HEAD_DIM)


def causal(tokens):
    rows_index = lax.broadcasted_iota(jnp.int32, (tokens, tokens), 0)
    cols_index = lax.broadcasted_iota(jnp.int32, (tokens, tokens), 1)
    return rows_index >= cols_index


def total_kernel(lines, *refs):
    parts, outs = refs[:PLANE], refs[PLANE:]
    _, z = place()
    rows = outs[0].shape[0]
    for k in range(lines):
        at = pl.ds(pl.multiple_of(lax.rem(z + k, lines) * rows, 8), rows)
        total = parts[0][at, :]
        for part in parts[1:]:
            total = total + part[at, :]
        outs[k][...] = total


def line_kernel(lines, reverse, *refs):
    pieces, outs = refs[:lines], refs[lines:]
    _, z = place()
    for k in range(lines):
        target = lax.rem(z + k, lines)
        total = None
        for j in range(lines):
            source = lax.rem(z + lines - j, lines)
            before = source > target if reverse else source < target
            term = pieces[j][...] * weight(before)
            total = term if total is None else total + term
        outs[k][...] = total


def spread_kernel(lines, reverse, *refs):
    entering, parts, outs = refs[:lines], refs[lines : lines + PLANE], refs[lines + PLANE :]
    p, z = place()
    rows = entering[0].shape[0]
    for i in range(lines):
        at = pl.ds(pl.multiple_of(lax.rem(z + lines - i, lines) * rows, 8), rows)
        base = entering[i][...]
        held = [part[at, :] for part in parts]
        for k in range(PLANE):
            target = p ^ k
            total = base
            for j in range(PLANE):
                source = p ^ j
                before = source > target if reverse else source < target
                total = total + held[j] * weight(before)
            outs[k][at, :] = total


def plane_send(parts):
    n = lax.axis_size("seq")
    return [parts[0]] + [
        lax.ppermute(parts[k], "seq", [(s, s ^ k) for s in range(n)]) for k in range(1, PLANE)
    ]


def line_send(pieces):
    n = lax.axis_size("seq")
    return [pieces[0]] + [
        lax.ppermute(pieces[k], "seq", [(s, (s + PLANE * k) % n) for s in range(n)])
        for k in range(1, len(pieces))
    ]


def line_scan_long(parts, reverse):
    n = lax.axis_size("seq")
    lines = n // PLANE
    z = lax.axis_index("seq") // PLANE
    total = sum(parts)
    groups = [[i + PLANE * l for l in range(lines)] for i in range(PLANE)]
    send = functools.partial(
        lax.all_to_all, axis_name="seq", split_axis=0, concat_axis=0, axis_index_groups=groups, tiled=True
    )
    every = send(total).reshape(lines, -1, HEAD_DIM)
    inclusive = lax.cumsum(every, axis=0, reverse=reverse)
    zero = jnp.zeros_like(every[:1])
    before = (
        jnp.concatenate([inclusive[1:], zero]) if reverse else jnp.concatenate([zero, inclusive[:-1]])
    )
    entering = send(before.reshape(total.shape)).reshape(lines, -1, HEAD_DIM)
    return [
        lax.dynamic_index_in_dim(entering, (z + lines - i) % lines, 0, keepdims=False) for i in range(lines)
    ]


def scan_states(groups, reverse):
    lines = lax.axis_size("seq") // PLANE
    rows = groups[0][0].shape[0]
    piece = rows // lines
    results = []
    for parts in groups:
        parts = plane_send(parts)
        if lines <= 4:
            pieces = call(functools.partial(total_kernel, lines), [f32(piece, HEAD_DIM)] * lines, *parts)
            pieces = line_send(pieces)
            pieces = call(functools.partial(line_kernel, lines, reverse), [f32(piece, HEAD_DIM)] * lines, *pieces)
            entering = line_send(pieces)
        else:
            entering = line_scan_long(parts, reverse)
        outs = call(
            functools.partial(spread_kernel, lines, reverse), [f32(rows, HEAD_DIM)] * PLANE, *entering, *parts
        )
        results.append(plane_send(outs))
    return results


def state_kernel(group, left, right, *outs):
    p, _ = place()
    per_owner = outs[0].shape[0] // HEAD_DIM
    for k in range(PLANE):
        for j in range(per_owner):
            at = head_columns(group, p ^ k, per_owner, j)
            outs[k][pl.ds(j * HEAD_DIM, HEAD_DIM), :] = dot(left[:, at], right[:, at], CONTRACT_ROWS)


def local_kernel(scale, queries, keys, values, weights, inner):
    mask = causal(queries.shape[0])
    for h in range(queries.shape[1] // HEAD_DIM):
        at = pl.ds(h * HEAD_DIM, HEAD_DIM)
        scores = dot(queries[:, at], keys[:, at], CONTRACT_COLUMNS) * scale
        w = jnp.where(mask, scores, 0.0).astype(jnp.bfloat16)
        weights[:, at] = w
        inner[:, at] = dot(w, values[:, at])


def attend_kernel(group, scale, queries, inner, cotangent, gain, *refs):
    parts, (attended, prefix_low, stats) = refs[:PLANE], refs[PLANE:]
    p, _ = place()
    per_owner = parts[0].shape[0] // HEAD_DIM
    squares = cross = None
    for k in range(PLANE):
        for j in range(per_owner):
            at = head_columns(group, p ^ k, per_owner, j)
            here = head_columns(0, p ^ k, per_owner, j)
            low = parts[k][pl.ds(j * HEAD_DIM, HEAD_DIM), :].astype(jnp.bfloat16)
            prefix_low[:, here] = low
            a = inner[:, at] + scale * dot(queries[:, at], low)
            attended[:, here] = a
            scaled = cotangent[:, at].astype(jnp.float32) * gain[:, at]
            squares = a * a if squares is None else squares + a * a
            cross = scaled * a if cross is None else cross + scaled * a
    stats[0] = squares
    stats[1] = cross


def grad_kernel(group, width, queries, cotangent, gain, stats, attended, grad, *outs):
    p, _ = place()
    per_owner = outs[0].shape[0] // HEAD_DIM
    inverse_rms = lax.rsqrt(jnp.sum(stats[0], axis=1, keepdims=True) / width + epsilon)
    cross = jnp.sum(stats[1], axis=1, keepdims=True) * inverse_rms / width
    for k in range(PLANE):
        for j in range(per_owner):
            at = head_columns(group, p ^ k, per_owner, j)
            here = head_columns(0, p ^ k, per_owner, j)
            normed = attended[:, here] * inverse_rms
            scaled = cotangent[:, at].astype(jnp.float32) * gain[:, at]
            g = ((scaled - normed * cross) * inverse_rms).astype(jnp.bfloat16)
            grad[:, here] = g
            outs[k][pl.ds(j * HEAD_DIM, HEAD_DIM), :] = dot(queries[:, at], g, CONTRACT_ROWS)


def local_grad_kernel(scale, *refs):
    queries, keys, values, weights = refs[:4]
    grads, lows = refs[4 : 4 + GROUPS], refs[4 + GROUPS : 4 + 2 * GROUPS]
    query_grad, key_inner, value_inner = refs[4 + 2 * GROUPS :]
    mask = causal(queries.shape[0])
    heads = queries.shape[1] // HEAD_DIM // GROUPS
    for h in range(heads * GROUPS):
        at = pl.ds(h * HEAD_DIM, HEAD_DIM)
        here = pl.ds((h % heads) * HEAD_DIM, HEAD_DIM)
        g = grads[h // heads][:, here]
        low = lows[h // heads][:, here]
        scores = dot(g, values[:, at], CONTRACT_COLUMNS) * scale
        gw = jnp.where(mask, scores, 0.0).astype(jnp.bfloat16)
        query = dot(gw, keys[:, at]) + scale * dot(g, low, CONTRACT_COLUMNS)
        query_grad[:, at] = query.astype(jnp.bfloat16)
        key_inner[:, at] = dot(gw, queries[:, at], CONTRACT_ROWS)
        value_inner[:, at] = dot(weights[:, at], g, CONTRACT_ROWS)


def finish_kernel(scale, keys, values, key_inner, value_inner, *refs):
    parts, (key_grad, value_grad) = refs[: PLANE * GROUPS], refs[PLANE * GROUPS :]
    p, _ = place()
    per_owner = parts[0].shape[0] // HEAD_DIM
    for group in range(GROUPS):
        for k in range(PLANE):
            for j in range(per_owner):
                at = head_columns(group, p ^ k, per_owner, j)
                low = parts[group * PLANE + k][pl.ds(j * HEAD_DIM, HEAD_DIM), :].astype(jnp.bfloat16)
                key = key_inner[:, at] + scale * dot(values[:, at], low, CONTRACT_COLUMNS)
                key_grad[:, at] = key.astype(jnp.bfloat16)
                value = value_inner[:, at] + scale * dot(keys[:, at], low)
                value_grad[:, at] = value.astype(jnp.bfloat16)


def per_device(queries, keys, values, cotangent, gain):
    tokens, width = queries.shape
    total_width = width * lax.axis_size("head")
    scale = HEAD_DIM ** (-0.5)
    share = width // GROUPS
    state = f32(share // PLANE, HEAD_DIM)
    product = 2 * tokens * width * HEAD_DIM
    gain = gain[None, :]

    with jax.named_scope("state"):
        states = [
            call(functools.partial(state_kernel, g), [state] * PLANE, keys, values, flops=product // GROUPS)
            for g in range(GROUPS)
        ]
    with jax.named_scope("prefix"):
        prefixes = scan_states(states, False)
    with jax.named_scope("local"):
        weights, inner = call(
            functools.partial(local_kernel, scale),
            [bf16(tokens, width), f32(tokens, width)],
            queries, keys, values, flops=2 * product,
        )
    with jax.named_scope("attend"):
        attended = [
            call(
                functools.partial(attend_kernel, g, scale),
                [f32(tokens, share), bf16(HEAD_DIM, share), f32(2, tokens, HEAD_DIM)],
                queries, inner, cotangent, gain, *prefixes[g], flops=product // GROUPS,
            )
            for g in range(GROUPS)
        ]
        stats = lax.psum(sum(a[2] for a in attended), "head")
    with jax.named_scope("grad"):
        grads = [
            call(
                functools.partial(grad_kernel, g, total_width),
                [bf16(tokens, share)] + [state] * PLANE,
                queries, cotangent, gain, stats, attended[g][0], flops=product // GROUPS,
            )
            for g in range(GROUPS)
        ]
    with jax.named_scope("suffix"):
        suffixes = scan_states([g[1:] for g in grads], True)
    with jax.named_scope("local_grad"):
        query_grad, key_inner, value_inner = call(
            functools.partial(local_grad_kernel, scale),
            [bf16(tokens, width), f32(tokens, width), f32(tokens, width)],
            queries, keys, values, weights, *[g[0] for g in grads], *[a[1] for a in attended],
            flops=5 * product,
        )
    with jax.named_scope("finish"):
        key_grad, value_grad = call(
            functools.partial(finish_kernel, scale),
            [bf16(tokens, width)] * 2,
            keys, values, key_inner, value_inner, *[s for group in suffixes for s in group],
            flops=2 * product,
        )
    return query_grad, key_grad, value_grad


def solution(mesh):
    return jax.shard_map(
        per_device,
        mesh=mesh,
        in_specs=(P("seq", "head"), P("seq", "head"), P("seq", "head"), P("seq", "head"), P("head")),
        out_specs=(P("seq", "head"), P("seq", "head"), P("seq", "head")),
        check_vma=False,
    )
```

time: 831 us -> 182 us (0.22)
  waiting for transfers between devices: 685 us -> 71.6 us
  other arithmetic: 78.3 us -> 0.67 us
  starting transfers between devices: 0.08 us -> 66 us
  matrix products: 28.1 us -> 0 us
  Pallas kernels: 0 us -> 20.8 us
  local copies, waits for them, and re-layouts: 20.3 us -> 8.71 us
    all_gather x2 -> x0, waiting for transfers between devices: 685 us -> none  [entering(): everything = lax.all_gather(value, axis)]
    select_n x32 -> x0, other arithmetic: 74 us -> none  [step(): return jnp.where(reached, new, before)]
    ppermute x0 -> x48, starting transfers between devices: none -> 65.9 us  [the longest x24 35.1 us: line_send(): lax.ppermute(pieces[k], 'seq', [(s, (s + PLANE * k) % n) for s in range(n)])]
    ppermute x0 -> x48, waiting for transfers between devices: none -> 54.4 us  [the longest x24 29.3 us: plane_send(): lax.ppermute(parts[k], 'seq', [(s, s ^ k) for s in range(n)])]
    dot_general x12 -> x0, matrix products: 28.1 us -> none  [the longest x1 4.46 us: per_device(): jnp.einsum('thd,hde->the', query_heads, prefix_low, preferred_element_typ...]
    pallas_call x0 -> x21, Pallas kernels: none -> 20.8 us  [call(): pl.pallas_call(body, out_shape=outs, in_specs=[pl.BlockSpec(memory_space=...]
    psum x0 -> x1, waiting for transfers between devices: none -> 17.2 us  [per_device(): stats = lax.psum(sum((a[2] for a in attended)), 'head')]
  transfers between devices with their start and end apart: 2 -> 49, of which waited for: 2 -> 22; matrix products, arithmetic and copies ran while one was open for 2% -> 0% of each run, Pallas kernels for 0% -> 9%
where the time goes in v1:
time: 182 us
  waiting for transfers between devices  71.6 us (39%)
  starting transfers between devices  66 us (36%)
  Pallas kernels  20.8 us (11%)
  between operations  14.3 us (8%)
  local copies, waits for them, and re-layouts  8.71 us (5%)
    ppermute x24, starting transfers between devices, line_send(): lax.ppermute(pieces[k], 'seq', [(s, (s + PLANE * k) % n) for s in range(n)])  35.1 us
    ppermute x24, starting transfers between devices, plane_send(): lax.ppermute(parts[k], 'seq', [(s, s ^ k) for s in range(n)])  30.8 us
    ppermute x24, waiting for transfers between devices, plane_send(): lax.ppermute(parts[k], 'seq', [(s, s ^ k) for s in range(n)])  29.3 us
    ppermute x24, waiting for transfers between devices, line_send(): lax.ppermute(pieces[k], 'seq', [(s, (s + PLANE * k) % n) for s in range(n)])  25.1 us
    pallas_call x21, Pallas kernels, call(): pl.pallas_call(body, out_shape=outs, in_specs=[pl.BlockSpec(memory_space=...  20.8 us
    psum x1, waiting for transfers between devices, per_device(): stats = lax.psum(sum((a[2] for a in attended)), 'head')  17.2 us
    unnamed x42, local copies, waits for them, and re-layouts  8.71 us
  transfers between devices with their start and end apart: 49, of which 22 were waited for; matrix products, arithmetic and copies ran while one was open for 0% of the time, Pallas kernels for 9%

profile of v1, /device:TPU:0, one launch (start us, length us, event | category | flops | bytes accessed | tf_op | source)
XLA Modules:
  0.0 182.0 jit_solution(16245750516868649981)
XLA Ops:
  10.1 3.0 %collective-permute-start.12 = (f32[512,128]{1,0:T(8,128)S(1)}, f32[512,128]{1,0:T(8,128)S(1)}, u32[]{:S(2)}, u32[]{:S(2)}) collective-permute-start(f32[512,128]{1,0:T(8,128)S(1)} %get-tuple-element.102), channel_id=1, source_target_pairs={{0,2},{2,0},{4,6},{6,4},{8,10},{10,8},{12,14},{14,12},{16,18},{18,... | collective-permute-start | bytes 786440 | tf_op jit(solution)/shard_map/prefix/ppermute | solution.py:112
  14.7 5.6 %collective-permute-done.12.refs_1_.refs_5_ = f32[512,128]{1,0:T(8,128)S(1)} collective-permute-done((f32[512,128]{1,0:T(8,128)S(1)}, f32[512,128]{1,0:T(8,128)S(1)}, u32[]{:S(2)}, u32[]{:S(2)}) %collective-permute-start.12) | collective-permute-done | bytes 262176 | tf_op jit(solution)/shard_map/prefix/ppermute | solution.py:112
  20.3 6.2 %collective-permute-done.13.refs_2_.refs_6_ = f32[512,128]{1,0:T(8,128)S(1)} collective-permute-done((f32[512,128]{1,0:T(8,128)S(1)}, f32[512,128]{1,0:T(8,128)S(1)}, u32[]{:S(2)}, u32[]{:S(2)}) %collective-permute-start.13) | collective-permute-done | bytes 262176 | tf_op jit(solution)/shard_map/prefix/ppermute | solution.py:112
  28.2 2.6 %collective-permute-start.16 = (f32[128,128]{1,0:T(8,128)S(1)}, f32[128,128]{1,0:T(8,128)S(1)}, u32[]{:S(2)}, u32[]{:S(2)}) collective-permute-start(f32[128,128]{1,0:T(8,128)S(1)} %get-tuple-element.107), channel_id=1, source_target_pairs={{0,16},{2,18},{4,20},{6,22},{8,24},{10,26},{12,28},{14,30},{16,0},... | collective-permute-start | bytes 196616 | tf_op jit(solution)/shard_map/prefix/ppermute | solution.py:119
  39.0 3.6 %collective-permute-done.18.refs_1_ = f32[128,128]{1,0:T(8,128)S(1)} collective-permute-done((f32[128,128]{1,0:T(8,128)S(1)}, f32[128,128]{1,0:T(8,128)S(1)}, u32[]{:S(2)}, u32[]{:S(2)}) %collective-permute-start.18) | collective-permute-done | bytes 65568 | tf_op jit(solution)/shard_map/prefix/ppermute | solution.py:119
  43.6 3.2 %collective-permute-done.20.refs_3_ = f32[128,128]{1,0:T(8,128)S(1)} collective-permute-done((f32[128,128]{1,0:T(8,128)S(1)}, f32[128,128]{1,0:T(8,128)S(1)}, u32[]{:S(2)}, u32[]{:S(2)}) %collective-permute-start.20) | collective-permute-done | bytes 65568 | tf_op jit(solution)/shard_map/prefix/ppermute | solution.py:119
  48.6 3.1 %collective-permute-start.4 = (f32[128,128]{1,0:T(8,128)S(1)}, f32[128,128]{1,0:T(8,128)S(1)}, u32[]{:S(2)}, u32[]{:S(2)}) collective-permute-start(f32[128,128]{1,0:T(8,128)S(1)} %get-tuple-element.90), channel_id=1, source_target_pairs={{0,16},{2,18},{4,20},{6,22},{8,24},{10,26},{12,28},{14,30},{16,0},... | collective-permute-start | bytes 196616 | tf_op jit(solution)/shard_map/prefix/ppermute | solution.py:119
  52.4 2.4 %collective-permute-done.3.refs_1_ = f32[128,128]{1,0:T(8,128)S(1)} collective-permute-done((f32[128,128]{1,0:T(8,128)S(1)}, f32[128,128]{1,0:T(8,128)S(1)}, u32[]{:S(2)}, u32[]{:S(2)}) %collective-permute-start.3) | collective-permute-done | bytes 65568 | tf_op jit(solution)/shard_map/prefix/ppermute | solution.py:119
  59.0 2.6 %collective-permute-start.7 = (f32[128,128]{1,0:T(8,128)S(1)}, f32[128,128]{1,0:T(8,128)S(1)}, u32[]{:S(2)}, u32[]{:S(2)}) collective-permute-start(f32[128,128]{1,0:T(8,128)S(1)} %get-tuple-element.94), channel_id=1, source_target_pairs={{0,16},{2,18},{4,20},{6,22},{8,24},{10,26},{12,28},{14,30},{16,0},... | collective-permute-start | bytes 196616 | tf_op jit(solution)/shard_map/prefix/ppermute | solution.py:119
  63.2 2.5 %collective-permute-start.23 = (f32[512,128]{1,0:T(8,128)S(1)}, f32[512,128]{1,0:T(8,128)S(1)}, u32[]{:S(2)}, u32[]{:S(2)}) collective-permute-start(f32[512,128]{1,0:T(8,128)S(1)} %get-tuple-element.116), channel_id=1, source_target_pairs={{0,6},{2,4},{4,2},{6,0},{8,14},{10,12},{12,10},{14,8},{16,22},{18,... | collective-permute-start | bytes 786440 | tf_op jit(solution)/shard_map/prefix/ppermute | solution.py:112
  69.7 5.1 %local.1 = (bf16[128,4096]{1,0:T(8,128)(2,1)S(1)}, f32[128,4096]{1,0:T(8,128)S(1)}) custom-call(bf16[128,4096]{1,0:T(8,128)(2,1)S(1)} %copy-done, bf16[128,4096]{1,0:T(8,128)(2,1)S(1)} %copy-done.2, bf16[128,4096]{1,0:T(8,128)(2,1)S(1)} %copy-done.4), custom_call_target="tpu_custom_call" | custom-call | flops 268435456 | bytes 6291456 | tf_op jit(solution)/shard_map/local/pallas_call | solution.py:27
  76.5 2.5 %collective-permute-done.10.refs_2_ = f32[512,128]{1,0:T(8,128)S(1)} collective-permute-done((f32[512,128]{1,0:T(8,128)S(1)}, f32[512,128]{1,0:T(8,128)S(1)}, u32[]{:S(2)}, u32[]{:S(2)}) %collective-permute-start.10) | collective-permute-done | bytes 262176 | tf_op jit(solution)/shard_map/prefix/ppermute | solution.py:112
  82.1 17.2 %all-reduce.2.cloned.1.call-done.stats = f32[2,128,128]{2,1,0:T(8,128)} async-done(((f32[2,128,128]{2,1,0:T(8,128)}), f32[2,128,128]{2,1,0:T(8,128)}) %all-reduce.2.cloned.1.call-update) | async-done | bytes 131088 | tf_op jit(solution)/shard_map/attend/psum | solution.py:286
  107.0 5.6 %collective-permute-done.36.refs_1_.refs_5_ = f32[512,128]{1,0:T(8,128)S(1)} collective-permute-done((f32[512,128]{1,0:T(8,128)S(1)}, f32[512,128]{1,0:T(8,128)S(1)}, u32[]{:S(2)}, u32[]{:S(2)}) %collective-permute-start.36) | collective-permute-done | bytes 262176 | tf_op jit(solution)/shard_map/suffix/ppermute | solution.py:112
  112.6 6.4 %collective-permute-done.37.refs_2_.refs_6_ = f32[512,128]{1,0:T(8,128)S(1)} collective-permute-done((f32[512,128]{1,0:T(8,128)S(1)}, f32[512,128]{1,0:T(8,128)S(1)}, u32[]{:S(2)}, u32[]{:S(2)}) %collective-permute-start.37) | collective-permute-done | bytes 262176 | tf_op jit(solution)/shard_map/suffix/ppermute | solution.py:112
  120.6 2.4 %collective-permute-start.40 = (f32[128,128]{1,0:T(8,128)S(1)}, f32[128,128]{1,0:T(8,128)S(1)}, u32[]{:S(2)}, u32[]{:S(2)}) collective-permute-start(f32[128,128]{1,0:T(8,128)S(1)} %get-tuple-element.149), channel_id=1, source_target_pairs={{0,16},{2,18},{4,20},{6,22},{8,24},{10,26},{12,28},{14,30},{16,0},... | collective-permute-start | bytes 196616 | tf_op jit(solution)/shard_map/suffix/ppermute | solution.py:119
  131.3 3.9 %collective-permute-done.42.refs_1_ = f32[128,128]{1,0:T(8,128)S(1)} collective-permute-done((f32[128,128]{1,0:T(8,128)S(1)}, f32[128,128]{1,0:T(8,128)S(1)}, u32[]{:S(2)}, u32[]{:S(2)}) %collective-permute-start.42) | collective-permute-done | bytes 65568 | tf_op jit(solution)/shard_map/suffix/ppermute | solution.py:119
  136.8 2.6 %collective-permute-done.44.refs_3_ = f32[128,128]{1,0:T(8,128)S(1)} collective-permute-done((f32[128,128]{1,0:T(8,128)S(1)}, f32[128,128]{1,0:T(8,128)S(1)}, u32[]{:S(2)}, u32[]{:S(2)}) %collective-permute-start.44) | collective-permute-done | bytes 65568 | tf_op jit(solution)/shard_map/suffix/ppermute | solution.py:119
  141.4 2.5 %collective-permute-start.28 = (f32[128,128]{1,0:T(8,128)S(1)}, f32[128,128]{1,0:T(8,128)S(1)}, u32[]{:S(2)}, u32[]{:S(2)}) collective-permute-start(f32[128,128]{1,0:T(8,128)S(1)} %get-tuple-element.133), channel_id=1, source_target_pairs={{0,16},{2,18},{4,20},{6,22},{8,24},{10,26},{12,28},{14,30},{16,0},... | collective-permute-start | bytes 196616 | tf_op jit(solution)/shard_map/suffix/ppermute | solution.py:119
  145.2 2.2 %collective-permute-done.27.refs_1_ = f32[128,128]{1,0:T(8,128)S(1)} collective-permute-done((f32[128,128]{1,0:T(8,128)S(1)}, f32[128,128]{1,0:T(8,128)S(1)}, u32[]{:S(2)}, u32[]{:S(2)}) %collective-permute-start.27) | collective-permute-done | bytes 65568 | tf_op jit(solution)/shard_map/suffix/ppermute | solution.py:119
  148.2 3.8 %collective-permute-start.30 = (f32[128,128]{1,0:T(8,128)S(1)}, f32[128,128]{1,0:T(8,128)S(1)}, u32[]{:S(2)}, u32[]{:S(2)}) collective-permute-start(f32[128,128]{1,0:T(8,128)S(1)} %get-tuple-element.136), channel_id=1, source_target_pairs={{0,8},{2,10},{4,12},{6,14},{8,16},{10,18},{12,20},{14,22},{16,24},... | collective-permute-start | bytes 196616 | tf_op jit(solution)/shard_map/suffix/ppermute | solution.py:119
  162.0 7.8 %local_grad.1 = (bf16[128,4096]{1,0:T(8,128)(2,1)}, f32[128,4096]{1,0:T(8,128)S(1)}, f32[128,4096]{1,0:T(8,128)S(1)}) custom-call(bf16[128,4096]{1,0:T(8,128)(2,1)S(1)} %copy-done, bf16[128,4096]{1,0:T(8,128)(2,1)S(1)} %copy-done.2, bf16[128,4096]{1,0:T(8,128)(2,1)S(1)} %copy-done.4, bf16[128,4096]{1,0:T(8,128)(2,1)S(1)} %copy-done.13, ...), custom_call_target="tpu_custom_call" | custom-call | flops 671088640 | bytes 11534336 | tf_op jit(solution)/shard_map/local_grad/pallas_call | solution.py:27
  169.8 2.8 %collective-permute-done.34.refs_2_ = f32[512,128]{1,0:T(8,128)S(1)} collective-permute-done((f32[512,128]{1,0:T(8,128)S(1)}, f32[512,128]{1,0:T(8,128)S(1)}, u32[]{:S(2)}, u32[]{:S(2)}) %collective-permute-start.34) | collective-permute-done | bytes 262176 | tf_op jit(solution)/shard_map/suffix/ppermute | solution.py:112
  172.6 2.6 %finish.1 = (bf16[128,4096]{1,0:T(8,128)(2,1)}, bf16[128,4096]{1,0:T(8,128)(2,1)}) custom-call(bf16[128,4096]{1,0:T(8,128)(2,1)S(1)} %copy-done.2, bf16[128,4096]{1,0:T(8,128)(2,1)S(1)} %copy-done.4, f32[128,4096]{1,0:T(8,128)S(1)} %get-tuple-element.125.key_inner, f32[128,4096]{1,0:T(8,128)S(1)} %get-tuple-element.126.value_inner, ...), custom_call_target="tpu_custom_call" | custom-call | flops 268435456 | bytes 10485760 | tf_op jit(solution)/shard_map/finish/pallas_call | solution.py:27
  (139 shorter events, 65.4 us)
Async XLA Ops:
  7.2 92.1 %all-reduce.2.cloned.1.call-start = ((), (), s32[]{:S(2)}) async-start(), calls=%async_computation | async-start | bytes 262144 | tf_op jit(solution)/shard_map/attend/psum | solution.py:286
  10.1 10.1 %collective-permute-start.12 = (f32[512,128]{1,0:T(8,128)S(1)}, f32[512,128]{1,0:T(8,128)S(1)}, u32[]{:S(2)}, u32[]{:S(2)}) collective-permute-start(f32[512,128]{1,0:T(8,128)S(1)} %get-tuple-element.102), channel_id=1, source_target_pairs={{0,2},{2,0},{4,6},{6,4},{8,10},{10,8},{12,14},{14,12},{16,18},{18,... | collective-permute-start | bytes 786440 | tf_op jit(solution)/shard_map/prefix/ppermute | solution.py:112
  13.1 13.4 %collective-permute-start.13 = (f32[512,128]{1,0:T(8,128)S(1)}, f32[512,128]{1,0:T(8,128)S(1)}, u32[]{:S(2)}, u32[]{:S(2)}) collective-permute-start(f32[512,128]{1,0:T(8,128)S(1)} %get-tuple-element.103), channel_id=1, source_target_pairs={{0,4},{2,6},{4,0},{6,2},{8,12},{10,14},{12,8},{14,10},{16,20},{18,... | collective-permute-start | bytes 786440 | tf_op jit(solution)/shard_map/prefix/ppermute | solution.py:112
  14.7 11.9 %collective-permute-start.14 = (f32[512,128]{1,0:T(8,128)S(1)}, f32[512,128]{1,0:T(8,128)S(1)}, u32[]{:S(2)}, u32[]{:S(2)}) collective-permute-start(f32[512,128]{1,0:T(8,128)S(1)} %get-tuple-element.104), channel_id=1, source_target_pairs={{0,6},{2,4},{4,2},{6,0},{8,14},{10,12},{12,10},{14,8},{16,22},{18,... | collective-permute-start | bytes 786440 | tf_op jit(solution)/shard_map/prefix/ppermute | solution.py:112
  32.6 15.8 %collective-permute-start = (f32[512,128]{1,0:T(8,128)S(1)}, f32[512,128]{1,0:T(8,128)S(1)}, u32[]{:S(2)}, u32[]{:S(2)}) collective-permute-start(f32[512,128]{1,0:T(8,128)S(1)} %get-tuple-element.85), channel_id=1, source_target_pairs={{0,2},{2,0},{4,6},{6,4},{8,10},{10,8},{12,14},{14,12},{16,18},{18,... | collective-permute-start | bytes 786440 | tf_op jit(solution)/shard_map/prefix/ppermute | solution.py:112
  33.9 14.6 %collective-permute-start.1 = (f32[512,128]{1,0:T(8,128)S(1)}, f32[512,128]{1,0:T(8,128)S(1)}, u32[]{:S(2)}, u32[]{:S(2)}) collective-permute-start(f32[512,128]{1,0:T(8,128)S(1)} %get-tuple-element.86), channel_id=1, source_target_pairs={{0,4},{2,6},{4,0},{6,2},{8,12},{10,14},{12,8},{14,10},{16,20},{18,... | collective-permute-start | bytes 786440 | tf_op jit(solution)/shard_map/prefix/ppermute | solution.py:112
  34.7 13.7 %collective-permute-start.2 = (f32[512,128]{1,0:T(8,128)S(1)}, f32[512,128]{1,0:T(8,128)S(1)}, u32[]{:S(2)}, u32[]{:S(2)}) collective-permute-start(f32[512,128]{1,0:T(8,128)S(1)} %get-tuple-element.87), channel_id=1, source_target_pairs={{0,6},{2,4},{4,2},{6,0},{8,14},{10,12},{12,10},{14,8},{16,22},{18,... | collective-permute-start | bytes 786440 | tf_op jit(solution)/shard_map/prefix/ppermute | solution.py:112
  47.2 21.4 %collective-permute-start.21 = (f32[512,128]{1,0:T(8,128)S(1)}, f32[512,128]{1,0:T(8,128)S(1)}, u32[]{:S(2)}, u32[]{:S(2)}) collective-permute-start(f32[512,128]{1,0:T(8,128)S(1)} %get-tuple-element.114), channel_id=1, source_target_pairs={{0,2},{2,0},{4,6},{6,4},{8,10},{10,8},{12,14},{14,12},{16,18},{18,... | collective-permute-start | bytes 786440 | tf_op jit(solution)/shard_map/prefix/ppermute | solution.py:112
  61.6 13.2 %collective-permute-start.22 = (f32[512,128]{1,0:T(8,128)S(1)}, f32[512,128]{1,0:T(8,128)S(1)}, u32[]{:S(2)}, u32[]{:S(2)}) collective-permute-start(f32[512,128]{1,0:T(8,128)S(1)} %get-tuple-element.115), channel_id=1, source_target_pairs={{0,4},{2,6},{4,0},{6,2},{8,12},{10,14},{12,8},{14,10},{16,20},{18,... | collective-permute-start | bytes 786440 | tf_op jit(solution)/shard_map/prefix/ppermute | solution.py:112
  63.2 11.6 %collective-permute-start.23 = (f32[512,128]{1,0:T(8,128)S(1)}, f32[512,128]{1,0:T(8,128)S(1)}, u32[]{:S(2)}, u32[]{:S(2)}) collective-permute-start(f32[512,128]{1,0:T(8,128)S(1)} %get-tuple-element.116), channel_id=1, source_target_pairs={{0,6},{2,4},{4,2},{6,0},{8,14},{10,12},{12,10},{14,8},{16,22},{18,... | collective-permute-start | bytes 786440 | tf_op jit(solution)/shard_map/prefix/ppermute | solution.py:112
  66.1 10.4 %collective-permute-start.9 = (f32[512,128]{1,0:T(8,128)S(1)}, f32[512,128]{1,0:T(8,128)S(1)}, u32[]{:S(2)}, u32[]{:S(2)}) collective-permute-start(f32[512,128]{1,0:T(8,128)S(1)} %get-tuple-element.97), channel_id=1, source_target_pairs={{0,2},{2,0},{4,6},{6,4},{8,10},{10,8},{12,14},{14,12},{16,18},{18,... | collective-permute-start | bytes 786440 | tf_op jit(solution)/shard_map/prefix/ppermute | solution.py:112
  67.1 11.9 %collective-permute-start.10 = (f32[512,128]{1,0:T(8,128)S(1)}, f32[512,128]{1,0:T(8,128)S(1)}, u32[]{:S(2)}, u32[]{:S(2)}) collective-permute-start(f32[512,128]{1,0:T(8,128)S(1)} %get-tuple-element.98), channel_id=1, source_target_pairs={{0,4},{2,6},{4,0},{6,2},{8,12},{10,14},{12,8},{14,10},{16,20},{18,... | collective-permute-start | bytes 786440 | tf_op jit(solution)/shard_map/prefix/ppermute | solution.py:112
  68.6 10.4 %collective-permute-start.11 = (f32[512,128]{1,0:T(8,128)S(1)}, f32[512,128]{1,0:T(8,128)S(1)}, u32[]{:S(2)}, u32[]{:S(2)}) collective-permute-start(f32[512,128]{1,0:T(8,128)S(1)} %get-tuple-element.99), channel_id=1, source_target_pairs={{0,6},{2,4},{4,2},{6,0},{8,14},{10,12},{12,10},{14,8},{16,22},{18,... | collective-permute-start | bytes 786440 | tf_op jit(solution)/shard_map/prefix/ppermute | solution.py:112
  105.2 13.9 %collective-permute-start.37 = (f32[512,128]{1,0:T(8,128)S(1)}, f32[512,128]{1,0:T(8,128)S(1)}, u32[]{:S(2)}, u32[]{:S(2)}) collective-permute-start(f32[512,128]{1,0:T(8,128)S(1)} %get-tuple-element.145), channel_id=1, source_target_pairs={{0,4},{2,6},{4,0},{6,2},{8,12},{10,14},{12,8},{14,10},{16,20},{18,... | collective-permute-start | bytes 786440 | tf_op jit(solution)/shard_map/suffix/ppermute | solution.py:112
  106.7 12.4 %collective-permute-start.38 = (f32[512,128]{1,0:T(8,128)S(1)}, f32[512,128]{1,0:T(8,128)S(1)}, u32[]{:S(2)}, u32[]{:S(2)}) collective-permute-start(f32[512,128]{1,0:T(8,128)S(1)} %get-tuple-element.146), channel_id=1, source_target_pairs={{0,6},{2,4},{4,2},{6,0},{8,14},{10,12},{12,10},{14,8},{16,22},{18,... | collective-permute-start | bytes 786440 | tf_op jit(solution)/shard_map/suffix/ppermute | solution.py:112
  125.2 16.0 %collective-permute-start.24 = (f32[512,128]{1,0:T(8,128)S(1)}, f32[512,128]{1,0:T(8,128)S(1)}, u32[]{:S(2)}, u32[]{:S(2)}) collective-permute-start(f32[512,128]{1,0:T(8,128)S(1)} %get-tuple-element.128), channel_id=1, source_target_pairs={{0,2},{2,0},{4,6},{6,4},{8,10},{10,8},{12,14},{14,12},{16,18},{18,... | collective-permute-start | bytes 786440 | tf_op jit(solution)/shard_map/suffix/ppermute | solution.py:112
  126.5 14.7 %collective-permute-start.25 = (f32[512,128]{1,0:T(8,128)S(1)}, f32[512,128]{1,0:T(8,128)S(1)}, u32[]{:S(2)}, u32[]{:S(2)}) collective-permute-start(f32[512,128]{1,0:T(8,128)S(1)} %get-tuple-element.129), channel_id=1, source_target_pairs={{0,4},{2,6},{4,0},{6,2},{8,12},{10,14},{12,8},{14,10},{16,20},{18,... | collective-permute-start | bytes 786440 | tf_op jit(solution)/shard_map/suffix/ppermute | solution.py:112
  127.3 13.9 %collective-permute-start.26 = (f32[512,128]{1,0:T(8,128)S(1)}, f32[512,128]{1,0:T(8,128)S(1)}, u32[]{:S(2)}, u32[]{:S(2)}) collective-permute-start(f32[512,128]{1,0:T(8,128)S(1)} %get-tuple-element.130), channel_id=1, source_target_pairs={{0,6},{2,4},{4,2},{6,0},{8,14},{10,12},{12,10},{14,8},{16,22},{18,... | collective-permute-start | bytes 786440 | tf_op jit(solution)/shard_map/suffix/ppermute | solution.py:112
  139.7 20.9 %collective-permute-start.45 = (f32[512,128]{1,0:T(8,128)S(1)}, f32[512,128]{1,0:T(8,128)S(1)}, u32[]{:S(2)}, u32[]{:S(2)}) collective-permute-start(f32[512,128]{1,0:T(8,128)S(1)} %get-tuple-element.156), channel_id=1, source_target_pairs={{0,2},{2,0},{4,6},{6,4},{8,10},{10,8},{12,14},{14,12},{16,18},{18,... | collective-permute-start | bytes 786440 | tf_op jit(solution)/shard_map/suffix/ppermute | solution.py:112
  154.5 15.3 %collective-permute-start.46 = (f32[512,128]{1,0:T(8,128)S(1)}, f32[512,128]{1,0:T(8,128)S(1)}, u32[]{:S(2)}, u32[]{:S(2)}) collective-permute-start(f32[512,128]{1,0:T(8,128)S(1)} %get-tuple-element.157), channel_id=1, source_target_pairs={{0,4},{2,6},{4,0},{6,2},{8,12},{10,14},{12,8},{14,10},{16,20},{18,... | collective-permute-start | bytes 786440 | tf_op jit(solution)/shard_map/suffix/ppermute | solution.py:112
  155.3 14.5 %collective-permute-start.47 = (f32[512,128]{1,0:T(8,128)S(1)}, f32[512,128]{1,0:T(8,128)S(1)}, u32[]{:S(2)}, u32[]{:S(2)}) collective-permute-start(f32[512,128]{1,0:T(8,128)S(1)} %get-tuple-element.158), channel_id=1, source_target_pairs={{0,6},{2,4},{4,2},{6,0},{8,14},{10,12},{12,10},{14,8},{16,22},{18,... | collective-permute-start | bytes 786440 | tf_op jit(solution)/shard_map/suffix/ppermute | solution.py:112
  158.4 11.4 %collective-permute-start.33 = (f32[512,128]{1,0:T(8,128)S(1)}, f32[512,128]{1,0:T(8,128)S(1)}, u32[]{:S(2)}, u32[]{:S(2)}) collective-permute-start(f32[512,128]{1,0:T(8,128)S(1)} %get-tuple-element.140), channel_id=1, source_target_pairs={{0,2},{2,0},{4,6},{6,4},{8,10},{10,8},{12,14},{14,12},{16,18},{18,... | collective-permute-start | bytes 786440 | tf_op jit(solution)/shard_map/suffix/ppermute | solution.py:112
  159.1 13.5 %collective-permute-start.34 = (f32[512,128]{1,0:T(8,128)S(1)}, f32[512,128]{1,0:T(8,128)S(1)}, u32[]{:S(2)}, u32[]{:S(2)}) collective-permute-start(f32[512,128]{1,0:T(8,128)S(1)} %get-tuple-element.141), channel_id=1, source_target_pairs={{0,4},{2,6},{4,0},{6,2},{8,12},{10,14},{12,8},{14,10},{16,20},{18,... | collective-permute-start | bytes 786440 | tf_op jit(solution)/shard_map/suffix/ppermute | solution.py:112
  160.6 12.0 %collective-permute-start.35 = (f32[512,128]{1,0:T(8,128)S(1)}, f32[512,128]{1,0:T(8,128)S(1)}, u32[]{:S(2)}, u32[]{:S(2)}) collective-permute-start(f32[512,128]{1,0:T(8,128)S(1)} %get-tuple-element.142), channel_id=1, source_target_pairs={{0,6},{2,4},{4,2},{6,0},{8,14},{10,12},{12,10},{14,8},{16,22},{18,... | collective-permute-start | bytes 786440 | tf_op jit(solution)/shard_map/suffix/ppermute | solution.py:112
  (46 other events, 430.1 us)
Sparse Core Ops, SparseCore 0:
  82.3 17.0 all-reduce.1

commit v2 on v1

v2 whole, which is shorter than its diff:
```python
import functools
import math

import jax
import jax.numpy as jnp
from jax import lax
from jax.experimental import pallas as pl
from jax.experimental.pallas import tpu as pltpu
from jax.sharding import PartitionSpec as P

HEAD_DIM = 128
GROUPS = 2
HIDDEN = 4 * 10**9
PLANE = 4

epsilon = 1e-05

CONTRACT_ROWS = (((0,), (0,)), ((), ()))
CONTRACT_COLUMNS = (((1,), (1,)), ((), ()))


def dot(a, b, dims=(((1,), (0,)), ((), ()))):
    return lax.dot_general(a, b, dims, preferred_element_type=jnp.float32)


class Chain:
    def __init__(self):
        self.last = None

    def __call__(self, body, outs, *args, flops=1):
        specs = [pl.BlockSpec(memory_space=pltpu.VMEM)] * len(args)
        kernel, operands, count = body, args, len(args)
        if self.last is not None:
            specs, operands = specs + [pl.BlockSpec(memory_space=pl.ANY)], (*args, self.last)

            def kernel(*refs):
                body(*refs[:count], *refs[count + 1 :])

        results = pl.pallas_call(
            kernel,
            out_shape=outs,
            in_specs=specs,
            out_specs=[pl.BlockSpec(memory_space=pltpu.VMEM)] * len(outs),
            cost_estimate=pl.CostEstimate(flops=flops, bytes_accessed=1, transcendentals=0),
            compiler_params=pltpu.CompilerParams(vmem_limit_bytes=16 * 1024 * 1024),
        )(*operands)
        self.last = results[-1]
        return results


def f32(*shape):
    return jax.ShapeDtypeStruct(shape, jnp.float32)


def bf16(*shape):
    return jax.ShapeDtypeStruct(shape, jnp.bfloat16)


def place():
    me = lax.axis_index("seq")
    return lax.rem(me, PLANE), lax.div(me, PLANE)


def weight(condition):
    return jnp.where(condition, 1.0, 0.0).astype(jnp.float32)


def head_columns(group, owner, per_owner, j):
    return pl.ds(pl.multiple_of(((group * PLANE + owner) * per_owner + j) * HEAD_DIM, HEAD_DIM), HEAD_DIM)


def causal(tokens):
    rows_index = lax.broadcasted_iota(jnp.int32, (tokens, tokens), 0)
    cols_index = lax.broadcasted_iota(jnp.int32, (tokens, tokens), 1)
    return rows_index >= cols_index


def exchange(value, distance):
    n = lax.axis_size("seq")
    return lax.ppermute(value, "seq", [(s, s ^ distance) for s in range(n)])


def plane_send(parts):
    return [parts[0]] + [exchange(parts[k], k) for k in range(1, PLANE)]


def bit(level):
    _, z = place()
    return lax.rem(lax.div(z, 1 << level), 2)


def half(side, rows):
    return pl.ds(pl.multiple_of(side * rows, 8), rows)


def total_kernel(level, *refs):
    parts, outs = refs[:-2], refs[-2:]
    rows = outs[0].shape[0]
    side = bit(level)
    for out, at in zip(outs, (half(side, rows), half(1 - side, rows))):
        total = parts[0][at, :]
        for part in parts[1:]:
            total = total + part[at, :]
        out[...] = total


def sum_kernel(*refs):
    total = refs[0][...]
    for part in refs[1:-1]:
        total = total + part[...]
    refs[-1][...] = total


def first(level, reverse):
    later = bit(level).astype(jnp.float32)
    return (1.0 - later, later) if reverse else (later, 1.0 - later)


def edge_kernel(level, reverse, other, mine, theirs, to_me, to_partner):
    entering = other[...] * first(level + 1, reverse)[0]
    before_me, before_partner = first(level, reverse)
    to_me[...] = entering + theirs[...] * before_me
    to_partner[...] = entering + mine[...] * before_partner


def inner_kernel(level, reverse, kept, received, mine, theirs, to_me, to_partner):
    rows = kept.shape[0]
    side = bit(level + 1)
    before_me, before_partner = first(level, reverse)
    for entering, at in ((kept, half(side, rows)), (received, half(1 - side, rows))):
        to_me[at, :] = entering[...] + theirs[at, :] * before_me
        to_partner[at, :] = entering[...] + mine[at, :] * before_partner


def spread_kernel(reverse, kept, received, *refs):
    parts, outs = refs[:PLANE], refs[PLANE:]
    p, _ = place()
    rows = kept.shape[0]
    side = bit(0)
    for base, at in ((kept, half(side, rows)), (received, half(1 - side, rows))):
        held = [part[at, :] for part in parts]
        for k in range(PLANE):
            target = p ^ k
            total = base[...]
            for j in range(PLANE):
                source = p ^ j
                before = source > target if reverse else source < target
                total = total + held[j] * weight(before)
            outs[k][at, :] = total


def line_steps(run, parts, reverse, level=0):
    levels = (lax.axis_size("seq") // PLANE).bit_length() - 1
    distance = PLANE << level
    rows = parts[0].shape[0] // 2
    mine, send = run(functools.partial(total_kernel, level), [f32(rows, HEAD_DIM)] * 2, *parts)
    theirs = exchange(send, distance)
    yield
    if level == levels - 2:
        (total,) = run(sum_kernel, [f32(rows, HEAD_DIM)], mine, theirs)
        entering = (exchange(total, 2 * distance),)
        body = edge_kernel
        yield
    else:
        entering = yield from line_steps(run, (mine, theirs), reverse, level + 1)
        body = inner_kernel
    kept, send = run(
        functools.partial(body, level, reverse), [f32(rows, HEAD_DIM)] * 2, *entering, mine, theirs
    )
    received = exchange(send, distance)
    yield
    return kept, received


def scan_steps(run, parts, reverse, results):
    parts = plane_send(parts)
    yield
    kept, received = yield from line_steps(run, parts, reverse)
    rows = parts[0].shape[0]
    outs = run(
        functools.partial(spread_kernel, reverse), [f32(rows, HEAD_DIM)] * PLANE, kept, received, *parts
    )
    results.append(plane_send(outs))


def scan_states(run, groups, reverse):
    results = []
    steps = [scan_steps(run, parts, reverse, results) for parts in groups]
    for one in steps:
        next(one)
    time, ended = 0, set()
    while len(ended) < len(steps):
        for g, one in reversed(list(enumerate(steps))):
            if g not in ended and time >= 2 * g:
                try:
                    next(one)
                except StopIteration:
                    ended.add(g)
        time += 1
    return results


def state_kernel(group, left, right, *outs):
    p, _ = place()
    per_owner = outs[0].shape[0] // HEAD_DIM
    for k in range(PLANE):
        for j in range(per_owner):
            at = head_columns(group, p ^ k, per_owner, j)
            outs[k][pl.ds(j * HEAD_DIM, HEAD_DIM), :] = dot(left[:, at], right[:, at], CONTRACT_ROWS)


def local_kernel(scale, queries, keys, values, weights, inner):
    mask = causal(queries.shape[0])
    for h in range(queries.shape[1] // HEAD_DIM):
        at = pl.ds(h * HEAD_DIM, HEAD_DIM)
        scores = dot(queries[:, at], keys[:, at], CONTRACT_COLUMNS) * scale
        w = jnp.where(mask, scores, 0.0).astype(jnp.bfloat16)
        weights[:, at] = w
        inner[:, at] = dot(w, values[:, at])


def attend_kernel(group, scale, queries, inner, cotangent, gain, *refs):
    parts, (attended, prefix_low, stats) = refs[:PLANE], refs[-3:]
    earlier = refs[PLANE:-3]
    p, _ = place()
    per_owner = parts[0].shape[0] // HEAD_DIM
    squares, cross = (earlier[0][0], earlier[0][1]) if earlier else (0.0, 0.0)
    for k in range(PLANE):
        for j in range(per_owner):
            at = head_columns(group, p ^ k, per_owner, j)
            here = head_columns(0, p ^ k, per_owner, j)
            low = parts[k][pl.ds(j * HEAD_DIM, HEAD_DIM), :].astype(jnp.bfloat16)
            prefix_low[:, here] = low
            a = inner[:, at] + scale * dot(queries[:, at], low)
            attended[:, here] = a
            scaled = cotangent[:, at].astype(jnp.float32) * gain[:, at]
            squares = squares + a * a
            cross = cross + scaled * a
    stats[0] = squares
    stats[1] = cross


def grad_kernel(group, width, queries, cotangent, gain, attended, *refs):
    p, _ = place()
    stats, (grad, *outs) = refs[: -PLANE - 1], refs[-PLANE - 1 :]
    per_owner = outs[0].shape[0] // HEAD_DIM
    squares, cross = stats[0][0], stats[0][1]
    for other in stats[1:]:
        squares, cross = squares + other[0], cross + other[1]
    inverse_rms = lax.rsqrt(jnp.sum(squares, axis=1, keepdims=True) / width + epsilon)
    cross = jnp.sum(cross, axis=1, keepdims=True) * inverse_rms / width
    for k in range(PLANE):
        for j in range(per_owner):
            at = head_columns(group, p ^ k, per_owner, j)
            here = head_columns(0, p ^ k, per_owner, j)
            normed = attended[:, here] * inverse_rms
            scaled = cotangent[:, at].astype(jnp.float32) * gain[:, at]
            g = ((scaled - normed * cross) * inverse_rms).astype(jnp.bfloat16)
            grad[:, here] = g
            outs[k][pl.ds(j * HEAD_DIM, HEAD_DIM), :] = dot(queries[:, at], g, CONTRACT_ROWS)


def local_grad_kernel(scale, *refs):
    queries, keys, values, weights = refs[:4]
    grads, lows = refs[4 : 4 + GROUPS], refs[4 + GROUPS : 4 + 2 * GROUPS]
    query_grad, key_inner, value_inner = refs[4 + 2 * GROUPS :]
    mask = causal(queries.shape[0])
    heads = queries.shape[1] // HEAD_DIM // GROUPS
    for h in range(heads * GROUPS):
        at = pl.ds(h * HEAD_DIM, HEAD_DIM)
        here = pl.ds((h % heads) * HEAD_DIM, HEAD_DIM)
        g = grads[h // heads][:, here]
        low = lows[h // heads][:, here]
        scores = dot(g, values[:, at], CONTRACT_COLUMNS) * scale
        gw = jnp.where(mask, scores, 0.0).astype(jnp.bfloat16)
        query = dot(gw, keys[:, at]) + scale * dot(g, low, CONTRACT_COLUMNS)
        query_grad[:, at] = query.astype(jnp.bfloat16)
        key_inner[:, at] = dot(gw, queries[:, at], CONTRACT_ROWS)
        value_inner[:, at] = dot(weights[:, at], g, CONTRACT_ROWS)


def finish_kernel(group, scale, keys, values, key_inner, value_inner, *refs):
    parts, (key_grad, value_grad) = refs[:PLANE], refs[-2:]
    p, _ = place()
    per_owner = parts[0].shape[0] // HEAD_DIM
    base = group if key_grad.shape == keys.shape else 0
    earlier = refs[PLANE:-2]
    share = per_owner * PLANE * HEAD_DIM
    for g in range(len(earlier) // 2):
        key_grad[:, pl.ds(g * share, share)] = earlier[2 * g][...]
        value_grad[:, pl.ds(g * share, share)] = earlier[2 * g + 1][...]
    for k in range(PLANE):
        for j in range(per_owner):
            at = head_columns(group, p ^ k, per_owner, j)
            there = head_columns(base, p ^ k, per_owner, j)
            low = parts[k][pl.ds(j * HEAD_DIM, HEAD_DIM), :].astype(jnp.bfloat16)
            key = key_inner[:, at] + scale * dot(values[:, at], low, CONTRACT_COLUMNS)
            key_grad[:, there] = key.astype(jnp.bfloat16)
            value = value_inner[:, at] + scale * dot(keys[:, at], low)
            value_grad[:, there] = value.astype(jnp.bfloat16)


def per_device(queries, keys, values, cotangent, gain):
    tokens, width = queries.shape
    ways = lax.axis_size("head")
    scale = HEAD_DIM ** (-0.5)
    share = width // GROUPS
    state = f32(share // PLANE, HEAD_DIM)
    gain = gain[None, :]
    run = Chain()

    with jax.named_scope("state"):
        states = [
            run(functools.partial(state_kernel, g), [state] * PLANE, keys, values)
            for g in range(GROUPS)
        ]
    with jax.named_scope("local"):
        weights, inner = run(
            functools.partial(local_kernel, scale),
            [bf16(tokens, width), f32(tokens, width)],
            queries, keys, values,
        )
    with jax.named_scope("prefix"):
        prefixes = scan_states(run, states, False)
    with jax.named_scope("attend"):
        attended = []
        for g in range(GROUPS):
            attended.append(
                run(
                    functools.partial(attend_kernel, g, scale),
                    [f32(tokens, share), bf16(HEAD_DIM, share), f32(2, tokens, HEAD_DIM)],
                    queries, inner, cotangent, gain, *prefixes[g], *[a[2] for a in attended[-1:]],
                    flops=HIDDEN if g < GROUPS - 1 else 1,
                )
            )
        stats = [attended[-1][2]]
        for k in range(1, ways):
            stats.append(lax.ppermute(stats[0], "head", [(h, (h + k) % ways) for h in range(ways)]))
    with jax.named_scope("grad"):
        grads = [
            run(
                functools.partial(grad_kernel, g, width * ways),
                [bf16(tokens, share)] + [state] * PLANE,
                queries, cotangent, gain, attended[g][0], *stats,
            )
            for g in range(GROUPS)
        ]
    with jax.named_scope("local_grad"):
        query_grad, key_inner, value_inner = run(
            functools.partial(local_grad_kernel, scale),
            [bf16(tokens, width), f32(tokens, width), f32(tokens, width)],
            queries, keys, values, weights, *[g[0] for g in grads], *[a[1] for a in attended],
        )
    with jax.named_scope("suffix"):
        suffixes = scan_states(run, [g[1:] for g in grads], True)
    with jax.named_scope("finish"):
        done = []
        for g in range(GROUPS):
            last = g == GROUPS - 1
            done += run(
                functools.partial(finish_kernel, g, scale),
                [bf16(tokens, width if last else share)] * 2,
                keys, values, key_inner, value_inner, *suffixes[g], *(done if last else []),
                flops=1 if last else HIDDEN,
            )
        key_grad, value_grad = done[-2:]
    return query_grad, key_grad, value_grad


def solution(mesh):
    return jax.shard_map(
        per_device,
        mesh=mesh,
        in_specs=(P("seq", "head"), P("seq", "head"), P("seq", "head"), P("seq", "head"), P("head")),
        out_specs=(P("seq", "head"), P("seq", "head"), P("seq", "head")),
        check_vma=False,
    )
```

time: 182 us -> 129 us (0.71)
  starting transfers between devices: 66 us -> 47.3 us
  waiting for transfers between devices: 71.6 us -> 57.7 us
  between operations: 14.3 us -> 0.84 us
  local copies, waits for them, and re-layouts: 8.71 us -> 2.56 us
    ppermute x48 -> x37, starting transfers between devices: 65.9 us -> 47.3 us  [the longest x36 47.2 us: exchange(): return lax.ppermute(value, 'seq', [(s, s ^ distance) for s in range(n)])]
    psum x1 -> x0, waiting for transfers between devices: 17.2 us -> none  [per_device(): stats = lax.psum(sum((a[2] for a in attended)), 'head')]
    unnamed x42 -> x14, local copies, waits for them, and re-layouts: 8.71 us -> 2.56 us
    ppermute x48 -> x37, waiting for transfers between devices: 54.4 us -> 57.7 us  [the longest x36 56.3 us: exchange(): return lax.ppermute(value, 'seq', [(s, s ^ distance) for s in range(n)])]
    pallas_call x21 -> x26, Pallas kernels: 20.8 us -> 20.8 us  [__call__(): pl.pallas_call(kernel, out_shape=outs, in_specs=specs, out_specs=[pl.Bloc...]
  transfers between devices with their start and end apart: 49 -> 37, of which waited for: 22 -> 24; matrix products, arithmetic and copies ran while one was open for 0% -> 0% of each run, Pallas kernels for 9% -> 13%
where the time goes in v2:
time: 129 us
  waiting for transfers between devices  57.7 us (45%)
  starting transfers between devices  47.3 us (37%)
  Pallas kernels  20.8 us (16%)
  local copies, waits for them, and re-layouts  2.56 us (2%)
    ppermute x36, waiting for transfers between devices, exchange(): return lax.ppermute(value, 'seq', [(s, s ^ distance) for s in range(n)])  56.3 us
    ppermute x36, starting transfers between devices, exchange(): return lax.ppermute(value, 'seq', [(s, s ^ distance) for s in range(n)])  47.2 us
    pallas_call x26, Pallas kernels, __call__(): pl.pallas_call(kernel, out_shape=outs, in_specs=specs, out_specs=[pl.Bloc...  20.8 us
  transfers between devices with their start and end apart: 37, of which 24 were waited for; matrix products, arithmetic and copies ran while one was open for 0% of the time, Pallas kernels for 13%

profile of v2, /device:TPU:0, one launch (start us, length us, event | category | flops | bytes accessed | tf_op | source)
XLA Modules:
  0.0 129.1 jit_solution(3094942660540868116)
XLA Ops:
  3.6 4.0 %collective-permute-start.2 = (f32[512,128]{1,0:T(8,128)S(1)}, f32[512,128]{1,0:T(8,128)S(1)}, u32[]{:S(2)}, u32[]{:S(2)}) collective-permute-start(f32[512,128]{1,0:T(8,128)S(1)} %get-tuple-element.68.refs_2_), channel_id=1, source_target_pairs={{0,6},{2,4},{4,2},{6,0},{8,14},{10,12},{12,10},{14,8},{16,22},{18,... | collective-permute-start | bytes 786440 | tf_op jit(solution)/shard_map/prefix/ppermute | solution.py:80
  8.7 2.9 %collective-permute-start.7 = (f32[512,128]{1,0:T(8,128)S(1)}, f32[512,128]{1,0:T(8,128)S(1)}, u32[]{:S(2)}, u32[]{:S(2)}) collective-permute-start(f32[512,128]{1,0:T(8,128)S(1)} %get-tuple-element.69.refs_3_), channel_id=1, source_target_pairs={{0,6},{2,4},{4,2},{6,0},{8,14},{10,12},{12,10},{14,8},{16,22},{18,... | collective-permute-start | bytes 786440 | tf_op jit(solution)/shard_map/prefix/ppermute | solution.py:80
  12.2 5.1 %local.1 = (bf16[128,4096]{1,0:T(8,128)(2,1)S(1)}, f32[128,4096]{1,0:T(8,128)S(1)}) custom-call(bf16[128,4096]{1,0:T(8,128)(2,1)S(1)} %copy-done, bf16[128,4096]{1,0:T(8,128)(2,1)S(1)} %copy-done.1, bf16[128,4096]{1,0:T(8,128)(2,1)S(1)} %copy-done.3, f32[512,128]{1,0:T(8,128)S(1)} %get-tuple-element.69.refs_3_), custom_call_target="tpu_custom_call" | custom-call | flops 1 | bytes 1 | tf_op jit(solution)/shard_map/local/pallas_call | solution.py:39
  17.4 3.5 %collective-permute-done.refs_1_.refs_3_ = f32[512,128]{1,0:T(8,128)S(1)} collective-permute-done((f32[512,128]{1,0:T(8,128)S(1)}, f32[512,128]{1,0:T(8,128)S(1)}, u32[]{:S(2)}, u32[]{:S(2)}) %collective-permute-start) | collective-permute-done | bytes 262176 | tf_op jit(solution)/shard_map/prefix/ppermute | solution.py:80
  22.7 3.4 %collective-permute-done.3.refs_1_.refs_2_ = f32[256,128]{1,0:T(8,128)S(1)} collective-permute-done((f32[256,128]{1,0:T(8,128)S(1)}, f32[256,128]{1,0:T(8,128)S(1)}, u32[]{:S(2)}, u32[]{:S(2)}) %collective-permute-start.3) | collective-permute-done | bytes 131104 | tf_op jit(solution)/shard_map/prefix/ppermute | solution.py:80
  26.1 2.8 %collective-permute-start.4 = (f32[256,128]{1,0:T(8,128)S(1)}, f32[256,128]{1,0:T(8,128)S(1)}, u32[]{:S(2)}, u32[]{:S(2)}) collective-permute-start(f32[256,128]{1,0:T(8,128)S(1)} %prefix.9.refs_4_), channel_id=1, source_target_pairs={{0,16},{2,18},{4,20},{6,22},{8,24},{10,26},{12,28},{14,30},{16,0},... | collective-permute-start | bytes 393224 | tf_op jit(solution)/shard_map/prefix/ppermute | solution.py:80
  28.9 2.2 %collective-permute-done.5.refs_1_.refs_3_ = f32[512,128]{1,0:T(8,128)S(1)} collective-permute-done((f32[512,128]{1,0:T(8,128)S(1)}, f32[512,128]{1,0:T(8,128)S(1)}, u32[]{:S(2)}, u32[]{:S(2)}) %collective-permute-start.5) | collective-permute-done | bytes 262176 | tf_op jit(solution)/shard_map/prefix/ppermute | solution.py:80
  35.1 2.5 %collective-permute-done.9.refs_1_.refs_2_ = f32[256,128]{1,0:T(8,128)S(1)} collective-permute-done((f32[256,128]{1,0:T(8,128)S(1)}, f32[256,128]{1,0:T(8,128)S(1)}, u32[]{:S(2)}, u32[]{:S(2)}) %collective-permute-start.9) | collective-permute-done | bytes 131104 | tf_op jit(solution)/shard_map/prefix/ppermute | solution.py:80
  37.6 1.9 %collective-permute-start.13 = (f32[256,128]{1,0:T(8,128)S(1)}, f32[256,128]{1,0:T(8,128)S(1)}, u32[]{:S(2)}, u32[]{:S(2)}) collective-permute-start(f32[256,128]{1,0:T(8,128)S(1)} %prefix.12.refs_6_), channel_id=1, source_target_pairs={{0,16},{2,18},{4,20},{6,22},{8,24},{10,26},{12,28},{14,30},{16,0},... | collective-permute-start | bytes 393224 | tf_op jit(solution)/shard_map/prefix/ppermute | solution.py:80
  43.8 2.1 %collective-permute-done.13.refs_0_ = f32[256,128]{1,0:T(8,128)S(1)} collective-permute-done((f32[256,128]{1,0:T(8,128)S(1)}, f32[256,128]{1,0:T(8,128)S(1)}, u32[]{:S(2)}, u32[]{:S(2)}) %collective-permute-start.13) | collective-permute-done | bytes 131104 | tf_op jit(solution)/shard_map/prefix/ppermute | solution.py:80
  46.0 5.0 %collective-permute-done.14.refs_1_ = f32[256,128]{1,0:T(8,128)S(1)} collective-permute-done((f32[256,128]{1,0:T(8,128)S(1)}, f32[256,128]{1,0:T(8,128)S(1)}, u32[]{:S(2)}, u32[]{:S(2)}) %collective-permute-start.14) | collective-permute-done | bytes 131104 | tf_op jit(solution)/shard_map/prefix/ppermute | solution.py:80
  55.6 5.0 %collective-permute-done.15.refs_5_ = f32[512,128]{1,0:T(8,128)S(1)} collective-permute-done((f32[512,128]{1,0:T(8,128)S(1)}, f32[512,128]{1,0:T(8,128)S(1)}, u32[]{:S(2)}, u32[]{:S(2)}) %collective-permute-start.15) | collective-permute-done | bytes 262176 | tf_op jit(solution)/shard_map/prefix/ppermute | solution.py:80
  60.6 5.1 %collective-permute-done.16.refs_6_ = f32[512,128]{1,0:T(8,128)S(1)} collective-permute-done((f32[512,128]{1,0:T(8,128)S(1)}, f32[512,128]{1,0:T(8,128)S(1)}, u32[]{:S(2)}, u32[]{:S(2)}) %collective-permute-start.16) | collective-permute-done | bytes 262176 | tf_op jit(solution)/shard_map/prefix/ppermute | solution.py:80
  74.9 7.8 %local_grad.1 = (bf16[128,4096]{1,0:T(8,128)(2,1)}, f32[128,4096]{1,0:T(8,128)S(1)}, f32[128,4096]{1,0:T(8,128)S(1)}) custom-call(bf16[128,4096]{1,0:T(8,128)(2,1)S(1)} %copy-done, bf16[128,4096]{1,0:T(8,128)(2,1)S(1)} %copy-done.2, bf16[128,4096]{1,0:T(8,128)(2,1)S(1)} %copy-done.4, bf16[128,4096]{1,0:T(8,128)(2,1)S(1)} %get-tuple-element.70.refs_3_, ...), custom_call_target="tpu_custom_call" | custom-call | flops 1 | bytes 1 | tf_op jit(solution)/shard_map/local_grad/pallas_call | solution.py:39
  84.7 1.7 %collective-permute-start.25 = (f32[256,128]{1,0:T(8,128)S(1)}, f32[256,128]{1,0:T(8,128)S(1)}, u32[]{:S(2)}, u32[]{:S(2)}) collective-permute-start(f32[256,128]{1,0:T(8,128)S(1)} %get-tuple-element.114.refs_2_), channel_id=1, source_target_pairs={{0,8},{2,10},{4,12},{6,14},{8,0},{10,2},{12,4},{14,6},{16,24},{18,... | collective-permute-start | bytes 393224 | tf_op jit(solution)/shard_map/suffix/ppermute | solution.py:80
  86.4 3.3 %collective-permute-done.25.refs_1_.refs_2_ = f32[256,128]{1,0:T(8,128)S(1)} collective-permute-done((f32[256,128]{1,0:T(8,128)S(1)}, f32[256,128]{1,0:T(8,128)S(1)}, u32[]{:S(2)}, u32[]{:S(2)}) %collective-permute-start.25) | collective-permute-done | bytes 131104 | tf_op jit(solution)/shard_map/suffix/ppermute | solution.py:80
  89.7 2.1 %collective-permute-start.27 = (f32[256,128]{1,0:T(8,128)S(1)}, f32[256,128]{1,0:T(8,128)S(1)}, u32[]{:S(2)}, u32[]{:S(2)}) collective-permute-start(f32[256,128]{1,0:T(8,128)S(1)} %suffix.9.refs_4_), channel_id=1, source_target_pairs={{0,16},{2,18},{4,20},{6,22},{8,24},{10,26},{12,28},{14,30},{16,0},... | collective-permute-start | bytes 393224 | tf_op jit(solution)/shard_map/suffix/ppermute | solution.py:80
  94.8 1.9 %collective-permute-start.26 = (f32[256,128]{1,0:T(8,128)S(1)}, f32[256,128]{1,0:T(8,128)S(1)}, u32[]{:S(2)}, u32[]{:S(2)}) collective-permute-start(f32[256,128]{1,0:T(8,128)S(1)} %get-tuple-element.116.refs_3_), channel_id=1, source_target_pairs={{0,8},{2,10},{4,12},{6,14},{8,0},{10,2},{12,4},{14,6},{16,24},{18,... | collective-permute-start | bytes 393224 | tf_op jit(solution)/shard_map/suffix/ppermute | solution.py:80
  97.5 3.8 %collective-permute-done.26.refs_1_.refs_2_ = f32[256,128]{1,0:T(8,128)S(1)} collective-permute-done((f32[256,128]{1,0:T(8,128)S(1)}, f32[256,128]{1,0:T(8,128)S(1)}, u32[]{:S(2)}, u32[]{:S(2)}) %collective-permute-start.26) | collective-permute-done | bytes 131104 | tf_op jit(solution)/shard_map/suffix/ppermute | solution.py:80
  101.3 2.1 %collective-permute-start.28 = (f32[256,128]{1,0:T(8,128)S(1)}, f32[256,128]{1,0:T(8,128)S(1)}, u32[]{:S(2)}, u32[]{:S(2)}) collective-permute-start(f32[256,128]{1,0:T(8,128)S(1)} %suffix.12.refs_6_), channel_id=1, source_target_pairs={{0,16},{2,18},{4,20},{6,22},{8,24},{10,26},{12,28},{14,30},{16,0},... | collective-permute-start | bytes 393224 | tf_op jit(solution)/shard_map/suffix/ppermute | solution.py:80
  109.4 4.5 %collective-permute-done.30.refs_1_ = f32[256,128]{1,0:T(8,128)S(1)} collective-permute-done((f32[256,128]{1,0:T(8,128)S(1)}, f32[256,128]{1,0:T(8,128)S(1)}, u32[]{:S(2)}, u32[]{:S(2)}) %collective-permute-start.30) | collective-permute-done | bytes 131104 | tf_op jit(solution)/shard_map/suffix/ppermute | solution.py:80
  119.2 4.8 %collective-permute-done.31.refs_5_ = f32[512,128]{1,0:T(8,128)S(1)} collective-permute-done((f32[512,128]{1,0:T(8,128)S(1)}, f32[512,128]{1,0:T(8,128)S(1)}, u32[]{:S(2)}, u32[]{:S(2)}) %collective-permute-start.31) | collective-permute-done | bytes 262176 | tf_op jit(solution)/shard_map/suffix/ppermute | solution.py:80
  124.0 3.2 %collective-permute-done.32.refs_6_ = f32[512,128]{1,0:T(8,128)S(1)} collective-permute-done((f32[512,128]{1,0:T(8,128)S(1)}, f32[512,128]{1,0:T(8,128)S(1)}, u32[]{:S(2)}, u32[]{:S(2)}) %collective-permute-start.32) | collective-permute-done | bytes 262176 | tf_op jit(solution)/shard_map/suffix/ppermute | solution.py:80
  127.1 2.0 %finish.3 = (bf16[128,4096]{1,0:T(8,128)(2,1)}, bf16[128,4096]{1,0:T(8,128)(2,1)}) custom-call(bf16[128,4096]{1,0:T(8,128)(2,1)S(1)} %copy-done.2, bf16[128,4096]{1,0:T(8,128)(2,1)S(1)} %copy-done.4, f32[128,4096]{1,0:T(8,128)S(1)} %get-tuple-element.105.refs_2_, f32[128,4096]{1,0:T(8,128)S(1)} %get-tuple-element.106.refs_4_.refs_3_, ...), custom_call_target="tpu_custom_call" | custom-call | flops 1 | bytes 1 | tf_op jit(solution)/shard_map/finish/pallas_call | solution.py:39
  (90 shorter events, 45.7 us)
Async XLA Ops:
  3.6 13.6 %collective-permute-start.2 = (f32[512,128]{1,0:T(8,128)S(1)}, f32[512,128]{1,0:T(8,128)S(1)}, u32[]{:S(2)}, u32[]{:S(2)}) collective-permute-start(f32[512,128]{1,0:T(8,128)S(1)} %get-tuple-element.68.refs_2_), channel_id=1, source_target_pairs={{0,6},{2,4},{4,2},{6,0},{8,14},{10,12},{12,10},{14,8},{16,22},{18,... | collective-permute-start | bytes 786440 | tf_op jit(solution)/shard_map/prefix/ppermute | solution.py:80
  7.6 13.4 %collective-permute-start = (f32[512,128]{1,0:T(8,128)S(1)}, f32[512,128]{1,0:T(8,128)S(1)}, u32[]{:S(2)}, u32[]{:S(2)}) collective-permute-start(f32[512,128]{1,0:T(8,128)S(1)} %get-tuple-element.73), channel_id=1, source_target_pairs={{0,2},{2,0},{4,6},{6,4},{8,10},{10,8},{12,14},{14,12},{16,18},{18,... | collective-permute-start | bytes 786440 | tf_op jit(solution)/shard_map/prefix/ppermute | solution.py:80
  8.1 12.8 %collective-permute-start.1 = (f32[512,128]{1,0:T(8,128)S(1)}, f32[512,128]{1,0:T(8,128)S(1)}, u32[]{:S(2)}, u32[]{:S(2)}) collective-permute-start(f32[512,128]{1,0:T(8,128)S(1)} %get-tuple-element.74), channel_id=1, source_target_pairs={{0,4},{2,6},{4,0},{6,2},{8,12},{10,14},{12,8},{14,10},{16,20},{18,... | collective-permute-start | bytes 786440 | tf_op jit(solution)/shard_map/prefix/ppermute | solution.py:80
  8.7 20.2 %collective-permute-start.7 = (f32[512,128]{1,0:T(8,128)S(1)}, f32[512,128]{1,0:T(8,128)S(1)}, u32[]{:S(2)}, u32[]{:S(2)}) collective-permute-start(f32[512,128]{1,0:T(8,128)S(1)} %get-tuple-element.69.refs_3_), channel_id=1, source_target_pairs={{0,6},{2,4},{4,2},{6,0},{8,14},{10,12},{12,10},{14,8},{16,22},{18,... | collective-permute-start | bytes 786440 | tf_op jit(solution)/shard_map/prefix/ppermute | solution.py:80
  11.6 19.5 %collective-permute-start.5 = (f32[512,128]{1,0:T(8,128)S(1)}, f32[512,128]{1,0:T(8,128)S(1)}, u32[]{:S(2)}, u32[]{:S(2)}) collective-permute-start(f32[512,128]{1,0:T(8,128)S(1)} %get-tuple-element.78), channel_id=1, source_target_pairs={{0,2},{2,0},{4,6},{6,4},{8,10},{10,8},{12,14},{14,12},{16,18},{18,... | collective-permute-start | bytes 786440 | tf_op jit(solution)/shard_map/prefix/ppermute | solution.py:80
  17.3 13.8 %collective-permute-start.6 = (f32[512,128]{1,0:T(8,128)S(1)}, f32[512,128]{1,0:T(8,128)S(1)}, u32[]{:S(2)}, u32[]{:S(2)}) collective-permute-start(f32[512,128]{1,0:T(8,128)S(1)} %get-tuple-element.79), channel_id=1, source_target_pairs={{0,4},{2,6},{4,0},{6,2},{8,12},{10,14},{12,8},{14,10},{16,20},{18,... | collective-permute-start | bytes 786440 | tf_op jit(solution)/shard_map/prefix/ppermute | solution.py:80
  40.2 14.4 %collective-permute-start.10 = (f32[512,128]{1,0:T(8,128)S(1)}, f32[512,128]{1,0:T(8,128)S(1)}, u32[]{:S(2)}, u32[]{:S(2)}) collective-permute-start(f32[512,128]{1,0:T(8,128)S(1)} %get-tuple-element.85), channel_id=1, source_target_pairs={{0,2},{2,0},{4,6},{6,4},{8,10},{10,8},{12,14},{14,12},{16,18},{18,... | collective-permute-start | bytes 786440 | tf_op jit(solution)/shard_map/prefix/ppermute | solution.py:80
  41.8 13.0 %collective-permute-start.11 = (f32[512,128]{1,0:T(8,128)S(1)}, f32[512,128]{1,0:T(8,128)S(1)}, u32[]{:S(2)}, u32[]{:S(2)}) collective-permute-start(f32[512,128]{1,0:T(8,128)S(1)} %get-tuple-element.86), channel_id=1, source_target_pairs={{0,4},{2,6},{4,0},{6,2},{8,12},{10,14},{12,8},{14,10},{16,20},{18,... | collective-permute-start | bytes 786440 | tf_op jit(solution)/shard_map/prefix/ppermute | solution.py:80
  43.4 11.6 %collective-permute-start.12 = (f32[512,128]{1,0:T(8,128)S(1)}, f32[512,128]{1,0:T(8,128)S(1)}, u32[]{:S(2)}, u32[]{:S(2)}) collective-permute-start(f32[512,128]{1,0:T(8,128)S(1)} %get-tuple-element.87.refs_3_), channel_id=1, source_target_pairs={{0,6},{2,4},{4,2},{6,0},{8,14},{10,12},{12,10},{14,8},{16,22},{18,... | collective-permute-start | bytes 786440 | tf_op jit(solution)/shard_map/prefix/ppermute | solution.py:80
  51.3 9.3 %collective-permute-start.15 = (f32[512,128]{1,0:T(8,128)S(1)}, f32[512,128]{1,0:T(8,128)S(1)}, u32[]{:S(2)}, u32[]{:S(2)}) collective-permute-start(f32[512,128]{1,0:T(8,128)S(1)} %get-tuple-element.93), channel_id=1, source_target_pairs={{0,2},{2,0},{4,6},{6,4},{8,10},{10,8},{12,14},{14,12},{16,18},{18,... | collective-permute-start | bytes 786440 | tf_op jit(solution)/shard_map/prefix/ppermute | solution.py:80
  53.0 12.8 %collective-permute-start.16 = (f32[512,128]{1,0:T(8,128)S(1)}, f32[512,128]{1,0:T(8,128)S(1)}, u32[]{:S(2)}, u32[]{:S(2)}) collective-permute-start(f32[512,128]{1,0:T(8,128)S(1)} %get-tuple-element.94), channel_id=1, source_target_pairs={{0,4},{2,6},{4,0},{6,2},{8,12},{10,14},{12,8},{14,10},{16,20},{18,... | collective-permute-start | bytes 786440 | tf_op jit(solution)/shard_map/prefix/ppermute | solution.py:80
  54.6 11.1 %collective-permute-start.17 = (f32[512,128]{1,0:T(8,128)S(1)}, f32[512,128]{1,0:T(8,128)S(1)}, u32[]{:S(2)}, u32[]{:S(2)}) collective-permute-start(f32[512,128]{1,0:T(8,128)S(1)} %get-tuple-element.90.refs_8_), channel_id=1, source_target_pairs={{0,6},{2,4},{4,2},{6,0},{8,14},{10,12},{12,10},{14,8},{16,22},{18,... | collective-permute-start | bytes 786440 | tf_op jit(solution)/shard_map/prefix/ppermute | solution.py:80
  68.5 14.2 %collective-permute-start.22 = (f32[512,128]{1,0:T(8,128)S(1)}, f32[512,128]{1,0:T(8,128)S(1)}, u32[]{:S(2)}, u32[]{:S(2)}) collective-permute-start(f32[512,128]{1,0:T(8,128)S(1)} %get-tuple-element.111), channel_id=1, source_target_pairs={{0,2},{2,0},{4,6},{6,4},{8,10},{10,8},{12,14},{14,12},{16,18},{18,... | collective-permute-start | bytes 786440 | tf_op jit(solution)/shard_map/suffix/ppermute | solution.py:80
  69.8 14.8 %collective-permute-start.23 = (f32[512,128]{1,0:T(8,128)S(1)}, f32[512,128]{1,0:T(8,128)S(1)}, u32[]{:S(2)}, u32[]{:S(2)}) collective-permute-start(f32[512,128]{1,0:T(8,128)S(1)} %get-tuple-element.112), channel_id=1, source_target_pairs={{0,4},{2,6},{4,0},{6,2},{8,12},{10,14},{12,8},{14,10},{16,20},{18,... | collective-permute-start | bytes 786440 | tf_op jit(solution)/shard_map/suffix/ppermute | solution.py:80
  70.6 14.0 %collective-permute-start.24 = (f32[512,128]{1,0:T(8,128)S(1)}, f32[512,128]{1,0:T(8,128)S(1)}, u32[]{:S(2)}, u32[]{:S(2)}) collective-permute-start(f32[512,128]{1,0:T(8,128)S(1)} %get-tuple-element.99.refs_6_), channel_id=1, source_target_pairs={{0,6},{2,4},{4,2},{6,0},{8,14},{10,12},{12,10},{14,8},{16,22},{18,... | collective-permute-start | bytes 786440 | tf_op jit(solution)/shard_map/suffix/ppermute | solution.py:80
  72.8 19.1 %collective-permute-start.19 = (f32[512,128]{1,0:T(8,128)S(1)}, f32[512,128]{1,0:T(8,128)S(1)}, u32[]{:S(2)}, u32[]{:S(2)}) collective-permute-start(f32[512,128]{1,0:T(8,128)S(1)} %get-tuple-element.108), channel_id=1, source_target_pairs={{0,2},{2,0},{4,6},{6,4},{8,10},{10,8},{12,14},{14,12},{16,18},{18,... | collective-permute-start | bytes 786440 | tf_op jit(solution)/shard_map/suffix/ppermute | solution.py:80
  74.1 19.1 %collective-permute-start.20 = (f32[512,128]{1,0:T(8,128)S(1)}, f32[512,128]{1,0:T(8,128)S(1)}, u32[]{:S(2)}, u32[]{:S(2)}) collective-permute-start(f32[512,128]{1,0:T(8,128)S(1)} %get-tuple-element.109), channel_id=1, source_target_pairs={{0,4},{2,6},{4,0},{6,2},{8,12},{10,14},{12,8},{14,10},{16,20},{18,... | collective-permute-start | bytes 786440 | tf_op jit(solution)/shard_map/suffix/ppermute | solution.py:80
  82.7 12.1 %collective-permute-start.21 = (f32[512,128]{1,0:T(8,128)S(1)}, f32[512,128]{1,0:T(8,128)S(1)}, u32[]{:S(2)}, u32[]{:S(2)}) collective-permute-start(f32[512,128]{1,0:T(8,128)S(1)} %get-tuple-element.103.refs_8_), channel_id=1, source_target_pairs={{0,6},{2,4},{4,2},{6,0},{8,14},{10,12},{12,10},{14,8},{16,22},{18,... | collective-permute-start | bytes 786440 | tf_op jit(solution)/shard_map/suffix/ppermute | solution.py:80
  104.4 11.7 %collective-permute-start.34 = (f32[512,128]{1,0:T(8,128)S(1)}, f32[512,128]{1,0:T(8,128)S(1)}, u32[]{:S(2)}, u32[]{:S(2)}) collective-permute-start(f32[512,128]{1,0:T(8,128)S(1)} %get-tuple-element.127), channel_id=1, source_target_pairs={{0,2},{2,0},{4,6},{6,4},{8,10},{10,8},{12,14},{14,12},{16,18},{18,... | collective-permute-start | bytes 786440 | tf_op jit(solution)/shard_map/suffix/ppermute | solution.py:80
  105.2 12.5 %collective-permute-start.35 = (f32[512,128]{1,0:T(8,128)S(1)}, f32[512,128]{1,0:T(8,128)S(1)}, u32[]{:S(2)}, u32[]{:S(2)}) collective-permute-start(f32[512,128]{1,0:T(8,128)S(1)} %get-tuple-element.128), channel_id=1, source_target_pairs={{0,4},{2,6},{4,0},{6,2},{8,12},{10,14},{12,8},{14,10},{16,20},{18,... | collective-permute-start | bytes 786440 | tf_op jit(solution)/shard_map/suffix/ppermute | solution.py:80
  106.4 12.1 %collective-permute-start.36 = (f32[512,128]{1,0:T(8,128)S(1)}, f32[512,128]{1,0:T(8,128)S(1)}, u32[]{:S(2)}, u32[]{:S(2)}) collective-permute-start(f32[512,128]{1,0:T(8,128)S(1)} %get-tuple-element.119.refs_3_), channel_id=1, source_target_pairs={{0,6},{2,4},{4,2},{6,0},{8,14},{10,12},{12,10},{14,8},{16,22},{18,... | collective-permute-start | bytes 786440 | tf_op jit(solution)/shard_map/suffix/ppermute | solution.py:80
  114.2 9.8 %collective-permute-start.31 = (f32[512,128]{1,0:T(8,128)S(1)}, f32[512,128]{1,0:T(8,128)S(1)}, u32[]{:S(2)}, u32[]{:S(2)}) collective-permute-start(f32[512,128]{1,0:T(8,128)S(1)} %get-tuple-element.123), channel_id=1, source_target_pairs={{0,2},{2,0},{4,6},{6,4},{8,10},{10,8},{12,14},{14,12},{16,18},{18,... | collective-permute-start | bytes 786440 | tf_op jit(solution)/shard_map/suffix/ppermute | solution.py:80
  115.0 12.1 %collective-permute-start.32 = (f32[512,128]{1,0:T(8,128)S(1)}, f32[512,128]{1,0:T(8,128)S(1)}, u32[]{:S(2)}, u32[]{:S(2)}) collective-permute-start(f32[512,128]{1,0:T(8,128)S(1)} %get-tuple-element.124), channel_id=1, source_target_pairs={{0,4},{2,6},{4,0},{6,2},{8,12},{10,14},{12,8},{14,10},{16,20},{18,... | collective-permute-start | bytes 786440 | tf_op jit(solution)/shard_map/suffix/ppermute | solution.py:80
  116.1 11.0 %collective-permute-start.33 = (f32[512,128]{1,0:T(8,128)S(1)}, f32[512,128]{1,0:T(8,128)S(1)}, u32[]{:S(2)}, u32[]{:S(2)}) collective-permute-start(f32[512,128]{1,0:T(8,128)S(1)} %get-tuple-element.125.refs_8_), channel_id=1, source_target_pairs={{0,6},{2,4},{4,2},{6,0},{8,14},{10,12},{12,10},{14,8},{16,22},{18,... | collective-permute-start | bytes 786440 | tf_op jit(solution)/shard_map/suffix/ppermute | solution.py:80
  (20 other events, 146.4 us)

commit v3 on v2

v3 whole, which is shorter than its diff:
```python
import functools

import jax
import jax.numpy as jnp
from jax import lax
from jax.experimental import pallas as pl
from jax.experimental.pallas import tpu as pltpu
from jax.sharding import PartitionSpec as P

HEAD_DIM = 128
GROUPS = 3
HIDDEN = 4 * 10**9
PLANE = 4

epsilon = 1e-05

CONTRACT_ROWS = (((0,), (0,)), ((), ()))
CONTRACT_COLUMNS = (((1,), (1,)), ((), ()))


def dot(a, b, dims=(((1,), (0,)), ((), ()))):
    return lax.dot_general(a, b, dims, preferred_element_type=jnp.float32)


class Chain:
    def __init__(self):
        self.last = None

    def __call__(self, body, outs, *args, flops=1, hbm_args=(), hbm_outs=0, aliases=None, scratch=()):
        specs = [pl.BlockSpec(memory_space=pltpu.HBM if i in hbm_args else pltpu.VMEM) for i in range(len(args))]
        kernel, operands, count = body, args, len(args)
        if self.last is not None and not any(self.last is arg for arg in args):
            specs, operands = specs + [pl.BlockSpec(memory_space=pl.ANY)], (*args, self.last)

            def kernel(*refs):
                body(*refs[:count], *refs[count + 1 :])

        results = pl.pallas_call(
            kernel,
            out_shape=outs,
            in_specs=specs,
            out_specs=[
                pl.BlockSpec(memory_space=pltpu.HBM if i < hbm_outs else pltpu.VMEM) for i in range(len(outs))
            ],
            scratch_shapes=scratch,
            input_output_aliases=aliases or {},
            cost_estimate=pl.CostEstimate(flops=flops, bytes_accessed=1, transcendentals=0),
            compiler_params=pltpu.CompilerParams(vmem_limit_bytes=16 * 1024 * 1024),
        )(*operands)
        self.last = results[-1]
        return results


def f32(*shape):
    return jax.ShapeDtypeStruct(shape, jnp.float32)


def bf16(*shape):
    return jax.ShapeDtypeStruct(shape, jnp.bfloat16)


def place():
    me = lax.axis_index("seq")
    return lax.rem(me, PLANE), lax.div(me, PLANE)


def weight(condition):
    return jnp.where(condition, 1.0, 0.0).astype(jnp.float32)


def columns(head, count=1):
    return pl.ds(pl.multiple_of(head * HEAD_DIM, HEAD_DIM), count * HEAD_DIM)


def split_heads(heads):
    per_owner = heads // PLANE
    groups = min(GROUPS, per_owner)
    sizes = [per_owner // groups + (g < per_owner % groups) for g in range(groups)]
    return [(PLANE * sum(sizes[:g]), sizes[g]) for g in range(groups)]


def causal(tokens):
    rows_index = lax.broadcasted_iota(jnp.int32, (tokens, tokens), 0)
    cols_index = lax.broadcasted_iota(jnp.int32, (tokens, tokens), 1)
    return rows_index >= cols_index


def exchange(value, distance):
    n = lax.axis_size("seq")
    return lax.ppermute(value, "seq", [(s, s ^ distance) for s in range(n)])


def plane_send(parts):
    return [parts[0]] + [exchange(parts[k], k) for k in range(1, PLANE)]


def bit(level):
    _, z = place()
    return lax.rem(lax.div(z, 1 << level), 2)


def half(side, rows):
    return pl.ds(pl.multiple_of(side * rows, 8), rows)


def total_kernel(level, *refs):
    parts, outs = refs[:-2], refs[-2:]
    rows = outs[0].shape[0]
    side = bit(level)
    for out, at in zip(outs, (half(side, rows), half(1 - side, rows))):
        total = parts[0][at, :]
        for part in parts[1:]:
            total = total + part[at, :]
        out[...] = total


def sum_kernel(*refs):
    total = refs[0][...]
    for part in refs[1:-1]:
        total = total + part[...]
    refs[-1][...] = total


def first(level, reverse):
    later = bit(level).astype(jnp.float32)
    return (1.0 - later, later) if reverse else (later, 1.0 - later)


def edge_kernel(level, reverse, other, mine, theirs, to_me, to_partner):
    entering = other[...] * first(level + 1, reverse)[0]
    before_me, before_partner = first(level, reverse)
    to_me[...] = entering + theirs[...] * before_me
    to_partner[...] = entering + mine[...] * before_partner


def inner_kernel(level, reverse, kept, received, mine, theirs, to_me, to_partner):
    rows = kept.shape[0]
    side = bit(level + 1)
    before_me, before_partner = first(level, reverse)
    for entering, at in ((kept, half(side, rows)), (received, half(1 - side, rows))):
        to_me[at, :] = entering[...] + theirs[at, :] * before_me
        to_partner[at, :] = entering[...] + mine[at, :] * before_partner


def spread_kernel(reverse, kept, received, *refs):
    parts, outs = refs[:PLANE], refs[PLANE:]
    p, _ = place()
    rows = kept.shape[0]
    side = bit(0)
    for base, at in ((kept, half(side, rows)), (received, half(1 - side, rows))):
        held = [part[at, :] for part in parts]
        for k in range(PLANE):
            target = p ^ k
            total = base[...]
            for j in range(PLANE):
                source = p ^ j
                before = source > target if reverse else source < target
                total = total + held[j] * weight(before)
            outs[k][at, :] = total


def line_steps(run, parts, reverse, level=0):
    levels = (lax.axis_size("seq") // PLANE).bit_length() - 1
    distance = PLANE << level
    rows = parts[0].shape[0] // 2
    mine, send = run(functools.partial(total_kernel, level), [f32(rows, HEAD_DIM)] * 2, *parts)
    theirs = exchange(send, distance)
    yield
    if level == levels - 2:
        (total,) = run(sum_kernel, [f32(rows, HEAD_DIM)], mine, theirs)
        entering = (exchange(total, 2 * distance),)
        body = edge_kernel
        yield
    else:
        entering = yield from line_steps(run, (mine, theirs), reverse, level + 1)
        body = inner_kernel
    kept, send = run(
        functools.partial(body, level, reverse), [f32(rows, HEAD_DIM)] * 2, *entering, mine, theirs
    )
    received = exchange(send, distance)
    yield
    return kept, received


def scan_steps(run, parts, reverse, results):
    parts = plane_send(parts)
    yield
    kept, received = yield from line_steps(run, parts, reverse)
    rows = parts[0].shape[0]
    outs = run(
        functools.partial(spread_kernel, reverse), [f32(rows, HEAD_DIM)] * PLANE, kept, received, *parts
    )
    results.append(plane_send(outs))


def scan_states(run, groups, reverse, fillers, use):
    results = []
    steps = [scan_steps(run, parts, reverse, results) for parts in groups]
    count = 2 * ((lax.axis_size("seq") // PLANE).bit_length() - 1)
    events = [(-1.0 if g == 0 else 1.0 + g / 10, filler) for g, filler in enumerate(fillers)]
    for g, one in enumerate(steps):
        next(one)
        behind = 0.5 + 1.2 * g if g else 0.0
        events += [(behind + step, functools.partial(next, one, None)) for step in range(count)]
        events.append((behind + count + 1, lambda g=g: use(g, results[g])))
    for _, event in sorted(events, key=lambda e: e[0]):
        event()


def state_of(first, count, p, left, right, outs):
    for k in range(PLANE):
        for j in range(count):
            at = columns(first + (p ^ k) * count + j)
            outs[k][pl.ds(j * HEAD_DIM, HEAD_DIM), :] = dot(left[:, at], right[:, at], CONTRACT_ROWS)


def first_state_kernel(first, count, keys, values, *refs):
    outs, (left, right, sems) = refs[:PLANE], refs[PLANE:]
    here = pl.ds(first * HEAD_DIM, PLANE * count * HEAD_DIM)
    copies = [
        pltpu.make_async_copy(source.at[:, here], target, sems.at[i])
        for i, (source, target) in enumerate(((keys, left), (values, right)))
    ]
    for copy in copies:
        copy.start()
    for copy in copies:
        copy.wait()
    state_of(0, count, place()[0], left, right, outs)


def state_kernel(first, count, keys, values, *outs):
    state_of(first, count, place()[0], keys, values, outs)


def local_kernel(first, scale, queries, keys, values, weights, inner):
    mask = causal(queries.shape[0])
    for h in range(inner.shape[1] // HEAD_DIM):
        at, here = columns(first + h), columns(h)
        scores = dot(queries[:, at], keys[:, at], CONTRACT_COLUMNS) * scale
        w = jnp.where(mask, scores, 0.0).astype(jnp.bfloat16)
        weights[:, here] = w
        inner[:, here] = dot(w, values[:, at])


def attend_kernel(first, count, scale, queries, inner, cotangent, gain, *refs):
    parts, (attended, prefix_low, stats) = refs[:PLANE], refs[-3:]
    earlier = refs[PLANE:-3]
    p, _ = place()
    squares, cross = (earlier[0][0], earlier[0][1]) if earlier else (0.0, 0.0)
    for k in range(PLANE):
        for j in range(count):
            h = (p ^ k) * count + j
            at, here = columns(first + h), columns(h)
            low = parts[k][pl.ds(j * HEAD_DIM, HEAD_DIM), :].astype(jnp.bfloat16)
            prefix_low[:, here] = low
            a = inner[:, here] + scale * dot(queries[:, at], low)
            attended[:, here] = a
            scaled = cotangent[:, at].astype(jnp.float32) * gain[:, at]
            squares = squares + a * a
            cross = cross + scaled * a
    stats[0] = squares
    stats[1] = cross


def grad_kernel(first, count, width, queries, cotangent, gain, attended, *refs):
    p, _ = place()
    stats, (grad, *outs) = refs[: -PLANE - 1], refs[-PLANE - 1 :]
    squares, cross = stats[0][0], stats[0][1]
    for other in stats[1:]:
        squares, cross = squares + other[0], cross + other[1]
    inverse_rms = lax.rsqrt(jnp.sum(squares, axis=1, keepdims=True) / width + epsilon)
    cross = jnp.sum(cross, axis=1, keepdims=True) * inverse_rms / width
    for k in range(PLANE):
        for j in range(count):
            h = (p ^ k) * count + j
            at, here = columns(first + h), columns(h)
            normed = attended[:, here] * inverse_rms
            scaled = cotangent[:, at].astype(jnp.float32) * gain[:, at]
            g = ((scaled - normed * cross) * inverse_rms).astype(jnp.bfloat16)
            grad[:, here] = g
            outs[k][pl.ds(j * HEAD_DIM, HEAD_DIM), :] = dot(queries[:, at], g, CONTRACT_ROWS)


def local_grad_kernel(first, scale, queries, keys, values, weights, grad, prefix_low, *refs):
    query_grad, key_inner, value_inner, query_block, sem = refs[-5:]
    mask = causal(queries.shape[0])
    heads = grad.shape[1] // HEAD_DIM
    for h in range(heads):
        at, here = columns(first + h), columns(h)
        g = grad[:, here]
        scores = dot(g, values[:, at], CONTRACT_COLUMNS) * scale
        gw = jnp.where(mask, scores, 0.0).astype(jnp.bfloat16)
        query = dot(gw, keys[:, at]) + scale * dot(g, prefix_low[:, here], CONTRACT_COLUMNS)
        query_block[:, here] = query.astype(jnp.bfloat16)
        key_inner[:, here] = dot(gw, queries[:, at], CONTRACT_ROWS)
        value_inner[:, here] = dot(weights[:, here], g, CONTRACT_ROWS)
    copy = pltpu.make_async_copy(query_block, query_grad.at[:, pl.ds(first * HEAD_DIM, heads * HEAD_DIM)], sem.at[0])
    copy.start()
    copy.wait()


def finish_kernel(first, count, scale, keys, values, key_inner, value_inner, *refs):
    parts, (key_grad, value_grad, key_block, value_block, sems) = refs[:PLANE], refs[-5:]
    p, _ = place()
    copies = []
    for k in range(PLANE):
        owner = (p ^ k) * count
        for j in range(count):
            at, here = columns(first + owner + j), columns(owner + j)
            low = parts[k][pl.ds(j * HEAD_DIM, HEAD_DIM), :].astype(jnp.bfloat16)
            key = key_inner[:, here] + scale * dot(values[:, at], low, CONTRACT_COLUMNS)
            key_block[:, here] = key.astype(jnp.bfloat16)
            value = value_inner[:, here] + scale * dot(keys[:, at], low)
            value_block[:, here] = value.astype(jnp.bfloat16)
        for i, (block, result) in enumerate(((key_block, key_grad), (value_block, value_grad))):
            copies.append(
                pltpu.make_async_copy(
                    block.at[:, columns(owner, count)],
                    result.at[:, columns(first + owner, count)],
                    sems.at[2 * k + i],
                )
            )
            copies[-1].start()
    for copy in copies:
        copy.wait()


def per_device(queries, keys, values, cotangent, gain):
    tokens, width = queries.shape
    ways = lax.axis_size("head")
    scale = HEAD_DIM ** (-0.5)
    gain = gain[None, :]
    groups = split_heads(width // HEAD_DIM)
    shares = [PLANE * count * HEAD_DIM for _, count in groups]
    states_of = [[f32(count * HEAD_DIM, HEAD_DIM)] * PLANE for _, count in groups]
    final = len(groups) - 1
    run = Chain()

    def block(g):
        return pltpu.VMEM((tokens, shares[g]), jnp.bfloat16)

    with jax.named_scope("state"):
        states = []
        for g, (first, count) in enumerate(groups):
            states.append(
                run(
                    functools.partial(state_kernel if g else first_state_kernel, first, count),
                    states_of[g], keys, values,
                    hbm_args=() if g else (0, 1),
                    scratch=[] if g else [block(0), block(0), pltpu.SemaphoreType.DMA((2,))],
                )
            )

    local, attended, local_grads, ends = [], [], [], []

    def run_local(g):
        local.append(
            run(
                functools.partial(local_kernel, groups[g][0], scale),
                [bf16(tokens, shares[g]), f32(tokens, shares[g])],
                queries, keys, values,
            )
        )

    def attend(g, prefix):
        attended.append(
            run(
                functools.partial(attend_kernel, *groups[g], scale),
                [f32(tokens, shares[g]), bf16(HEAD_DIM, shares[g]), f32(2, tokens, HEAD_DIM)],
                queries, local[g][1], cotangent, gain, *prefix, *[a[2] for a in attended[-1:]],
                flops=1 if g == final else HIDDEN,
            )
        )

    with jax.named_scope("prefix"):
        scan_states(run, states, False, [functools.partial(run_local, g) for g in range(final + 1)], attend)
    with jax.named_scope("statistics"):
        stats = [attended[-1][2]]
        for k in range(1, ways):
            stats.append(lax.ppermute(stats[0], "head", [(h, (h + k) % ways) for h in range(ways)]))
    with jax.named_scope("grad"):
        grads = [
            run(
                functools.partial(grad_kernel, first, count, width * ways),
                [bf16(tokens, shares[g])] + states_of[g],
                queries, cotangent, gain, attended[g][0], *stats,
            )
            for g, (first, count) in enumerate(groups)
        ]

    def run_local_grad(g):
        earlier = [r[0] for r in local_grads[-1:]]
        local_grads.append(
            run(
                functools.partial(local_grad_kernel, groups[g][0], scale),
                [bf16(tokens, width), f32(tokens, shares[g]), f32(tokens, shares[g])],
                queries, keys, values, local[g][0], grads[g][0], attended[g][1], *earlier,
                hbm_args=(6,), hbm_outs=1, aliases={6: 0} if earlier else {},
                scratch=[block(g), pltpu.SemaphoreType.DMA((1,))],
            )
        )

    def finish(g, suffix):
        at = 4 + PLANE
        earlier = ends[-1] if ends else []
        ends.append(
            run(
                functools.partial(finish_kernel, *groups[g], scale),
                [bf16(tokens, width)] * 2,
                keys, values, local_grads[g][1], local_grads[g][2], *suffix, *earlier,
                flops=1 if g == final else HIDDEN,
                hbm_args=(at, at + 1), hbm_outs=2, aliases={at: 0, at + 1: 1} if earlier else {},
                scratch=[block(g), block(g), pltpu.SemaphoreType.DMA((2 * PLANE,))],
            )
        )

    with jax.named_scope("suffix"):
        scan_states(
            run, [g[1:] for g in grads], True, [functools.partial(run_local_grad, g) for g in range(final + 1)], finish
        )
    return local_grads[-1][0], *ends[-1]


def solution(mesh):
    return jax.shard_map(
        per_device,
        mesh=mesh,
        in_specs=(P("seq", "head"), P("seq", "head"), P("seq", "head"), P("seq", "head"), P("head")),
        out_specs=(P("seq", "head"), P("seq", "head"), P("seq", "head")),
        check_vma=False,
    )
```

time: 129 us -> 135 us (1.047)
  starting transfers between devices: 47.3 us -> 66.8 us
  waiting for transfers between devices: 57.7 us -> 38.7 us
  Pallas kernels: 20.8 us -> 24.1 us
    ppermute x36 -> x54, starting transfers between devices: 47.2 us -> 66.7 us  [exchange(): return lax.ppermute(value, 'seq', [(s, s ^ distance) for s in range(n)])]
    ppermute x36 -> x54, waiting for transfers between devices: 56.3 us -> 37.4 us  [exchange(): return lax.ppermute(value, 'seq', [(s, s ^ distance) for s in range(n)])]
    pallas_call x26 -> x42, Pallas kernels: 20.8 us -> 24.1 us  [__call__(): pl.pallas_call(kernel, out_shape=outs, in_specs=specs, out_specs=[pl.Bloc...]
    unnamed x14 -> x16, local copies, waits for them, and re-layouts: 2.56 us -> 3.69 us
  transfers between devices with their start and end apart: 37 -> 55, of which waited for: 24 -> 24; matrix products, arithmetic and copies ran while one was open for 0% -> 0% of each run, Pallas kernels for 13% -> 16%
where the time goes in v3:
time: 135 us; the launch traced here: 134 us
  starting transfers between devices  66.8 us (49%)
  waiting for transfers between devices  38.7 us (29%)
  Pallas kernels  24.1 us (18%)
  local copies, waits for them, and re-layouts  3.69 us (3%)
    ppermute x54, starting transfers between devices, exchange(): return lax.ppermute(value, 'seq', [(s, s ^ distance) for s in range(n)])  66.7 us
    ppermute x54, waiting for transfers between devices, exchange(): return lax.ppermute(value, 'seq', [(s, s ^ distance) for s in range(n)])  37.4 us
    pallas_call x42, Pallas kernels, __call__(): pl.pallas_call(kernel, out_shape=outs, in_specs=specs, out_specs=[pl.Bloc...  24.1 us
    unnamed x16, local copies, waits for them, and re-layouts  3.69 us
  transfers between devices with their start and end apart: 55, of which 24 were waited for; matrix products, arithmetic and copies ran while one was open for 0% of the time, Pallas kernels for 16%

profile of v3, /device:TPU:0, one launch (start us, length us, event | category | flops | bytes accessed | tf_op | source)
XLA Modules:
  0.0 134.4 jit_solution(7228824678888770224)
XLA Ops:
  3.5 4.0 %collective-permute-start.2 = (f32[384,128]{1,0:T(8,128)S(1)}, f32[384,128]{1,0:T(8,128)S(1)}, u32[]{:S(2)}, u32[]{:S(2)}) collective-permute-start(f32[384,128]{1,0:T(8,128)S(1)} %get-tuple-element.111.refs_2_), channel_id=1, source_target_pairs={{0,6},{2,4},{4,2},{6,0},{8,14},{10,12},{12,10},{14,8},{16,22},{18,... | collective-permute-start | bytes 589832 | tf_op jit(solution)/shard_map/prefix/ppermute | solution.py:90
  8.5 2.9 %collective-permute-start.9 = (f32[384,128]{1,0:T(8,128)S(1)}, f32[384,128]{1,0:T(8,128)S(1)}, u32[]{:S(2)}, u32[]{:S(2)}) collective-permute-start(f32[384,128]{1,0:T(8,128)S(1)} %get-tuple-element.112.refs_2_), channel_id=1, source_target_pairs={{0,6},{2,4},{4,2},{6,0},{8,14},{10,12},{12,10},{14,8},{16,22},{18,... | collective-permute-start | bytes 589832 | tf_op jit(solution)/shard_map/prefix/ppermute | solution.py:90
  13.2 2.1 %collective-permute-start.8 = (f32[384,128]{1,0:T(8,128)S(1)}, f32[384,128]{1,0:T(8,128)S(1)}, u32[]{:S(2)}, u32[]{:S(2)}) collective-permute-start(f32[384,128]{1,0:T(8,128)S(1)} %get-tuple-element.125), channel_id=1, source_target_pairs={{0,4},{2,6},{4,0},{6,2},{8,12},{10,14},{12,8},{14,10},{16,20},{18,... | collective-permute-start | bytes 589832 | tf_op jit(solution)/shard_map/prefix/ppermute | solution.py:90
  15.3 2.0 %prefix.18 = (bf16[128,1536]{1,0:T(8,128)(2,1)S(1)}, f32[128,1536]{1,0:T(8,128)S(1)}) custom-call(bf16[128,4096]{1,0:T(8,128)(2,1)S(1)} %copy-done, bf16[128,4096]{1,0:T(8,128)(2,1)S(1)} %copy-done.1, bf16[128,4096]{1,0:T(8,128)(2,1)S(1)} %copy-done.3, f32[256,128]{1,0:T(8,128)S(1)} %get-tuple-element.113.refs_3_), custom_call_target="tpu_custom_call" | custom-call | flops 1 | bytes 1 | tf_op jit(solution)/shard_map/prefix/pallas_call | solution.py:38
  19.7 3.0 %collective-permute-done.3.refs_1_.refs_2_ = f32[192,128]{1,0:T(8,128)S(1)} collective-permute-done((f32[192,128]{1,0:T(8,128)S(1)}, f32[192,128]{1,0:T(8,128)S(1)}, u32[]{:S(2)}, u32[]{:S(2)}) %collective-permute-start.3) | collective-permute-done | bytes 98336 | tf_op jit(solution)/shard_map/prefix/ppermute | solution.py:90
  22.8 2.6 %collective-permute-start.11 = (f32[192,128]{1,0:T(8,128)S(1)}, f32[192,128]{1,0:T(8,128)S(1)}, u32[]{:S(2)}, u32[]{:S(2)}) collective-permute-start(f32[192,128]{1,0:T(8,128)S(1)} %prefix.20.refs_3_), channel_id=1, source_target_pairs={{0,16},{2,18},{4,20},{6,22},{8,24},{10,26},{12,28},{14,30},{16,0},... | collective-permute-start | bytes 294920 | tf_op jit(solution)/shard_map/prefix/ppermute | solution.py:90
  25.4 2.5 %collective-permute-start.6 = (f32[256,128]{1,0:T(8,128)S(1)}, f32[256,128]{1,0:T(8,128)S(1)}, u32[]{:S(2)}, u32[]{:S(2)}) collective-permute-start(f32[256,128]{1,0:T(8,128)S(1)} %get-tuple-element.113.refs_3_), channel_id=1, source_target_pairs={{0,6},{2,4},{4,2},{6,0},{8,14},{10,12},{12,10},{14,8},{16,22},{18,... | collective-permute-start | bytes 393224 | tf_op jit(solution)/shard_map/prefix/ppermute | solution.py:90
  28.9 2.0 %prefix.21 = (bf16[128,1536]{1,0:T(8,128)(2,1)S(1)}, f32[128,1536]{1,0:T(8,128)S(1)}) custom-call(bf16[128,4096]{1,0:T(8,128)(2,1)S(1)} %copy-done, bf16[128,4096]{1,0:T(8,128)(2,1)S(1)} %copy-done.2, bf16[128,4096]{1,0:T(8,128)(2,1)S(1)} %copy-done.4, f32[192,128]{1,0:T(8,128)S(1)} %prefix.20.refs_3_), custom_call_target="tpu_custom_call" | custom-call | flops 1 | bytes 1 | tf_op jit(solution)/shard_map/prefix/pallas_call | solution.py:38
  34.5 2.5 %collective-permute-done.10.refs_1_.refs_2_ = f32[192,128]{1,0:T(8,128)S(1)} collective-permute-done((f32[192,128]{1,0:T(8,128)S(1)}, f32[192,128]{1,0:T(8,128)S(1)}, u32[]{:S(2)}, u32[]{:S(2)}) %collective-permute-start.10) | collective-permute-done | bytes 98336 | tf_op jit(solution)/shard_map/prefix/ppermute | solution.py:90
  45.5 2.0 %collective-permute-done.12.refs_1_.refs_2_ = f32[128,128]{1,0:T(8,128)S(1)} collective-permute-done((f32[128,128]{1,0:T(8,128)S(1)}, f32[128,128]{1,0:T(8,128)S(1)}, u32[]{:S(2)}, u32[]{:S(2)}) %collective-permute-start.12) | collective-permute-done | bytes 65568 | tf_op jit(solution)/shard_map/prefix/ppermute | solution.py:90
  48.7 2.6 %collective-permute-start.26 = (f32[384,128]{1,0:T(8,128)S(1)}, f32[384,128]{1,0:T(8,128)S(1)}, u32[]{:S(2)}, u32[]{:S(2)}) collective-permute-start(f32[384,128]{1,0:T(8,128)S(1)} %get-tuple-element.135.refs_3_), channel_id=1, source_target_pairs={{0,6},{2,4},{4,2},{6,0},{8,14},{10,12},{12,10},{14,8},{16,22},{18,... | collective-permute-start | bytes 589832 | tf_op jit(solution)/shard_map/prefix/ppermute | solution.py:90
  51.3 2.0 %collective-permute-done.15.refs_0_ = f32[128,128]{1,0:T(8,128)S(1)} collective-permute-done((f32[128,128]{1,0:T(8,128)S(1)}, f32[128,128]{1,0:T(8,128)S(1)}, u32[]{:S(2)}, u32[]{:S(2)}) %collective-permute-start.15) | collective-permute-done | bytes 65568 | tf_op jit(solution)/shard_map/prefix/ppermute | solution.py:90
  64.4 2.4 %collective-permute-done.23.refs_3_ = f32[256,128]{1,0:T(8,128)S(1)} collective-permute-done((f32[256,128]{1,0:T(8,128)S(1)}, f32[256,128]{1,0:T(8,128)S(1)}, u32[]{:S(2)}, u32[]{:S(2)}) %collective-permute-start.23) | collective-permute-done | bytes 131104 | tf_op jit(solution)/shard_map/prefix/ppermute | solution.py:90
  70.5 2.2 %collective-permute-start.30 = (f32[384,128]{1,0:T(8,128)S(1)}, f32[384,128]{1,0:T(8,128)S(1)}, u32[]{:S(2)}, u32[]{:S(2)}) collective-permute-start(f32[384,128]{1,0:T(8,128)S(1)} %get-tuple-element.154.refs_6_), channel_id=1, source_target_pairs={{0,6},{2,4},{4,2},{6,0},{8,14},{10,12},{12,10},{14,8},{16,22},{18,... | collective-permute-start | bytes 589832 | tf_op jit(solution)/shard_map/suffix/ppermute | solution.py:90
  77.7 3.4 %suffix.18 = (bf16[128,4096]{1,0:T(8,128)(2,1)}, f32[128,1536]{1,0:T(8,128)S(1)}, f32[128,1536]{1,0:T(8,128)S(1)}) custom-call(bf16[128,4096]{1,0:T(8,128)(2,1)S(1)} %copy-done, bf16[128,4096]{1,0:T(8,128)(2,1)S(1)} %copy-done.2, bf16[128,4096]{1,0:T(8,128)(2,1)S(1)} %copy-done.4, bf16[128,1536]{1,0:T(8,128)(2,1)S(1)} %get-tuple-element.161.refs_3_, ...), custom_call_target="tpu_custom_call" | custom-call | flops 1 | bytes 1 | tf_op jit(solution)/shard_map/suffix/pallas_call | solution.py:38
  83.1 3.2 %collective-permute-done.31.refs_1_.refs_2_ = f32[192,128]{1,0:T(8,128)S(1)} collective-permute-done((f32[192,128]{1,0:T(8,128)S(1)}, f32[192,128]{1,0:T(8,128)S(1)}, u32[]{:S(2)}, u32[]{:S(2)}) %collective-permute-start.31) | collective-permute-done | bytes 98336 | tf_op jit(solution)/shard_map/suffix/ppermute | solution.py:90
  91.5 3.5 %suffix.21 = (bf16[128,4096]{1,0:T(8,128)(2,1)}, f32[128,1536]{1,0:T(8,128)S(1)}, f32[128,1536]{1,0:T(8,128)S(1)}) custom-call(bf16[128,4096]{1,0:T(8,128)(2,1)S(1)} %copy-done, bf16[128,4096]{1,0:T(8,128)(2,1)S(1)} %copy-done.2, bf16[128,4096]{1,0:T(8,128)(2,1)S(1)} %copy-done.4, ...), custom_call_target="tpu_custom_call", output_to_operand_aliasing={{0}: (6, {})} | custom-call | flops 1 | bytes 1 | tf_op jit(solution)/shard_map/suffix/pallas_call | solution.py:38
  95.1 2.5 %suffix.22 = (bf16[128,4096]{1,0:T(8,128)(2,1)}, f32[128,1024]{1,0:T(8,128)S(1)}, f32[128,1024]{1,0:T(8,128)S(1)}) custom-call(bf16[128,4096]{1,0:T(8,128)(2,1)S(1)} %copy-done, bf16[128,4096]{1,0:T(8,128)(2,1)S(1)} %copy-done.2, bf16[128,4096]{1,0:T(8,128)(2,1)S(1)} %copy-done.4, ...), custom_call_target="tpu_custom_call", output_to_operand_aliasing={{0}: (6, {})} | custom-call | flops 1 | bytes 1 | tf_op jit(solution)/shard_map/suffix/pallas_call | solution.py:38
  99.8 3.4 %collective-permute-done.38.refs_1_.refs_2_ = f32[192,128]{1,0:T(8,128)S(1)} collective-permute-done((f32[192,128]{1,0:T(8,128)S(1)}, f32[192,128]{1,0:T(8,128)S(1)}, u32[]{:S(2)}, u32[]{:S(2)}) %collective-permute-start.38) | collective-permute-done | bytes 98336 | tf_op jit(solution)/shard_map/suffix/ppermute | solution.py:90
  104.8 2.5 %collective-permute-start.46 = (f32[384,128]{1,0:T(8,128)S(1)}, f32[384,128]{1,0:T(8,128)S(1)}, u32[]{:S(2)}, u32[]{:S(2)}) collective-permute-start(f32[384,128]{1,0:T(8,128)S(1)} %get-tuple-element.197), channel_id=1, source_target_pairs={{0,2},{2,0},{4,6},{6,4},{8,10},{10,8},{12,14},{14,12},{16,18},{18,... | collective-permute-start | bytes 589832 | tf_op jit(solution)/shard_map/suffix/ppermute | solution.py:90
  111.0 2.1 %collective-permute-done.40.refs_1_.refs_2_ = f32[128,128]{1,0:T(8,128)S(1)} collective-permute-done((f32[128,128]{1,0:T(8,128)S(1)}, f32[128,128]{1,0:T(8,128)S(1)}, u32[]{:S(2)}, u32[]{:S(2)}) %collective-permute-start.40) | collective-permute-done | bytes 65568 | tf_op jit(solution)/shard_map/suffix/ppermute | solution.py:90
  118.3 2.0 %collective-permute-start.45 = (f32[128,128]{1,0:T(8,128)S(1)}, f32[128,128]{1,0:T(8,128)S(1)}, u32[]{:S(2)}, u32[]{:S(2)}) collective-permute-start(f32[128,128]{1,0:T(8,128)S(1)} %get-tuple-element.194.refs_8_), channel_id=1, source_target_pairs={{0,8},{2,10},{4,12},{6,14},{8,0},{10,2},{12,4},{14,6},{16,24},{18,... | collective-permute-start | bytes 196616 | tf_op jit(solution)/shard_map/suffix/ppermute | solution.py:90
  124.6 2.1 %collective-permute-start.49 = (f32[256,128]{1,0:T(8,128)S(1)}, f32[256,128]{1,0:T(8,128)S(1)}, u32[]{:S(2)}, u32[]{:S(2)}) collective-permute-start(f32[256,128]{1,0:T(8,128)S(1)} %get-tuple-element.201), channel_id=1, source_target_pairs={{0,2},{2,0},{4,6},{6,4},{8,10},{10,8},{12,14},{14,12},{16,18},{18,... | collective-permute-start | bytes 393224 | tf_op jit(solution)/shard_map/suffix/ppermute | solution.py:90
  129.7 3.4 %collective-permute-done.50.refs_2_ = f32[256,128]{1,0:T(8,128)S(1)} collective-permute-done((f32[256,128]{1,0:T(8,128)S(1)}, f32[256,128]{1,0:T(8,128)S(1)}, u32[]{:S(2)}, u32[]{:S(2)}) %collective-permute-start.50) | collective-permute-done | bytes 131104 | tf_op jit(solution)/shard_map/suffix/ppermute | solution.py:90
  (144 shorter events, 70.5 us)
Async XLA Ops:
  7.5 10.6 %collective-permute-start = (f32[384,128]{1,0:T(8,128)S(1)}, f32[384,128]{1,0:T(8,128)S(1)}, u32[]{:S(2)}, u32[]{:S(2)}) collective-permute-start(f32[384,128]{1,0:T(8,128)S(1)} %get-tuple-element.109), channel_id=1, source_target_pairs={{0,2},{2,0},{4,6},{6,4},{8,10},{10,8},{12,14},{14,12},{16,18},{18,... | collective-permute-start | bytes 589832 | tf_op jit(solution)/shard_map/prefix/ppermute | solution.py:90
  8.0 10.0 %collective-permute-start.1 = (f32[384,128]{1,0:T(8,128)S(1)}, f32[384,128]{1,0:T(8,128)S(1)}, u32[]{:S(2)}, u32[]{:S(2)}) collective-permute-start(f32[384,128]{1,0:T(8,128)S(1)} %get-tuple-element.110), channel_id=1, source_target_pairs={{0,4},{2,6},{4,0},{6,2},{8,12},{10,14},{12,8},{14,10},{16,20},{18,... | collective-permute-start | bytes 589832 | tf_op jit(solution)/shard_map/prefix/ppermute | solution.py:90
  8.5 19.4 %collective-permute-start.9 = (f32[384,128]{1,0:T(8,128)S(1)}, f32[384,128]{1,0:T(8,128)S(1)}, u32[]{:S(2)}, u32[]{:S(2)}) collective-permute-start(f32[384,128]{1,0:T(8,128)S(1)} %get-tuple-element.112.refs_2_), channel_id=1, source_target_pairs={{0,6},{2,4},{4,2},{6,0},{8,14},{10,12},{12,10},{14,8},{16,22},{18,... | collective-permute-start | bytes 589832 | tf_op jit(solution)/shard_map/prefix/ppermute | solution.py:90
  11.4 17.0 %collective-permute-start.7 = (f32[384,128]{1,0:T(8,128)S(1)}, f32[384,128]{1,0:T(8,128)S(1)}, u32[]{:S(2)}, u32[]{:S(2)}) collective-permute-start(f32[384,128]{1,0:T(8,128)S(1)} %get-tuple-element.124), channel_id=1, source_target_pairs={{0,2},{2,0},{4,6},{6,4},{8,10},{10,8},{12,14},{14,12},{16,18},{18,... | collective-permute-start | bytes 589832 | tf_op jit(solution)/shard_map/prefix/ppermute | solution.py:90
  13.2 19.1 %collective-permute-start.8 = (f32[384,128]{1,0:T(8,128)S(1)}, f32[384,128]{1,0:T(8,128)S(1)}, u32[]{:S(2)}, u32[]{:S(2)}) collective-permute-start(f32[384,128]{1,0:T(8,128)S(1)} %get-tuple-element.125), channel_id=1, source_target_pairs={{0,4},{2,6},{4,0},{6,2},{8,12},{10,14},{12,8},{14,10},{16,20},{18,... | collective-permute-start | bytes 589832 | tf_op jit(solution)/shard_map/prefix/ppermute | solution.py:90
  22.8 11.2 %collective-permute-start.11 = (f32[192,128]{1,0:T(8,128)S(1)}, f32[192,128]{1,0:T(8,128)S(1)}, u32[]{:S(2)}, u32[]{:S(2)}) collective-permute-start(f32[192,128]{1,0:T(8,128)S(1)} %prefix.20.refs_3_), channel_id=1, source_target_pairs={{0,16},{2,18},{4,20},{6,22},{8,24},{10,26},{12,28},{14,30},{16,0},... | collective-permute-start | bytes 294920 | tf_op jit(solution)/shard_map/prefix/ppermute | solution.py:90
  25.4 12.0 %collective-permute-start.6 = (f32[256,128]{1,0:T(8,128)S(1)}, f32[256,128]{1,0:T(8,128)S(1)}, u32[]{:S(2)}, u32[]{:S(2)}) collective-permute-start(f32[256,128]{1,0:T(8,128)S(1)} %get-tuple-element.113.refs_3_), channel_id=1, source_target_pairs={{0,6},{2,4},{4,2},{6,0},{8,14},{10,12},{12,10},{14,8},{16,22},{18,... | collective-permute-start | bytes 393224 | tf_op jit(solution)/shard_map/prefix/ppermute | solution.py:90
  39.6 14.0 %collective-permute-start.18 = (f32[384,128]{1,0:T(8,128)S(1)}, f32[384,128]{1,0:T(8,128)S(1)}, u32[]{:S(2)}, u32[]{:S(2)}) collective-permute-start(f32[384,128]{1,0:T(8,128)S(1)} %get-tuple-element.139), channel_id=1, source_target_pairs={{0,2},{2,0},{4,6},{6,4},{8,10},{10,8},{12,14},{14,12},{16,18},{18,... | collective-permute-start | bytes 589832 | tf_op jit(solution)/shard_map/prefix/ppermute | solution.py:90
  41.2 13.8 %collective-permute-start.19 = (f32[384,128]{1,0:T(8,128)S(1)}, f32[384,128]{1,0:T(8,128)S(1)}, u32[]{:S(2)}, u32[]{:S(2)}) collective-permute-start(f32[384,128]{1,0:T(8,128)S(1)} %get-tuple-element.140), channel_id=1, source_target_pairs={{0,4},{2,6},{4,0},{6,2},{8,12},{10,14},{12,8},{14,10},{16,20},{18,... | collective-permute-start | bytes 589832 | tf_op jit(solution)/shard_map/prefix/ppermute | solution.py:90
  42.7 13.9 %collective-permute-start.20 = (f32[384,128]{1,0:T(8,128)S(1)}, f32[384,128]{1,0:T(8,128)S(1)}, u32[]{:S(2)}, u32[]{:S(2)}) collective-permute-start(f32[384,128]{1,0:T(8,128)S(1)} %get-tuple-element.132.refs_3_), channel_id=1, source_target_pairs={{0,6},{2,4},{4,2},{6,0},{8,14},{10,12},{12,10},{14,8},{16,22},{18,... | collective-permute-start | bytes 589832 | tf_op jit(solution)/shard_map/prefix/ppermute | solution.py:90
  48.7 12.9 %collective-permute-start.26 = (f32[384,128]{1,0:T(8,128)S(1)}, f32[384,128]{1,0:T(8,128)S(1)}, u32[]{:S(2)}, u32[]{:S(2)}) collective-permute-start(f32[384,128]{1,0:T(8,128)S(1)} %get-tuple-element.135.refs_3_), channel_id=1, source_target_pairs={{0,6},{2,4},{4,2},{6,0},{8,14},{10,12},{12,10},{14,8},{16,22},{18,... | collective-permute-start | bytes 589832 | tf_op jit(solution)/shard_map/prefix/ppermute | solution.py:90
  69.7 11.8 %collective-permute-start.29 = (f32[384,128]{1,0:T(8,128)S(1)}, f32[384,128]{1,0:T(8,128)S(1)}, u32[]{:S(2)}, u32[]{:S(2)}) collective-permute-start(f32[384,128]{1,0:T(8,128)S(1)} %get-tuple-element.168), channel_id=1, source_target_pairs={{0,4},{2,6},{4,0},{6,2},{8,12},{10,14},{12,8},{14,10},{16,20},{18,... | collective-permute-start | bytes 589832 | tf_op jit(solution)/shard_map/suffix/ppermute | solution.py:90
  70.5 11.1 %collective-permute-start.30 = (f32[384,128]{1,0:T(8,128)S(1)}, f32[384,128]{1,0:T(8,128)S(1)}, u32[]{:S(2)}, u32[]{:S(2)}) collective-permute-start(f32[384,128]{1,0:T(8,128)S(1)} %get-tuple-element.154.refs_6_), channel_id=1, source_target_pairs={{0,6},{2,4},{4,2},{6,0},{8,14},{10,12},{12,10},{14,8},{16,22},{18,... | collective-permute-start | bytes 589832 | tf_op jit(solution)/shard_map/suffix/ppermute | solution.py:90
  73.3 15.6 %collective-permute-start.35 = (f32[384,128]{1,0:T(8,128)S(1)}, f32[384,128]{1,0:T(8,128)S(1)}, u32[]{:S(2)}, u32[]{:S(2)}) collective-permute-start(f32[384,128]{1,0:T(8,128)S(1)} %get-tuple-element.181), channel_id=1, source_target_pairs={{0,2},{2,0},{4,6},{6,4},{8,10},{10,8},{12,14},{14,12},{16,18},{18,... | collective-permute-start | bytes 589832 | tf_op jit(solution)/shard_map/suffix/ppermute | solution.py:90
  73.9 16.0 %collective-permute-start.36 = (f32[384,128]{1,0:T(8,128)S(1)}, f32[384,128]{1,0:T(8,128)S(1)}, u32[]{:S(2)}, u32[]{:S(2)}) collective-permute-start(f32[384,128]{1,0:T(8,128)S(1)} %get-tuple-element.182), channel_id=1, source_target_pairs={{0,4},{2,6},{4,0},{6,2},{8,12},{10,14},{12,8},{14,10},{16,20},{18,... | collective-permute-start | bytes 589832 | tf_op jit(solution)/shard_map/suffix/ppermute | solution.py:90
  77.0 20.6 %collective-permute-start.37 = (f32[384,128]{1,0:T(8,128)S(1)}, f32[384,128]{1,0:T(8,128)S(1)}, u32[]{:S(2)}, u32[]{:S(2)}) collective-permute-start(f32[384,128]{1,0:T(8,128)S(1)} %get-tuple-element.155.refs_6_), channel_id=1, source_target_pairs={{0,6},{2,4},{4,2},{6,0},{8,14},{10,12},{12,10},{14,8},{16,22},{18,... | collective-permute-start | bytes 589832 | tf_op jit(solution)/shard_map/suffix/ppermute | solution.py:90
  86.3 12.4 %collective-permute-start.39 = (f32[192,128]{1,0:T(8,128)S(1)}, f32[192,128]{1,0:T(8,128)S(1)}, u32[]{:S(2)}, u32[]{:S(2)}) collective-permute-start(f32[192,128]{1,0:T(8,128)S(1)} %suffix.20.refs_7_), channel_id=1, source_target_pairs={{0,16},{2,18},{4,20},{6,22},{8,24},{10,26},{12,28},{14,30},{16,0},... | collective-permute-start | bytes 294920 | tf_op jit(solution)/shard_map/suffix/ppermute | solution.py:90
  88.0 15.7 %collective-permute-start.32 = (f32[256,128]{1,0:T(8,128)S(1)}, f32[256,128]{1,0:T(8,128)S(1)}, u32[]{:S(2)}, u32[]{:S(2)}) collective-permute-start(f32[256,128]{1,0:T(8,128)S(1)} %get-tuple-element.178), channel_id=1, source_target_pairs={{0,2},{2,0},{4,6},{6,4},{8,10},{10,8},{12,14},{14,12},{16,18},{18,... | collective-permute-start | bytes 393224 | tf_op jit(solution)/shard_map/suffix/ppermute | solution.py:90
  88.9 14.9 %collective-permute-start.33 = (f32[256,128]{1,0:T(8,128)S(1)}, f32[256,128]{1,0:T(8,128)S(1)}, u32[]{:S(2)}, u32[]{:S(2)}) collective-permute-start(f32[256,128]{1,0:T(8,128)S(1)} %get-tuple-element.179), channel_id=1, source_target_pairs={{0,4},{2,6},{4,0},{6,2},{8,12},{10,14},{12,8},{14,10},{16,20},{18,... | collective-permute-start | bytes 393224 | tf_op jit(solution)/shard_map/suffix/ppermute | solution.py:90
  89.8 13.9 %collective-permute-start.34 = (f32[256,128]{1,0:T(8,128)S(1)}, f32[256,128]{1,0:T(8,128)S(1)}, u32[]{:S(2)}, u32[]{:S(2)}) collective-permute-start(f32[256,128]{1,0:T(8,128)S(1)} %get-tuple-element.164.refs_6_), channel_id=1, source_target_pairs={{0,6},{2,4},{4,2},{6,0},{8,14},{10,12},{12,10},{14,8},{16,22},{18,... | collective-permute-start | bytes 393224 | tf_op jit(solution)/shard_map/suffix/ppermute | solution.py:90
  104.8 15.5 %collective-permute-start.46 = (f32[384,128]{1,0:T(8,128)S(1)}, f32[384,128]{1,0:T(8,128)S(1)}, u32[]{:S(2)}, u32[]{:S(2)}) collective-permute-start(f32[384,128]{1,0:T(8,128)S(1)} %get-tuple-element.197), channel_id=1, source_target_pairs={{0,2},{2,0},{4,6},{6,4},{8,10},{10,8},{12,14},{14,12},{16,18},{18,... | collective-permute-start | bytes 589832 | tf_op jit(solution)/shard_map/suffix/ppermute | solution.py:90
  107.2 13.9 %collective-permute-start.47 = (f32[384,128]{1,0:T(8,128)S(1)}, f32[384,128]{1,0:T(8,128)S(1)}, u32[]{:S(2)}, u32[]{:S(2)}) collective-permute-start(f32[384,128]{1,0:T(8,128)S(1)} %get-tuple-element.198), channel_id=1, source_target_pairs={{0,4},{2,6},{4,0},{6,2},{8,12},{10,14},{12,8},{14,10},{16,20},{18,... | collective-permute-start | bytes 589832 | tf_op jit(solution)/shard_map/suffix/ppermute | solution.py:90
  107.2 14.7 %collective-permute-start.48 = (f32[384,128]{1,0:T(8,128)S(1)}, f32[384,128]{1,0:T(8,128)S(1)}, u32[]{:S(2)}, u32[]{:S(2)}) collective-permute-start(f32[384,128]{1,0:T(8,128)S(1)} %get-tuple-element.189.refs_3_), channel_id=1, source_target_pairs={{0,6},{2,4},{4,2},{6,0},{8,14},{10,12},{12,10},{14,8},{16,22},{18,... | collective-permute-start | bytes 589832 | tf_op jit(solution)/shard_map/suffix/ppermute | solution.py:90
  115.8 12.5 %collective-permute-start.54 = (f32[384,128]{1,0:T(8,128)S(1)}, f32[384,128]{1,0:T(8,128)S(1)}, u32[]{:S(2)}, u32[]{:S(2)}) collective-permute-start(f32[384,128]{1,0:T(8,128)S(1)} %get-tuple-element.192.refs_3_), channel_id=1, source_target_pairs={{0,6},{2,4},{4,2},{6,0},{8,14},{10,12},{12,10},{14,8},{16,22},{18,... | collective-permute-start | bytes 589832 | tf_op jit(solution)/shard_map/suffix/ppermute | solution.py:90
  (39 other events, 236.7 us)

commit v4 on v3

--- a/solution.py
+++ b/solution.py
@@ -8,7 +8,7 @@
 from jax.sharding import PartitionSpec as P
 
 HEAD_DIM = 128
-GROUPS = 3
+GROUPS = 2
 HIDDEN = 4 * 10**9
 PLANE = 4
 
@@ -26,7 +26,7 @@
     def __init__(self):
         self.last = None
 
-    def __call__(self, body, outs, *args, flops=1, hbm_args=(), hbm_outs=0, aliases=None, scratch=()):
+    def __call__(self, body, outs, *args, flops=1, hbm_args=(), hbm_outs=0, aliases=None, scratch=(), mib=16):
         specs = [pl.BlockSpec(memory_space=pltpu.HBM if i in hbm_args else pltpu.VMEM) for i in range(len(args))]
         kernel, operands, count = body, args, len(args)
         if self.last is not None and not any(self.last is arg for arg in args):
@@ -45,10 +45,10 @@
             scratch_shapes=scratch,
             input_output_aliases=aliases or {},
             cost_estimate=pl.CostEstimate(flops=flops, bytes_accessed=1, transcendentals=0),
-            compiler_params=pltpu.CompilerParams(vmem_limit_bytes=16 * 1024 * 1024),
+            compiler_params=pltpu.CompilerParams(vmem_limit_bytes=mib * 1024 * 1024),
         )(*operands)
         self.last = results[-1]
-        return results
+        return list(results)
 
 
 def f32(*shape):
@@ -197,7 +197,7 @@
     results = []
     steps = [scan_steps(run, parts, reverse, results) for parts in groups]
     count = 2 * ((lax.axis_size("seq") // PLANE).bit_length() - 1)
-    events = [(-1.0 if g == 0 else 1.0 + g / 10, filler) for g, filler in enumerate(fillers)]
+    events = [(g / 10 - 1.0, filler) for g, filler in enumerate(fillers)]
     for g, one in enumerate(steps):
         next(one)
         behind = 0.5 + 1.2 * g if g else 0.0
@@ -207,39 +207,37 @@
         event()
 
 
-def state_of(first, count, p, left, right, outs):
-    for k in range(PLANE):
-        for j in range(count):
-            at = columns(first + (p ^ k) * count + j)
-            outs[k][pl.ds(j * HEAD_DIM, HEAD_DIM), :] = dot(left[:, at], right[:, at], CONTRACT_ROWS)
-
-
-def first_state_kernel(first, count, keys, values, *refs):
-    outs, (left, right, sems) = refs[:PLANE], refs[PLANE:]
-    here = pl.ds(first * HEAD_DIM, PLANE * count * HEAD_DIM)
+def fetch(first, sources, targets, sems):
+    here = pl.ds(first * HEAD_DIM, targets[0].shape[1])
     copies = [
         pltpu.make_async_copy(source.at[:, here], target, sems.at[i])
-        for i, (source, target) in enumerate(((keys, left), (values, right)))
+        for i, (source, target) in enumerate(zip(sources, targets, strict=True))
     ]
     for copy in copies:
         copy.start()
     for copy in copies:
         copy.wait()
-    state_of(0, count, place()[0], left, right, outs)
-
-
-def state_kernel(first, count, keys, values, *outs):
-    state_of(first, count, place()[0], keys, values, outs)
-
-
-def local_kernel(first, scale, queries, keys, values, weights, inner):
-    mask = causal(queries.shape[0])
+
+
+def state_kernel(first, count, keys, values, *refs):
+    outs, (left, right, sems) = refs[:PLANE], refs[PLANE:]
+    p, _ = place()
+    fetch(first, (keys, values), (left, right), sems)
+    for k in range(PLANE):
+        for j in range(count):
+            at = columns((p ^ k) * count + j)
+            outs[k][pl.ds(j * HEAD_DIM, HEAD_DIM), :] = dot(left[:, at], right[:, at], CONTRACT_ROWS)
+
+
+def local_kernel(first, scale, queries, keys, values, weights, inner, q, k, v, sems):
+    fetch(first, (queries, keys, values), (q, k, v), sems)
+    mask = causal(q.shape[0])
     for h in range(inner.shape[1] // HEAD_DIM):
-        at, here = columns(first + h), columns(h)
-        scores = dot(queries[:, at], keys[:, at], CONTRACT_COLUMNS) * scale
+        at = columns(h)
+        scores = dot(q[:, at], k[:, at], CONTRACT_COLUMNS) * scale
         w = jnp.where(mask, scores, 0.0).astype(jnp.bfloat16)
-        weights[:, here] = w
-        inner[:, here] = dot(w, values[:, at])
+        weights[:, at] = w
+        inner[:, at] = dot(w, v[:, at])
 
 
 def attend_kernel(first, count, scale, queries, inner, cotangent, gain, *refs):
@@ -344,12 +342,13 @@
         for g, (first, count) in enumerate(groups):
             states.append(
                 run(
-                    functools.partial(state_kernel if g else first_state_kernel, first, count),
+                    functools.partial(state_kernel, first, count),
                     states_of[g], keys, values,
-                    hbm_args=() if g else (0, 1),
-                    scratch=[] if g else [block(0), block(0), pltpu.SemaphoreType.DMA((2,))],
+                    hbm_args=(0, 1), scratch=[block(g)] * 2 + [pltpu.SemaphoreType.DMA((2,))],
+                    mib=16 if g else 54,
                 )
             )
+            run.last = states[-1][0]
 
     local, attended, local_grads, ends = [], [], [], []
 
@@ -359,6 +358,7 @@
                 functools.partial(local_kernel, groups[g][0], scale),
                 [bf16(tokens, shares[g]), f32(tokens, shares[g])],
                 queries, keys, values,
+                hbm_args=(0, 1, 2), scratch=[block(g)] * 3 + [pltpu.SemaphoreType.DMA((3,))],
             )
         )
 

time: 135 us -> 127 us (0.941)
  starting transfers between devices: 66.8 us -> 50 us
  waiting for transfers between devices: 38.7 us -> 50.5 us
  local copies, waits for them, and re-layouts: 3.69 us -> 0.97 us
    ppermute x54 -> x36, starting transfers between devices: 66.7 us -> 50 us  [exchange(): return lax.ppermute(value, 'seq', [(s, s ^ distance) for s in range(n)])]
    ppermute x54 -> x36, waiting for transfers between devices: 37.4 us -> 49.2 us  [exchange(): return lax.ppermute(value, 'seq', [(s, s ^ distance) for s in range(n)])]
    unnamed x16 -> x14, local copies, waits for them, and re-layouts: 3.69 us -> 0.97 us
    pallas_call x42 -> x28, Pallas kernels: 24.1 us -> 24.7 us  [__call__(): pl.pallas_call(kernel, out_shape=outs, in_specs=specs, out_specs=[pl.Bloc...]
  transfers between devices with their start and end apart: 55 -> 37, of which waited for: 24 -> 22; matrix products, arithmetic and copies ran while one was open for 0% -> 0% of each run, Pallas kernels for 16% -> 15%
where the time goes in v4:
time: 127 us
  waiting for transfers between devices  50.5 us (40%)
  starting transfers between devices  50 us (39%)
  Pallas kernels  24.7 us (19%)
    ppermute x36, starting transfers between devices, exchange(): return lax.ppermute(value, 'seq', [(s, s ^ distance) for s in range(n)])  50 us
    ppermute x36, waiting for transfers between devices, exchange(): return lax.ppermute(value, 'seq', [(s, s ^ distance) for s in range(n)])  49.2 us
    pallas_call x28, Pallas kernels, __call__(): pl.pallas_call(kernel, out_shape=outs, in_specs=specs, out_specs=[pl.Bloc...  24.7 us
  transfers between devices with their start and end apart: 37, of which 22 were waited for; matrix products, arithmetic and copies ran while one was open for 0% of the time, Pallas kernels for 15%

profile of v4, /device:TPU:0, one launch (start us, length us, event | category | flops | bytes accessed | tf_op | source)
XLA Modules:
  0.0 127.2 jit_solution(5788810283057216023)
XLA Ops:
  0.7 2.7 %state.2 = (f32[512,128]{1,0:T(8,128)}, f32[512,128]{1,0:T(8,128)}, f32[512,128]{1,0:T(8,128)}, f32[512,128]{1,0:T(8,128)}) custom-call(bf16[128,4096]{1,0:T(8,128)(2,1)} %keys.3, bf16[128,4096]{1,0:T(8,128)(2,1)} %values.3), custom_call_target="tpu_custom_call" | custom-call | flops 1 | bytes 1 | tf_op jit(solution)/shard_map/state/pallas_call | solution.py:38
  3.3 3.0 %collective-permute-start.3 = (f32[512,128]{1,0:T(8,128)}, f32[512,128]{1,0:T(8,128)S(1)}, u32[]{:S(2)}, u32[]{:S(2)}) collective-permute-start(f32[512,128]{1,0:T(8,128)} %get-tuple-element.81), channel_id=1, source_target_pairs={{0,2},{2,0},{4,6},{6,4},{8,10},{10,8},{12,14},{14,12},{16,18},{18,... | collective-permute-start | bytes 786440 | tf_op jit(solution)/shard_map/prefix/ppermute | solution.py:90
  9.4 2.0 %collective-permute-start = (f32[512,128]{1,0:T(8,128)S(1)}, f32[512,128]{1,0:T(8,128)S(1)}, u32[]{:S(2)}, u32[]{:S(2)}) collective-permute-start(f32[512,128]{1,0:T(8,128)S(1)} %get-tuple-element.78), channel_id=1, source_target_pairs={{0,2},{2,0},{4,6},{6,4},{8,10},{10,8},{12,14},{14,12},{16,18},{18,... | collective-permute-start | bytes 786440 | tf_op jit(solution)/shard_map/prefix/ppermute | solution.py:90
  12.9 2.7 %prefix.12 = (bf16[128,2048]{1,0:T(8,128)(2,1)S(1)}, f32[128,2048]{1,0:T(8,128)S(1)}) custom-call(bf16[128,4096]{1,0:T(8,128)(2,1)S(1)} %copy-done.2, bf16[128,4096]{1,0:T(8,128)(2,1)S(1)} %copy-done, bf16[128,4096]{1,0:T(8,128)(2,1)S(1)} %copy-done.1, f32[512,128]{1,0:T(8,128)S(1)} %get-tuple-element.74.refs_3_.refs_0_.refs_2_), custom_call_target="tpu_custom_call" | custom-call | flops 1 | bytes 1 | tf_op jit(solution)/shard_map/prefix/pallas_call | solution.py:38
  15.7 2.9 %prefix.13 = (bf16[128,2048]{1,0:T(8,128)(2,1)S(1)}, f32[128,2048]{1,0:T(8,128)S(1)}) custom-call(bf16[128,4096]{1,0:T(8,128)(2,1)S(1)} %copy-done.2, bf16[128,4096]{1,0:T(8,128)(2,1)S(1)} %copy-done, bf16[128,4096]{1,0:T(8,128)(2,1)S(1)} %copy-done.1, f32[128,2048]{1,0:T(8,128)S(1)} %get-tuple-element.75.refs_3_.refs_1_), custom_call_target="tpu_custom_call" | custom-call | flops 1 | bytes 1 | tf_op jit(solution)/shard_map/prefix/pallas_call | solution.py:38
  18.7 2.7 %collective-permute-done.4.refs_2_.refs_4_ = f32[512,128]{1,0:T(8,128)S(1)} collective-permute-done((f32[512,128]{1,0:T(8,128)}, f32[512,128]{1,0:T(8,128)S(1)}, u32[]{:S(2)}, u32[]{:S(2)}) %collective-permute-start.4) | collective-permute-done | bytes 262176 | tf_op jit(solution)/shard_map/prefix/ppermute | solution.py:90
  23.1 3.4 %collective-permute-done.6.refs_1_.refs_2_ = f32[256,128]{1,0:T(8,128)S(1)} collective-permute-done((f32[256,128]{1,0:T(8,128)S(1)}, f32[256,128]{1,0:T(8,128)S(1)}, u32[]{:S(2)}, u32[]{:S(2)}) %collective-permute-start.6) | collective-permute-done | bytes 131104 | tf_op jit(solution)/shard_map/prefix/ppermute | solution.py:90
  26.5 3.8 %collective-permute-start.8 = (f32[256,128]{1,0:T(8,128)S(1)}, f32[256,128]{1,0:T(8,128)S(1)}, u32[]{:S(2)}, u32[]{:S(2)}) collective-permute-start(f32[256,128]{1,0:T(8,128)S(1)} %prefix.15.refs_4_), channel_id=1, source_target_pairs={{0,16},{2,18},{4,20},{6,22},{8,24},{10,26},{12,28},{14,30},{16,0},... | collective-permute-start | bytes 393224 | tf_op jit(solution)/shard_map/prefix/ppermute | solution.py:90
  32.9 1.9 %collective-permute-done.8.refs_0_ = f32[256,128]{1,0:T(8,128)S(1)} collective-permute-done((f32[256,128]{1,0:T(8,128)S(1)}, f32[256,128]{1,0:T(8,128)S(1)}, u32[]{:S(2)}, u32[]{:S(2)}) %collective-permute-start.8) | collective-permute-done | bytes 131104 | tf_op jit(solution)/shard_map/prefix/ppermute | solution.py:90
  34.8 2.9 %collective-permute-done.7.refs_1_.refs_2_ = f32[256,128]{1,0:T(8,128)S(1)} collective-permute-done((f32[256,128]{1,0:T(8,128)S(1)}, f32[256,128]{1,0:T(8,128)S(1)}, u32[]{:S(2)}, u32[]{:S(2)}) %collective-permute-start.7) | collective-permute-done | bytes 131104 | tf_op jit(solution)/shard_map/prefix/ppermute | solution.py:90
  46.1 4.2 %collective-permute-done.11.refs_1_ = f32[256,128]{1,0:T(8,128)S(1)} collective-permute-done((f32[256,128]{1,0:T(8,128)S(1)}, f32[256,128]{1,0:T(8,128)S(1)}, u32[]{:S(2)}, u32[]{:S(2)}) %collective-permute-start.11) | collective-permute-done | bytes 131104 | tf_op jit(solution)/shard_map/prefix/ppermute | solution.py:90
  56.6 4.0 %collective-permute-done.12.refs_1_ = f32[512,128]{1,0:T(8,128)S(1)} collective-permute-done((f32[512,128]{1,0:T(8,128)S(1)}, f32[512,128]{1,0:T(8,128)S(1)}, u32[]{:S(2)}, u32[]{:S(2)}) %collective-permute-start.12) | collective-permute-done | bytes 262176 | tf_op jit(solution)/shard_map/prefix/ppermute | solution.py:90
  60.6 3.3 %collective-permute-done.13.refs_2_ = f32[512,128]{1,0:T(8,128)S(1)} collective-permute-done((f32[512,128]{1,0:T(8,128)S(1)}, f32[512,128]{1,0:T(8,128)S(1)}, u32[]{:S(2)}, u32[]{:S(2)}) %collective-permute-start.13) | collective-permute-done | bytes 262176 | tf_op jit(solution)/shard_map/prefix/ppermute | solution.py:90
  73.2 4.2 %suffix.12 = (bf16[128,4096]{1,0:T(8,128)(2,1)}, f32[128,2048]{1,0:T(8,128)S(1)}, f32[128,2048]{1,0:T(8,128)S(1)}) custom-call(bf16[128,4096]{1,0:T(8,128)(2,1)S(1)} %copy-done.2, bf16[128,4096]{1,0:T(8,128)(2,1)S(1)} %copy-done, bf16[128,4096]{1,0:T(8,128)(2,1)S(1)} %copy-done.1, bf16[128,2048]{1,0:T(8,128)(2,1)S(1)} %get-tuple-element.107.refs_3_, ...), custom_call_target="tpu_custom_call" | custom-call | flops 1 | bytes 1 | tf_op jit(solution)/shard_map/suffix/pallas_call | solution.py:38
  77.4 4.2 %suffix.13 = (bf16[128,4096]{1,0:T(8,128)(2,1)}, f32[128,2048]{1,0:T(8,128)S(1)}, f32[128,2048]{1,0:T(8,128)S(1)}) custom-call(bf16[128,4096]{1,0:T(8,128)(2,1)S(1)} %copy-done.2, bf16[128,4096]{1,0:T(8,128)(2,1)S(1)} %copy-done, bf16[128,4096]{1,0:T(8,128)(2,1)S(1)} %copy-done.1, ...), custom_call_target="tpu_custom_call", output_to_operand_aliasing={{0}: (6, {})} | custom-call | flops 1 | bytes 1 | tf_op jit(solution)/shard_map/suffix/pallas_call | solution.py:38
  84.8 3.3 %collective-permute-done.25.refs_1_.refs_2_ = f32[256,128]{1,0:T(8,128)S(1)} collective-permute-done((f32[256,128]{1,0:T(8,128)S(1)}, f32[256,128]{1,0:T(8,128)S(1)}, u32[]{:S(2)}, u32[]{:S(2)}) %collective-permute-start.25) | collective-permute-done | bytes 131104 | tf_op jit(solution)/shard_map/suffix/ppermute | solution.py:90
  88.2 2.7 %collective-permute-start.27 = (f32[256,128]{1,0:T(8,128)S(1)}, f32[256,128]{1,0:T(8,128)S(1)}, u32[]{:S(2)}, u32[]{:S(2)}) collective-permute-start(f32[256,128]{1,0:T(8,128)S(1)} %suffix.15.refs_4_), channel_id=1, source_target_pairs={{0,16},{2,18},{4,20},{6,22},{8,24},{10,26},{12,28},{14,30},{16,0},... | collective-permute-start | bytes 393224 | tf_op jit(solution)/shard_map/suffix/ppermute | solution.py:90
  90.9 2.0 %collective-permute-done.20.refs_2_.refs_4_ = f32[512,128]{1,0:T(8,128)S(1)} collective-permute-done((f32[512,128]{1,0:T(8,128)S(1)}, f32[512,128]{1,0:T(8,128)S(1)}, u32[]{:S(2)}, u32[]{:S(2)}) %collective-permute-start.20) | collective-permute-done | bytes 262176 | tf_op jit(solution)/shard_map/suffix/ppermute | solution.py:90
  92.9 1.9 %collective-permute-start.26 = (f32[256,128]{1,0:T(8,128)S(1)}, f32[256,128]{1,0:T(8,128)S(1)}, u32[]{:S(2)}, u32[]{:S(2)}) collective-permute-start(f32[256,128]{1,0:T(8,128)S(1)} %get-tuple-element.125.refs_3_), channel_id=1, source_target_pairs={{0,8},{2,10},{4,12},{6,14},{8,0},{10,2},{12,4},{14,6},{16,24},{18,... | collective-permute-start | bytes 393224 | tf_op jit(solution)/shard_map/suffix/ppermute | solution.py:90
  96.3 2.9 %collective-permute-done.26.refs_1_.refs_2_ = f32[256,128]{1,0:T(8,128)S(1)} collective-permute-done((f32[256,128]{1,0:T(8,128)S(1)}, f32[256,128]{1,0:T(8,128)S(1)}, u32[]{:S(2)}, u32[]{:S(2)}) %collective-permute-start.26) | collective-permute-done | bytes 131104 | tf_op jit(solution)/shard_map/suffix/ppermute | solution.py:90
  99.2 2.8 %collective-permute-start.28 = (f32[256,128]{1,0:T(8,128)S(1)}, f32[256,128]{1,0:T(8,128)S(1)}, u32[]{:S(2)}, u32[]{:S(2)}) collective-permute-start(f32[256,128]{1,0:T(8,128)S(1)} %suffix.18.refs_6_), channel_id=1, source_target_pairs={{0,16},{2,18},{4,20},{6,22},{8,24},{10,26},{12,28},{14,30},{16,0},... | collective-permute-start | bytes 393224 | tf_op jit(solution)/shard_map/suffix/ppermute | solution.py:90
  107.9 4.2 %collective-permute-done.30.refs_1_ = f32[256,128]{1,0:T(8,128)S(1)} collective-permute-done((f32[256,128]{1,0:T(8,128)S(1)}, f32[256,128]{1,0:T(8,128)S(1)}, u32[]{:S(2)}, u32[]{:S(2)}) %collective-permute-start.30) | collective-permute-done | bytes 131104 | tf_op jit(solution)/shard_map/suffix/ppermute | solution.py:90
  118.0 3.9 %collective-permute-done.31.refs_1_ = f32[512,128]{1,0:T(8,128)S(1)} collective-permute-done((f32[512,128]{1,0:T(8,128)S(1)}, f32[512,128]{1,0:T(8,128)S(1)}, u32[]{:S(2)}, u32[]{:S(2)}) %collective-permute-start.31) | collective-permute-done | bytes 262176 | tf_op jit(solution)/shard_map/suffix/ppermute | solution.py:90
  121.9 3.7 %collective-permute-done.32.refs_2_ = f32[512,128]{1,0:T(8,128)S(1)} collective-permute-done((f32[512,128]{1,0:T(8,128)S(1)}, f32[512,128]{1,0:T(8,128)S(1)}, u32[]{:S(2)}, u32[]{:S(2)}) %collective-permute-start.32) | collective-permute-done | bytes 262176 | tf_op jit(solution)/shard_map/suffix/ppermute | solution.py:90
  (92 shorter events, 50.9 us)
Async XLA Ops:
  3.3 15.3 %collective-permute-start.3 = (f32[512,128]{1,0:T(8,128)}, f32[512,128]{1,0:T(8,128)S(1)}, u32[]{:S(2)}, u32[]{:S(2)}) collective-permute-start(f32[512,128]{1,0:T(8,128)} %get-tuple-element.81), channel_id=1, source_target_pairs={{0,2},{2,0},{4,6},{6,4},{8,10},{10,8},{12,14},{14,12},{16,18},{18,... | collective-permute-start | bytes 786440 | tf_op jit(solution)/shard_map/prefix/ppermute | solution.py:90
  6.3 15.1 %collective-permute-start.4 = (f32[512,128]{1,0:T(8,128)}, f32[512,128]{1,0:T(8,128)S(1)}, u32[]{:S(2)}, u32[]{:S(2)}) collective-permute-start(f32[512,128]{1,0:T(8,128)} %get-tuple-element.82), channel_id=1, source_target_pairs={{0,4},{2,6},{4,0},{6,2},{8,12},{10,14},{12,8},{14,10},{16,20},{18,... | collective-permute-start | bytes 786440 | tf_op jit(solution)/shard_map/prefix/ppermute | solution.py:90
  7.8 13.5 %collective-permute-start.5 = (f32[512,128]{1,0:T(8,128)}, f32[512,128]{1,0:T(8,128)S(1)}, u32[]{:S(2)}, u32[]{:S(2)}) collective-permute-start(f32[512,128]{1,0:T(8,128)} %get-tuple-element.83), channel_id=1, source_target_pairs={{0,6},{2,4},{4,2},{6,0},{8,14},{10,12},{12,10},{14,8},{16,22},{18,... | collective-permute-start | bytes 786440 | tf_op jit(solution)/shard_map/prefix/ppermute | solution.py:90
  9.4 20.9 %collective-permute-start = (f32[512,128]{1,0:T(8,128)S(1)}, f32[512,128]{1,0:T(8,128)S(1)}, u32[]{:S(2)}, u32[]{:S(2)}) collective-permute-start(f32[512,128]{1,0:T(8,128)S(1)} %get-tuple-element.78), channel_id=1, source_target_pairs={{0,2},{2,0},{4,6},{6,4},{8,10},{10,8},{12,14},{14,12},{16,18},{18,... | collective-permute-start | bytes 786440 | tf_op jit(solution)/shard_map/prefix/ppermute | solution.py:90
  11.4 19.7 %collective-permute-start.1 = (f32[512,128]{1,0:T(8,128)S(1)}, f32[512,128]{1,0:T(8,128)S(1)}, u32[]{:S(2)}, u32[]{:S(2)}) collective-permute-start(f32[512,128]{1,0:T(8,128)S(1)} %get-tuple-element.79), channel_id=1, source_target_pairs={{0,4},{2,6},{4,0},{6,2},{8,12},{10,14},{12,8},{14,10},{16,20},{18,... | collective-permute-start | bytes 786440 | tf_op jit(solution)/shard_map/prefix/ppermute | solution.py:90
  18.6 12.5 %collective-permute-start.2 = (f32[512,128]{1,0:T(8,128)S(1)}, f32[512,128]{1,0:T(8,128)S(1)}, u32[]{:S(2)}, u32[]{:S(2)}) collective-permute-start(f32[512,128]{1,0:T(8,128)S(1)} %get-tuple-element.80), channel_id=1, source_target_pairs={{0,6},{2,4},{4,2},{6,0},{8,14},{10,12},{12,10},{14,8},{16,22},{18,... | collective-permute-start | bytes 786440 | tf_op jit(solution)/shard_map/prefix/ppermute | solution.py:90
  41.4 11.3 %collective-permute-start.15 = (f32[512,128]{1,0:T(8,128)S(1)}, f32[512,128]{1,0:T(8,128)S(1)}, u32[]{:S(2)}, u32[]{:S(2)}) collective-permute-start(f32[512,128]{1,0:T(8,128)S(1)} %get-tuple-element.98), channel_id=1, source_target_pairs={{0,2},{2,0},{4,6},{6,4},{8,10},{10,8},{12,14},{14,12},{16,18},{18,... | collective-permute-start | bytes 786440 | tf_op jit(solution)/shard_map/prefix/ppermute | solution.py:90
  42.0 12.2 %collective-permute-start.16 = (f32[512,128]{1,0:T(8,128)S(1)}, f32[512,128]{1,0:T(8,128)S(1)}, u32[]{:S(2)}, u32[]{:S(2)}) collective-permute-start(f32[512,128]{1,0:T(8,128)S(1)} %get-tuple-element.99), channel_id=1, source_target_pairs={{0,4},{2,6},{4,0},{6,2},{8,12},{10,14},{12,8},{14,10},{16,20},{18,... | collective-permute-start | bytes 786440 | tf_op jit(solution)/shard_map/prefix/ppermute | solution.py:90
  43.6 12.3 %collective-permute-start.17 = (f32[512,128]{1,0:T(8,128)S(1)}, f32[512,128]{1,0:T(8,128)S(1)}, u32[]{:S(2)}, u32[]{:S(2)}) collective-permute-start(f32[512,128]{1,0:T(8,128)S(1)} %get-tuple-element.90.refs_3_), channel_id=1, source_target_pairs={{0,6},{2,4},{4,2},{6,0},{8,14},{10,12},{12,10},{14,8},{16,22},{18,... | collective-permute-start | bytes 786440 | tf_op jit(solution)/shard_map/prefix/ppermute | solution.py:90
  50.7 9.9 %collective-permute-start.12 = (f32[512,128]{1,0:T(8,128)S(1)}, f32[512,128]{1,0:T(8,128)S(1)}, u32[]{:S(2)}, u32[]{:S(2)}) collective-permute-start(f32[512,128]{1,0:T(8,128)S(1)} %get-tuple-element.94), channel_id=1, source_target_pairs={{0,2},{2,0},{4,6},{6,4},{8,10},{10,8},{12,14},{14,12},{16,18},{18,... | collective-permute-start | bytes 786440 | tf_op jit(solution)/shard_map/prefix/ppermute | solution.py:90
  51.7 12.1 %collective-permute-start.13 = (f32[512,128]{1,0:T(8,128)S(1)}, f32[512,128]{1,0:T(8,128)S(1)}, u32[]{:S(2)}, u32[]{:S(2)}) collective-permute-start(f32[512,128]{1,0:T(8,128)S(1)} %get-tuple-element.95), channel_id=1, source_target_pairs={{0,4},{2,6},{4,0},{6,2},{8,12},{10,14},{12,8},{14,10},{16,20},{18,... | collective-permute-start | bytes 786440 | tf_op jit(solution)/shard_map/prefix/ppermute | solution.py:90
  52.7 11.1 %collective-permute-start.14 = (f32[512,128]{1,0:T(8,128)S(1)}, f32[512,128]{1,0:T(8,128)S(1)}, u32[]{:S(2)}, u32[]{:S(2)}) collective-permute-start(f32[512,128]{1,0:T(8,128)S(1)} %get-tuple-element.96.refs_8_), channel_id=1, source_target_pairs={{0,6},{2,4},{4,2},{6,0},{8,14},{10,12},{12,10},{14,8},{16,22},{18,... | collective-permute-start | bytes 786440 | tf_op jit(solution)/shard_map/prefix/ppermute | solution.py:90
  66.6 15.1 %collective-permute-start.22 = (f32[512,128]{1,0:T(8,128)S(1)}, f32[512,128]{1,0:T(8,128)S(1)}, u32[]{:S(2)}, u32[]{:S(2)}) collective-permute-start(f32[512,128]{1,0:T(8,128)S(1)} %get-tuple-element.120), channel_id=1, source_target_pairs={{0,2},{2,0},{4,6},{6,4},{8,10},{10,8},{12,14},{14,12},{16,18},{18,... | collective-permute-start | bytes 786440 | tf_op jit(solution)/shard_map/suffix/ppermute | solution.py:90
  67.9 15.1 %collective-permute-start.23 = (f32[512,128]{1,0:T(8,128)S(1)}, f32[512,128]{1,0:T(8,128)S(1)}, u32[]{:S(2)}, u32[]{:S(2)}) collective-permute-start(f32[512,128]{1,0:T(8,128)S(1)} %get-tuple-element.121), channel_id=1, source_target_pairs={{0,4},{2,6},{4,0},{6,2},{8,12},{10,14},{12,8},{14,10},{16,20},{18,... | collective-permute-start | bytes 786440 | tf_op jit(solution)/shard_map/suffix/ppermute | solution.py:90
  68.9 14.2 %collective-permute-start.24 = (f32[512,128]{1,0:T(8,128)S(1)}, f32[512,128]{1,0:T(8,128)S(1)}, u32[]{:S(2)}, u32[]{:S(2)}) collective-permute-start(f32[512,128]{1,0:T(8,128)S(1)} %get-tuple-element.104.refs_6_), channel_id=1, source_target_pairs={{0,6},{2,4},{4,2},{6,0},{8,14},{10,12},{12,10},{14,8},{16,22},{18,... | collective-permute-start | bytes 786440 | tf_op jit(solution)/shard_map/suffix/ppermute | solution.py:90
  70.9 20.0 %collective-permute-start.19 = (f32[512,128]{1,0:T(8,128)S(1)}, f32[512,128]{1,0:T(8,128)S(1)}, u32[]{:S(2)}, u32[]{:S(2)}) collective-permute-start(f32[512,128]{1,0:T(8,128)S(1)} %get-tuple-element.117), channel_id=1, source_target_pairs={{0,2},{2,0},{4,6},{6,4},{8,10},{10,8},{12,14},{14,12},{16,18},{18,... | collective-permute-start | bytes 786440 | tf_op jit(solution)/shard_map/suffix/ppermute | solution.py:90
  72.2 20.7 %collective-permute-start.20 = (f32[512,128]{1,0:T(8,128)S(1)}, f32[512,128]{1,0:T(8,128)S(1)}, u32[]{:S(2)}, u32[]{:S(2)}) collective-permute-start(f32[512,128]{1,0:T(8,128)S(1)} %get-tuple-element.118), channel_id=1, source_target_pairs={{0,4},{2,6},{4,0},{6,2},{8,12},{10,14},{12,8},{14,10},{16,20},{18,... | collective-permute-start | bytes 786440 | tf_op jit(solution)/shard_map/suffix/ppermute | solution.py:90
  81.7 11.1 %collective-permute-start.21 = (f32[512,128]{1,0:T(8,128)S(1)}, f32[512,128]{1,0:T(8,128)S(1)}, u32[]{:S(2)}, u32[]{:S(2)}) collective-permute-start(f32[512,128]{1,0:T(8,128)S(1)} %get-tuple-element.110.refs_6_), channel_id=1, source_target_pairs={{0,6},{2,4},{4,2},{6,0},{8,14},{10,12},{12,10},{14,8},{16,22},{18,... | collective-permute-start | bytes 786440 | tf_op jit(solution)/shard_map/suffix/ppermute | solution.py:90
  102.4 12.5 %collective-permute-start.34 = (f32[512,128]{1,0:T(8,128)S(1)}, f32[512,128]{1,0:T(8,128)S(1)}, u32[]{:S(2)}, u32[]{:S(2)}) collective-permute-start(f32[512,128]{1,0:T(8,128)S(1)} %get-tuple-element.137), channel_id=1, source_target_pairs={{0,2},{2,0},{4,6},{6,4},{8,10},{10,8},{12,14},{14,12},{16,18},{18,... | collective-permute-start | bytes 786440 | tf_op jit(solution)/shard_map/suffix/ppermute | solution.py:90
  103.8 12.2 %collective-permute-start.35 = (f32[512,128]{1,0:T(8,128)S(1)}, f32[512,128]{1,0:T(8,128)S(1)}, u32[]{:S(2)}, u32[]{:S(2)}) collective-permute-start(f32[512,128]{1,0:T(8,128)S(1)} %get-tuple-element.138), channel_id=1, source_target_pairs={{0,4},{2,6},{4,0},{6,2},{8,12},{10,14},{12,8},{14,10},{16,20},{18,... | collective-permute-start | bytes 786440 | tf_op jit(solution)/shard_map/suffix/ppermute | solution.py:90
  104.4 12.1 %collective-permute-start.36 = (f32[512,128]{1,0:T(8,128)S(1)}, f32[512,128]{1,0:T(8,128)S(1)}, u32[]{:S(2)}, u32[]{:S(2)}) collective-permute-start(f32[512,128]{1,0:T(8,128)S(1)} %get-tuple-element.128.refs_3_), channel_id=1, source_target_pairs={{0,6},{2,4},{4,2},{6,0},{8,14},{10,12},{12,10},{14,8},{16,22},{18,... | collective-permute-start | bytes 786440 | tf_op jit(solution)/shard_map/suffix/ppermute | solution.py:90
  112.4 9.5 %collective-permute-start.31 = (f32[512,128]{1,0:T(8,128)S(1)}, f32[512,128]{1,0:T(8,128)S(1)}, u32[]{:S(2)}, u32[]{:S(2)}) collective-permute-start(f32[512,128]{1,0:T(8,128)S(1)} %get-tuple-element.132), channel_id=1, source_target_pairs={{0,2},{2,0},{4,6},{6,4},{8,10},{10,8},{12,14},{14,12},{16,18},{18,... | collective-permute-start | bytes 786440 | tf_op jit(solution)/shard_map/suffix/ppermute | solution.py:90
  113.8 11.8 %collective-permute-start.32 = (f32[512,128]{1,0:T(8,128)S(1)}, f32[512,128]{1,0:T(8,128)S(1)}, u32[]{:S(2)}, u32[]{:S(2)}) collective-permute-start(f32[512,128]{1,0:T(8,128)S(1)} %get-tuple-element.133), channel_id=1, source_target_pairs={{0,4},{2,6},{4,0},{6,2},{8,12},{10,14},{12,8},{14,10},{16,20},{18,... | collective-permute-start | bytes 786440 | tf_op jit(solution)/shard_map/suffix/ppermute | solution.py:90
  114.9 10.7 %collective-permute-start.33 = (f32[512,128]{1,0:T(8,128)S(1)}, f32[512,128]{1,0:T(8,128)S(1)}, u32[]{:S(2)}, u32[]{:S(2)}) collective-permute-start(f32[512,128]{1,0:T(8,128)S(1)} %get-tuple-element.134.refs_8_), channel_id=1, source_target_pairs={{0,6},{2,4},{4,2},{6,0},{8,14},{10,12},{12,10},{14,8},{16,22},{18,... | collective-permute-start | bytes 786440 | tf_op jit(solution)/shard_map/suffix/ppermute | solution.py:90
  (20 other events, 118.8 us)

commit v5 on v4

--- a/solution.py
+++ b/solution.py
@@ -197,10 +197,12 @@
     results = []
     steps = [scan_steps(run, parts, reverse, results) for parts in groups]
     count = 2 * ((lax.axis_size("seq") // PLANE).bit_length() - 1)
-    events = [(g / 10 - 1.0, filler) for g, filler in enumerate(fillers)]
+    events = []
     for g, one in enumerate(steps):
         next(one)
         behind = 0.5 + 1.2 * g if g else 0.0
+        last = g > 0 and g == len(steps) - 1
+        events.append((behind + count + 0.5 if last else g / 10 - 1.0, fillers[g]))
         events += [(behind + step, functools.partial(next, one, None)) for step in range(count)]
         events.append((behind + count + 1, lambda g=g: use(g, results[g])))
     for _, event in sorted(events, key=lambda e: e[0]):

time: 127 us -> 127 us (level)
  waiting for transfers between devices: 50.5 us -> 48.3 us
    ppermute x36, waiting for transfers between devices: 49.2 us -> 46.9 us  [exchange(): return lax.ppermute(value, 'seq', [(s, s ^ distance) for s in range(n)])]
  transfers between devices with their start and end apart: 37 -> 37, of which waited for: 22 -> 20; matrix products, arithmetic and copies ran while one was open for 0% -> 0% of each run, Pallas kernels for 15% -> 15%
where the time goes in v5:
time: 127 us
  starting transfers between devices  51.1 us (40%)
  waiting for transfers between devices  48.3 us (38%)
  Pallas kernels  24.7 us (19%)
  local copies, waits for them, and re-layouts  2.19 us (2%)
    ppermute x36, starting transfers between devices, exchange(): return lax.ppermute(value, 'seq', [(s, s ^ distance) for s in range(n)])  51 us
    ppermute x36, waiting for transfers between devices, exchange(): return lax.ppermute(value, 'seq', [(s, s ^ distance) for s in range(n)])  46.9 us
    pallas_call x28, Pallas kernels, __call__(): pl.pallas_call(kernel, out_shape=outs, in_specs=specs, out_specs=[pl.Bloc...  24.7 us
  transfers between devices with their start and end apart: 37, of which 20 were waited for; matrix products, arithmetic and copies ran while one was open for 0% of the time, Pallas kernels for 15%

profile of v5, /device:TPU:0, one launch (start us, length us, event | category | flops | bytes accessed | tf_op | source)
XLA Modules:
  0.0 127.3 jit_solution(12844995424441627083)
XLA Ops:
  0.7 2.7 %state.2 = (f32[512,128]{1,0:T(8,128)}, f32[512,128]{1,0:T(8,128)}, f32[512,128]{1,0:T(8,128)}, f32[512,128]{1,0:T(8,128)}) custom-call(bf16[128,4096]{1,0:T(8,128)(2,1)} %keys.3, bf16[128,4096]{1,0:T(8,128)(2,1)} %values.3), custom_call_target="tpu_custom_call" | custom-call | flops 1 | bytes 1 | tf_op jit(solution)/shard_map/state/pallas_call | solution.py:38
  3.3 3.0 %collective-permute-start = (f32[512,128]{1,0:T(8,128)}, f32[512,128]{1,0:T(8,128)S(1)}, u32[]{:S(2)}, u32[]{:S(2)}) collective-permute-start(f32[512,128]{1,0:T(8,128)} %get-tuple-element.76), channel_id=1, source_target_pairs={{0,2},{2,0},{4,6},{6,4},{8,10},{10,8},{12,14},{14,12},{16,18},{18,... | collective-permute-start | bytes 786440 | tf_op jit(solution)/shard_map/prefix/ppermute | solution.py:90
  9.4 2.0 %collective-permute-start.5 = (f32[512,128]{1,0:T(8,128)S(1)}, f32[512,128]{1,0:T(8,128)S(1)}, u32[]{:S(2)}, u32[]{:S(2)}) collective-permute-start(f32[512,128]{1,0:T(8,128)S(1)} %get-tuple-element.81), channel_id=1, source_target_pairs={{0,2},{2,0},{4,6},{6,4},{8,10},{10,8},{12,14},{14,12},{16,18},{18,... | collective-permute-start | bytes 786440 | tf_op jit(solution)/shard_map/prefix/ppermute | solution.py:90
  12.9 2.7 %prefix.12 = (bf16[128,2048]{1,0:T(8,128)(2,1)S(1)}, f32[128,2048]{1,0:T(8,128)S(1)}) custom-call(bf16[128,4096]{1,0:T(8,128)(2,1)S(1)} %copy-done, bf16[128,4096]{1,0:T(8,128)(2,1)S(1)} %copy-done.1, bf16[128,4096]{1,0:T(8,128)(2,1)S(1)} %copy-done.2, f32[512,128]{1,0:T(8,128)S(1)} %get-tuple-element.74.refs_3_.refs_0_.refs_2_), custom_call_target="tpu_custom_call" | custom-call | flops 1 | bytes 1 | tf_op jit(solution)/shard_map/prefix/pallas_call | solution.py:38
  16.7 4.7 %collective-permute-done.1.refs_2_.refs_4_ = f32[512,128]{1,0:T(8,128)S(1)} collective-permute-done((f32[512,128]{1,0:T(8,128)}, f32[512,128]{1,0:T(8,128)S(1)}, u32[]{:S(2)}, u32[]{:S(2)}) %collective-permute-start.1) | collective-permute-done | bytes 262176 | tf_op jit(solution)/shard_map/prefix/ppermute | solution.py:90
  23.1 3.4 %collective-permute-done.3.refs_1_.refs_2_ = f32[256,128]{1,0:T(8,128)S(1)} collective-permute-done((f32[256,128]{1,0:T(8,128)S(1)}, f32[256,128]{1,0:T(8,128)S(1)}, u32[]{:S(2)}, u32[]{:S(2)}) %collective-permute-start.3) | collective-permute-done | bytes 131104 | tf_op jit(solution)/shard_map/prefix/ppermute | solution.py:90
  26.5 3.8 %collective-permute-start.4 = (f32[256,128]{1,0:T(8,128)S(1)}, f32[256,128]{1,0:T(8,128)S(1)}, u32[]{:S(2)}, u32[]{:S(2)}) collective-permute-start(f32[256,128]{1,0:T(8,128)S(1)} %prefix.14.refs_4_), channel_id=1, source_target_pairs={{0,16},{2,18},{4,20},{6,22},{8,24},{10,26},{12,28},{14,30},{16,0},... | collective-permute-start | bytes 393224 | tf_op jit(solution)/shard_map/prefix/ppermute | solution.py:90
  32.9 1.9 %collective-permute-done.4.refs_0_ = f32[256,128]{1,0:T(8,128)S(1)} collective-permute-done((f32[256,128]{1,0:T(8,128)S(1)}, f32[256,128]{1,0:T(8,128)S(1)}, u32[]{:S(2)}, u32[]{:S(2)}) %collective-permute-start.4) | collective-permute-done | bytes 131104 | tf_op jit(solution)/shard_map/prefix/ppermute | solution.py:90
  34.8 2.9 %collective-permute-done.9.refs_1_.refs_2_ = f32[256,128]{1,0:T(8,128)S(1)} collective-permute-done((f32[256,128]{1,0:T(8,128)S(1)}, f32[256,128]{1,0:T(8,128)S(1)}, u32[]{:S(2)}, u32[]{:S(2)}) %collective-permute-start.9) | collective-permute-done | bytes 131104 | tf_op jit(solution)/shard_map/prefix/ppermute | solution.py:90
  37.7 1.8 %collective-permute-start.13 = (f32[256,128]{1,0:T(8,128)S(1)}, f32[256,128]{1,0:T(8,128)S(1)}, u32[]{:S(2)}, u32[]{:S(2)}) collective-permute-start(f32[256,128]{1,0:T(8,128)S(1)} %prefix.17.refs_6_), channel_id=1, source_target_pairs={{0,16},{2,18},{4,20},{6,22},{8,24},{10,26},{12,28},{14,30},{16,0},... | collective-permute-start | bytes 393224 | tf_op jit(solution)/shard_map/prefix/ppermute | solution.py:90
  46.1 4.2 %collective-permute-done.14.refs_1_ = f32[256,128]{1,0:T(8,128)S(1)} collective-permute-done((f32[256,128]{1,0:T(8,128)S(1)}, f32[256,128]{1,0:T(8,128)S(1)}, u32[]{:S(2)}, u32[]{:S(2)}) %collective-permute-start.14) | collective-permute-done | bytes 131104 | tf_op jit(solution)/shard_map/prefix/ppermute | solution.py:90
  56.6 2.9 %prefix.22 = (bf16[128,2048]{1,0:T(8,128)(2,1)S(1)}, f32[128,2048]{1,0:T(8,128)S(1)}) custom-call(bf16[128,4096]{1,0:T(8,128)(2,1)S(1)} %copy-done, bf16[128,4096]{1,0:T(8,128)(2,1)S(1)} %copy-done.1, bf16[128,4096]{1,0:T(8,128)(2,1)S(1)} %copy-done.2, f32[2,128,128]{2,1,0:T(8,128)S(1)} %get-tuple-element.95.refs_3_.refs_4_), custom_call_target="tpu_custom_call" | custom-call | flops 1 | bytes 1 | tf_op jit(solution)/shard_map/prefix/pallas_call | solution.py:38
  60.6 3.3 %collective-permute-done.16.refs_2_ = f32[512,128]{1,0:T(8,128)S(1)} collective-permute-done((f32[512,128]{1,0:T(8,128)S(1)}, f32[512,128]{1,0:T(8,128)S(1)}, u32[]{:S(2)}, u32[]{:S(2)}) %collective-permute-start.16) | collective-permute-done | bytes 262176 | tf_op jit(solution)/shard_map/prefix/ppermute | solution.py:90
  73.2 4.2 %suffix.12 = (bf16[128,4096]{1,0:T(8,128)(2,1)}, f32[128,2048]{1,0:T(8,128)S(1)}, f32[128,2048]{1,0:T(8,128)S(1)}) custom-call(bf16[128,4096]{1,0:T(8,128)(2,1)S(1)} %copy-done, bf16[128,4096]{1,0:T(8,128)(2,1)S(1)} %copy-done.1, bf16[128,4096]{1,0:T(8,128)(2,1)S(1)} %copy-done.2, bf16[128,2048]{1,0:T(8,128)(2,1)S(1)} %get-tuple-element.107.refs_3_, ...), custom_call_target="tpu_custom_call" | custom-call | flops 1 | bytes 1 | tf_op jit(solution)/shard_map/suffix/pallas_call | solution.py:38
  78.8 3.9 %collective-permute-done.20.refs_2_.refs_4_ = f32[512,128]{1,0:T(8,128)S(1)} collective-permute-done((f32[512,128]{1,0:T(8,128)S(1)}, f32[512,128]{1,0:T(8,128)S(1)}, u32[]{:S(2)}, u32[]{:S(2)}) %collective-permute-start.20) | collective-permute-done | bytes 262176 | tf_op jit(solution)/shard_map/suffix/ppermute | solution.py:90
  82.8 1.9 %collective-permute-start.22 = (f32[256,128]{1,0:T(8,128)S(1)}, f32[256,128]{1,0:T(8,128)S(1)}, u32[]{:S(2)}, u32[]{:S(2)}) collective-permute-start(f32[256,128]{1,0:T(8,128)S(1)} %get-tuple-element.118.refs_2_), channel_id=1, source_target_pairs={{0,8},{2,10},{4,12},{6,14},{8,0},{10,2},{12,4},{14,6},{16,24},{18,... | collective-permute-start | bytes 393224 | tf_op jit(solution)/shard_map/suffix/ppermute | solution.py:90
  84.7 3.1 %collective-permute-done.22.refs_1_.refs_2_ = f32[256,128]{1,0:T(8,128)S(1)} collective-permute-done((f32[256,128]{1,0:T(8,128)S(1)}, f32[256,128]{1,0:T(8,128)S(1)}, u32[]{:S(2)}, u32[]{:S(2)}) %collective-permute-start.22) | collective-permute-done | bytes 131104 | tf_op jit(solution)/shard_map/suffix/ppermute | solution.py:90
  87.8 2.3 %collective-permute-start.23 = (f32[256,128]{1,0:T(8,128)S(1)}, f32[256,128]{1,0:T(8,128)S(1)}, u32[]{:S(2)}, u32[]{:S(2)}) collective-permute-start(f32[256,128]{1,0:T(8,128)S(1)} %suffix.14.refs_4_), channel_id=1, source_target_pairs={{0,16},{2,18},{4,20},{6,22},{8,24},{10,26},{12,28},{14,30},{16,0},... | collective-permute-start | bytes 393224 | tf_op jit(solution)/shard_map/suffix/ppermute | solution.py:90
  90.2 2.7 %collective-permute-done.25.refs_2_.refs_4_ = f32[512,128]{1,0:T(8,128)S(1)} collective-permute-done((f32[512,128]{1,0:T(8,128)S(1)}, f32[512,128]{1,0:T(8,128)S(1)}, u32[]{:S(2)}, u32[]{:S(2)}) %collective-permute-start.25) | collective-permute-done | bytes 262176 | tf_op jit(solution)/shard_map/suffix/ppermute | solution.py:90
  92.9 1.9 %collective-permute-start.28 = (f32[256,128]{1,0:T(8,128)S(1)}, f32[256,128]{1,0:T(8,128)S(1)}, u32[]{:S(2)}, u32[]{:S(2)}) collective-permute-start(f32[256,128]{1,0:T(8,128)S(1)} %get-tuple-element.122.refs_3_), channel_id=1, source_target_pairs={{0,8},{2,10},{4,12},{6,14},{8,0},{10,2},{12,4},{14,6},{16,24},{18,... | collective-permute-start | bytes 393224 | tf_op jit(solution)/shard_map/suffix/ppermute | solution.py:90
  95.8 3.3 %collective-permute-done.28.refs_1_.refs_2_ = f32[256,128]{1,0:T(8,128)S(1)} collective-permute-done((f32[256,128]{1,0:T(8,128)S(1)}, f32[256,128]{1,0:T(8,128)S(1)}, u32[]{:S(2)}, u32[]{:S(2)}) %collective-permute-start.28) | collective-permute-done | bytes 131104 | tf_op jit(solution)/shard_map/suffix/ppermute | solution.py:90
  99.2 2.8 %collective-permute-start.32 = (f32[256,128]{1,0:T(8,128)S(1)}, f32[256,128]{1,0:T(8,128)S(1)}, u32[]{:S(2)}, u32[]{:S(2)}) collective-permute-start(f32[256,128]{1,0:T(8,128)S(1)} %suffix.17.refs_6_), channel_id=1, source_target_pairs={{0,16},{2,18},{4,20},{6,22},{8,24},{10,26},{12,28},{14,30},{16,0},... | collective-permute-start | bytes 393224 | tf_op jit(solution)/shard_map/suffix/ppermute | solution.py:90
  107.9 4.2 %collective-permute-done.33.refs_1_ = f32[256,128]{1,0:T(8,128)S(1)} collective-permute-done((f32[256,128]{1,0:T(8,128)S(1)}, f32[256,128]{1,0:T(8,128)S(1)}, u32[]{:S(2)}, u32[]{:S(2)}) %collective-permute-start.33) | collective-permute-done | bytes 131104 | tf_op jit(solution)/shard_map/suffix/ppermute | solution.py:90
  119.8 4.2 %suffix.22 = (bf16[128,4096]{1,0:T(8,128)(2,1)}, f32[128,2048]{1,0:T(8,128)S(1)}, f32[128,2048]{1,0:T(8,128)S(1)}) custom-call(bf16[128,4096]{1,0:T(8,128)(2,1)S(1)} %copy-done, bf16[128,4096]{1,0:T(8,128)(2,1)S(1)} %copy-done.1, bf16[128,4096]{1,0:T(8,128)(2,1)S(1)} %copy-done.2, ...), custom_call_target="tpu_custom_call", output_to_operand_aliasing={{0}: (6, {})} | custom-call | flops 1 | bytes 1 | tf_op jit(solution)/shard_map/suffix/pallas_call | solution.py:38
  (94 shorter events, 52.2 us)
Async XLA Ops:
  3.3 12.4 %collective-permute-start = (f32[512,128]{1,0:T(8,128)}, f32[512,128]{1,0:T(8,128)S(1)}, u32[]{:S(2)}, u32[]{:S(2)}) collective-permute-start(f32[512,128]{1,0:T(8,128)} %get-tuple-element.76), channel_id=1, source_target_pairs={{0,2},{2,0},{4,6},{6,4},{8,10},{10,8},{12,14},{14,12},{16,18},{18,... | collective-permute-start | bytes 786440 | tf_op jit(solution)/shard_map/prefix/ppermute | solution.py:90
  6.3 15.1 %collective-permute-start.1 = (f32[512,128]{1,0:T(8,128)}, f32[512,128]{1,0:T(8,128)S(1)}, u32[]{:S(2)}, u32[]{:S(2)}) collective-permute-start(f32[512,128]{1,0:T(8,128)} %get-tuple-element.77), channel_id=1, source_target_pairs={{0,4},{2,6},{4,0},{6,2},{8,12},{10,14},{12,8},{14,10},{16,20},{18,... | collective-permute-start | bytes 786440 | tf_op jit(solution)/shard_map/prefix/ppermute | solution.py:90
  7.8 13.5 %collective-permute-start.2 = (f32[512,128]{1,0:T(8,128)}, f32[512,128]{1,0:T(8,128)S(1)}, u32[]{:S(2)}, u32[]{:S(2)}) collective-permute-start(f32[512,128]{1,0:T(8,128)} %get-tuple-element.78), channel_id=1, source_target_pairs={{0,6},{2,4},{4,2},{6,0},{8,14},{10,12},{12,10},{14,8},{16,22},{18,... | collective-permute-start | bytes 786440 | tf_op jit(solution)/shard_map/prefix/ppermute | solution.py:90
  9.4 20.9 %collective-permute-start.5 = (f32[512,128]{1,0:T(8,128)S(1)}, f32[512,128]{1,0:T(8,128)S(1)}, u32[]{:S(2)}, u32[]{:S(2)}) collective-permute-start(f32[512,128]{1,0:T(8,128)S(1)} %get-tuple-element.81), channel_id=1, source_target_pairs={{0,2},{2,0},{4,6},{6,4},{8,10},{10,8},{12,14},{14,12},{16,18},{18,... | collective-permute-start | bytes 786440 | tf_op jit(solution)/shard_map/prefix/ppermute | solution.py:90
  11.4 19.7 %collective-permute-start.6 = (f32[512,128]{1,0:T(8,128)S(1)}, f32[512,128]{1,0:T(8,128)S(1)}, u32[]{:S(2)}, u32[]{:S(2)}) collective-permute-start(f32[512,128]{1,0:T(8,128)S(1)} %get-tuple-element.82), channel_id=1, source_target_pairs={{0,4},{2,6},{4,0},{6,2},{8,12},{10,14},{12,8},{14,10},{16,20},{18,... | collective-permute-start | bytes 786440 | tf_op jit(solution)/shard_map/prefix/ppermute | solution.py:90
  15.7 15.5 %collective-permute-start.7 = (f32[512,128]{1,0:T(8,128)S(1)}, f32[512,128]{1,0:T(8,128)S(1)}, u32[]{:S(2)}, u32[]{:S(2)}) collective-permute-start(f32[512,128]{1,0:T(8,128)S(1)} %get-tuple-element.83), channel_id=1, source_target_pairs={{0,6},{2,4},{4,2},{6,0},{8,14},{10,12},{12,10},{14,8},{16,22},{18,... | collective-permute-start | bytes 786440 | tf_op jit(solution)/shard_map/prefix/ppermute | solution.py:90
  41.4 11.3 %collective-permute-start.10 = (f32[512,128]{1,0:T(8,128)S(1)}, f32[512,128]{1,0:T(8,128)S(1)}, u32[]{:S(2)}, u32[]{:S(2)}) collective-permute-start(f32[512,128]{1,0:T(8,128)S(1)} %get-tuple-element.89), channel_id=1, source_target_pairs={{0,2},{2,0},{4,6},{6,4},{8,10},{10,8},{12,14},{14,12},{16,18},{18,... | collective-permute-start | bytes 786440 | tf_op jit(solution)/shard_map/prefix/ppermute | solution.py:90
  42.0 12.2 %collective-permute-start.11 = (f32[512,128]{1,0:T(8,128)S(1)}, f32[512,128]{1,0:T(8,128)S(1)}, u32[]{:S(2)}, u32[]{:S(2)}) collective-permute-start(f32[512,128]{1,0:T(8,128)S(1)} %get-tuple-element.90), channel_id=1, source_target_pairs={{0,4},{2,6},{4,0},{6,2},{8,12},{10,14},{12,8},{14,10},{16,20},{18,... | collective-permute-start | bytes 786440 | tf_op jit(solution)/shard_map/prefix/ppermute | solution.py:90
  43.6 12.3 %collective-permute-start.12 = (f32[512,128]{1,0:T(8,128)S(1)}, f32[512,128]{1,0:T(8,128)S(1)}, u32[]{:S(2)}, u32[]{:S(2)}) collective-permute-start(f32[512,128]{1,0:T(8,128)S(1)} %get-tuple-element.91.refs_3_), channel_id=1, source_target_pairs={{0,6},{2,4},{4,2},{6,0},{8,14},{10,12},{12,10},{14,8},{16,22},{18,... | collective-permute-start | bytes 786440 | tf_op jit(solution)/shard_map/prefix/ppermute | solution.py:90
  50.6 9.9 %collective-permute-start.15 = (f32[512,128]{1,0:T(8,128)S(1)}, f32[512,128]{1,0:T(8,128)S(1)}, u32[]{:S(2)}, u32[]{:S(2)}) collective-permute-start(f32[512,128]{1,0:T(8,128)S(1)} %get-tuple-element.99), channel_id=1, source_target_pairs={{0,2},{2,0},{4,6},{6,4},{8,10},{10,8},{12,14},{14,12},{16,18},{18,... | collective-permute-start | bytes 786440 | tf_op jit(solution)/shard_map/prefix/ppermute | solution.py:90
  51.7 12.1 %collective-permute-start.16 = (f32[512,128]{1,0:T(8,128)S(1)}, f32[512,128]{1,0:T(8,128)S(1)}, u32[]{:S(2)}, u32[]{:S(2)}) collective-permute-start(f32[512,128]{1,0:T(8,128)S(1)} %get-tuple-element.100), channel_id=1, source_target_pairs={{0,4},{2,6},{4,0},{6,2},{8,12},{10,14},{12,8},{14,10},{16,20},{18,... | collective-permute-start | bytes 786440 | tf_op jit(solution)/shard_map/prefix/ppermute | solution.py:90
  52.7 11.1 %collective-permute-start.17 = (f32[512,128]{1,0:T(8,128)S(1)}, f32[512,128]{1,0:T(8,128)S(1)}, u32[]{:S(2)}, u32[]{:S(2)}) collective-permute-start(f32[512,128]{1,0:T(8,128)S(1)} %get-tuple-element.94.refs_8_), channel_id=1, source_target_pairs={{0,6},{2,4},{4,2},{6,0},{8,14},{10,12},{12,10},{14,8},{16,22},{18,... | collective-permute-start | bytes 786440 | tf_op jit(solution)/shard_map/prefix/ppermute | solution.py:90
  66.6 10.8 %collective-permute-start.19 = (f32[512,128]{1,0:T(8,128)S(1)}, f32[512,128]{1,0:T(8,128)S(1)}, u32[]{:S(2)}, u32[]{:S(2)}) collective-permute-start(f32[512,128]{1,0:T(8,128)S(1)} %get-tuple-element.115), channel_id=1, source_target_pairs={{0,2},{2,0},{4,6},{6,4},{8,10},{10,8},{12,14},{14,12},{16,18},{18,... | collective-permute-start | bytes 786440 | tf_op jit(solution)/shard_map/suffix/ppermute | solution.py:90
  67.9 14.8 %collective-permute-start.20 = (f32[512,128]{1,0:T(8,128)S(1)}, f32[512,128]{1,0:T(8,128)S(1)}, u32[]{:S(2)}, u32[]{:S(2)}) collective-permute-start(f32[512,128]{1,0:T(8,128)S(1)} %get-tuple-element.116), channel_id=1, source_target_pairs={{0,4},{2,6},{4,0},{6,2},{8,12},{10,14},{12,8},{14,10},{16,20},{18,... | collective-permute-start | bytes 786440 | tf_op jit(solution)/shard_map/suffix/ppermute | solution.py:90
  68.9 13.8 %collective-permute-start.21 = (f32[512,128]{1,0:T(8,128)S(1)}, f32[512,128]{1,0:T(8,128)S(1)}, u32[]{:S(2)}, u32[]{:S(2)}) collective-permute-start(f32[512,128]{1,0:T(8,128)S(1)} %get-tuple-element.104.refs_6_), channel_id=1, source_target_pairs={{0,6},{2,4},{4,2},{6,0},{8,14},{10,12},{12,10},{14,8},{16,22},{18,... | collective-permute-start | bytes 786440 | tf_op jit(solution)/shard_map/suffix/ppermute | solution.py:90
  70.9 19.3 %collective-permute-start.24 = (f32[512,128]{1,0:T(8,128)S(1)}, f32[512,128]{1,0:T(8,128)S(1)}, u32[]{:S(2)}, u32[]{:S(2)}) collective-permute-start(f32[512,128]{1,0:T(8,128)S(1)} %get-tuple-element.120), channel_id=1, source_target_pairs={{0,2},{2,0},{4,6},{6,4},{8,10},{10,8},{12,14},{14,12},{16,18},{18,... | collective-permute-start | bytes 786440 | tf_op jit(solution)/shard_map/suffix/ppermute | solution.py:90
  72.2 20.7 %collective-permute-start.25 = (f32[512,128]{1,0:T(8,128)S(1)}, f32[512,128]{1,0:T(8,128)S(1)}, u32[]{:S(2)}, u32[]{:S(2)}) collective-permute-start(f32[512,128]{1,0:T(8,128)S(1)} %get-tuple-element.121), channel_id=1, source_target_pairs={{0,4},{2,6},{4,0},{6,2},{8,12},{10,14},{12,8},{14,10},{16,20},{18,... | collective-permute-start | bytes 786440 | tf_op jit(solution)/shard_map/suffix/ppermute | solution.py:90
  77.4 15.4 %collective-permute-start.26 = (f32[512,128]{1,0:T(8,128)S(1)}, f32[512,128]{1,0:T(8,128)S(1)}, u32[]{:S(2)}, u32[]{:S(2)}) collective-permute-start(f32[512,128]{1,0:T(8,128)S(1)} %get-tuple-element.110.refs_6_), channel_id=1, source_target_pairs={{0,6},{2,4},{4,2},{6,0},{8,14},{10,12},{12,10},{14,8},{16,22},{18,... | collective-permute-start | bytes 786440 | tf_op jit(solution)/shard_map/suffix/ppermute | solution.py:90
  102.3 12.2 %collective-permute-start.29 = (f32[512,128]{1,0:T(8,128)S(1)}, f32[512,128]{1,0:T(8,128)S(1)}, u32[]{:S(2)}, u32[]{:S(2)}) collective-permute-start(f32[512,128]{1,0:T(8,128)S(1)} %get-tuple-element.127), channel_id=1, source_target_pairs={{0,2},{2,0},{4,6},{6,4},{8,10},{10,8},{12,14},{14,12},{16,18},{18,... | collective-permute-start | bytes 786440 | tf_op jit(solution)/shard_map/suffix/ppermute | solution.py:90
  103.8 12.2 %collective-permute-start.30 = (f32[512,128]{1,0:T(8,128)S(1)}, f32[512,128]{1,0:T(8,128)S(1)}, u32[]{:S(2)}, u32[]{:S(2)}) collective-permute-start(f32[512,128]{1,0:T(8,128)S(1)} %get-tuple-element.128), channel_id=1, source_target_pairs={{0,4},{2,6},{4,0},{6,2},{8,12},{10,14},{12,8},{14,10},{16,20},{18,... | collective-permute-start | bytes 786440 | tf_op jit(solution)/shard_map/suffix/ppermute | solution.py:90
  104.4 12.7 %collective-permute-start.31 = (f32[512,128]{1,0:T(8,128)S(1)}, f32[512,128]{1,0:T(8,128)S(1)}, u32[]{:S(2)}, u32[]{:S(2)}) collective-permute-start(f32[512,128]{1,0:T(8,128)S(1)} %get-tuple-element.129.refs_3_), channel_id=1, source_target_pairs={{0,6},{2,4},{4,2},{6,0},{8,14},{10,12},{12,10},{14,8},{16,22},{18,... | collective-permute-start | bytes 786440 | tf_op jit(solution)/shard_map/suffix/ppermute | solution.py:90
  112.4 11.6 %collective-permute-start.34 = (f32[512,128]{1,0:T(8,128)S(1)}, f32[512,128]{1,0:T(8,128)S(1)}, u32[]{:S(2)}, u32[]{:S(2)}) collective-permute-start(f32[512,128]{1,0:T(8,128)S(1)} %get-tuple-element.138), channel_id=1, source_target_pairs={{0,2},{2,0},{4,6},{6,4},{8,10},{10,8},{12,14},{14,12},{16,18},{18,... | collective-permute-start | bytes 786440 | tf_op jit(solution)/shard_map/suffix/ppermute | solution.py:90
  113.8 11.9 %collective-permute-start.35 = (f32[512,128]{1,0:T(8,128)S(1)}, f32[512,128]{1,0:T(8,128)S(1)}, u32[]{:S(2)}, u32[]{:S(2)}) collective-permute-start(f32[512,128]{1,0:T(8,128)S(1)} %get-tuple-element.139), channel_id=1, source_target_pairs={{0,4},{2,6},{4,0},{6,2},{8,12},{10,14},{12,8},{14,10},{16,20},{18,... | collective-permute-start | bytes 786440 | tf_op jit(solution)/shard_map/suffix/ppermute | solution.py:90
  114.5 11.1 %collective-permute-start.36 = (f32[512,128]{1,0:T(8,128)S(1)}, f32[512,128]{1,0:T(8,128)S(1)}, u32[]{:S(2)}, u32[]{:S(2)}) collective-permute-start(f32[512,128]{1,0:T(8,128)S(1)} %get-tuple-element.132.refs_8_), channel_id=1, source_target_pairs={{0,6},{2,4},{4,2},{6,0},{8,14},{10,12},{12,10},{14,8},{16,22},{18,... | collective-permute-start | bytes 786440 | tf_op jit(solution)/shard_map/suffix/ppermute | solution.py:90
  (21 other events, 120.4 us)
